TPU v7x, 512 devices: a whole 4x8x8 slice. The times are simulated.
512 devices in a mesh: row: 16 (over y_hi, x), col: 32 (over y_lo, z, core).
Axes of the slice: x: 4, y: 8 (y_hi: 4, y_lo: 2; y = y_hi * 2 + y_lo), z: 8, core: 2. Of those that a mesh axis runs over, the one named last changes fastest.
Arguments:
- inputs: bfloat16 [1024, 16384], P('col', 'row'), may hold values from -0.1875 to 0.1875
- weight: bfloat16 [16384, 18432], P('row', 'col'), may hold values from -0.046875 to 0.046875
- grad_out: bfloat16 [1024, 18432], P('row', 'col'), may hold values from -6 to 6
- positions: int32 [1024], P('row'), may hold values from 0 to 8191
Outputs:
- input_grad: bfloat16 [1024, 16384], P('col', 'row')
- weight_grad: float32 [16384, 18432], P('row', 'col')
All inputs are finite; a program needn't handle non-finite values.
Results may differ from a plain program's by a relative error of at most 0.0065.
Values may be sent and summed in bfloat16 or wider, within the bound.
No kernel may reach another device: no remote copies, remote signals or barrier semaphores. Data moves between devices by JAX's collectives and lax.ppermute only.
A program may use at most 64 MiB of HBM per device.

v0:
```python
import math

import jax
import jax.numpy as jnp
from jax import lax
from jax.sharding import PartitionSpec as P

QHEADS = 128
KVHEADS = 8
HEAD = 128


def copy_for_each(array, axis):
    devices = lax.axis_size(axis)
    return lax.all_to_all(
        jnp.broadcast_to(array[None], (devices, *array.shape)), axis, 0, 0, tiled=True
    )


def joined_along(parts, dim):
    parts = jnp.moveaxis(parts, 0, dim)
    shape = parts.shape
    return parts.reshape(*shape[:dim], shape[dim] * shape[dim + 1], *shape[dim + 2 :])


def gather_directly(array, axis, dim):
    parts = copy_for_each(array, axis)
    return joined_along(parts, dim)


def in_blocks(array, dim, devices):
    before, after = (array.shape[:dim], array.shape[dim + 1 :])
    return jnp.moveaxis(array.reshape(*before, devices, -1, *after), dim, 0)


def summed_on_arrival(array, axis, dim):
    parts = in_blocks(array, dim, lax.axis_size(axis))
    arrived = lax.all_to_all(parts, axis, split_axis=0, concat_axis=0, tiled=True)
    return arrived.astype(jnp.float32).sum(axis=0)


def scaled_freq(within):
    base = jnp.exp(-(2.0 * within.astype(jnp.float32) / HEAD) * math.log(500000.0))
    wave = 2.0 * math.pi / base
    smooth = (8192.0 / wave - 1.0) / 3.0
    middle = (1.0 - smooth) * base / 8.0 + smooth * base
    return jnp.where(wave < 2048.0, base, jnp.where(wave > 8192.0, base / 8.0, middle))


def unrotate(grad, positions, col_start):
    rows = grad.shape[0]
    pairs = grad.shape[1] // 2
    columns = col_start + 2 * jnp.arange(pairs, dtype=jnp.int32)
    within = columns % HEAD // 2
    freq = scaled_freq(within)
    angle = positions.astype(jnp.float32)[:, None] * freq[None, :]
    cosine = jnp.cos(angle)
    sine = jnp.sin(angle)
    rotated = (columns < (QHEADS + KVHEADS) * HEAD)[None, :]
    cosine = jnp.where(rotated, cosine, 1.0)
    sine = jnp.where(rotated, sine, 0.0)
    split = grad.astype(jnp.float32).reshape(rows, pairs, 2)
    first = split[:, :, 0]
    second = split[:, :, 1]
    new_first = first * cosine + second * sine
    new_second = second * cosine - first * sine
    return jnp.stack([new_first, new_second], axis=2).reshape(rows, 2 * pairs).astype(jnp.bfloat16)


def outer_sum(left, right):
    return lax.dot_general(
        left, right, (((0,), (0,)), ((), ())), preferred_element_type=jnp.float32
    )


def per_device(inputs, weight, grad_out, positions):
    width = weight.shape[1]
    col_start = lax.axis_index("col") * width
    grad = unrotate(grad_out, positions, col_start)
    whole_grad = gather_directly(grad, "row", 0)
    weight_grad = outer_sum(gather_directly(inputs, "col", 0), whole_grad)
    summed = summed_on_arrival(
        lax.dot_general(
            whole_grad, weight, (((1,), (1,)), ((), ())), preferred_element_type=jnp.float32
        ).astype(jnp.bfloat16),
        "col",
        0,
    )
    input_grad = summed.astype(jnp.bfloat16)
    return (input_grad, weight_grad)


def solution(mesh):
    in_specs = (P("col", "row"), P("row", "col"), P("row", "col"), P("row"))
    out_specs = (P("col", "row"), P("row", "col"))
    return jax.shard_map(
        per_device, mesh=mesh, in_specs=in_specs, out_specs=out_specs, check_vma=False
    )
```

profile of v0, /device:TPU:9, one launch (start us, length us, event | category | flops | bytes accessed | tf_op | source)
XLA Modules:
  0.0 182.4 jit_solution(15483537795121438822)
XLA Ops:
  0.6 0.0 copy-start
  0.7 0.7 convert_element_type.24
  1.4 1.0 copy.6
  2.4 5.7 %add_convert_fusion = (bf16[64,288,1]{0,2,1:T(2,128)(2,1)S(1)}, bf16[64,288,1]{0,2,1:T(2,128)(2,1)S(1)}) fusion(f32[64,288,2]{0,2,1:T(2,128)S(1)} %bitcast.15, f32[288]{0:T(512)S(1)} %select_select_fusion, f32[64]{0:T(128)S(1)} %convert_element_type.24, pred[288]{0:T(512)(128)(4,1)S(1)} %fusion.7), kind=kLoop, calls=%fused_computation.8 | loop fusion | flops 202752 | bytes 222880 | tf_op jit(solution)/shard_map/convert.2
  8.1 0.4 pad_maximum_fusion
  8.5 0.1 copy.7
  8.7 0.1 broadcast_in_dim.36
  8.8 0.0 copy-start.1
  8.8 36.6 %all_to_all.15 = bf16[16,64,576]{2,1,0:T(8,128)(2,1)} all-to-all(bf16[16,64,576]{2,1,0:T(8,128)(2,1)S(1)} %broadcast_in_dim.36), channel_id=1, replica_groups=mesh['row'=16,'col'=32] {'row'}, dimensions={0} | all-to-all | bytes 2359296 | tf_op jit(solution)/shard_map/all_to_all | solution.py:15
  45.5 0.0 copy-done.1
  45.5 1.6 broadcast_in_dim.37
  47.1 19.6 %all-to-all-start.2 = ((bf16[32,32,1024]{2,1,0:T(8,128)(2,1)}), bf16[32,32,1024]{2,1,0:T(8,128)(2,1)S(1)}, u32[]{:S(2)}, u32[]{:S(2)}) async-start(bf16[32,32,1024]{2,1,0:T(8,128)(2,1)} %broadcast_in_dim.37), calls=%async_computation.2 | async-start | bytes 4194304 | tf_op jit(solution)/shard_map/all_to_all | solution.py:15
  66.7 0.0 copy-done
  66.7 4.4 %convolution_convert_fusion = bf16[1024,1024]{1,0:T(8,128)(2,1)} fusion(bf16[1024,576]{1,0:T(8,128)(2,1)} %bitcast.12, bf16[1024,576]{0,1:T(8,128)(2,1)S(1)} %copy-done), kind=kOutput, calls=%fused_computation | convolution fusion | flops 1209008128 | bytes 4456448 | tf_op jit(solution)/shard_map/dot_general | solution.py:83
  71.1 49.5 %all-to-all-done.2 = bf16[32,32,1024]{2,1,0:T(8,128)(2,1)S(1)} async-done(((bf16[32,32,1024]{2,1,0:T(8,128)(2,1)}), bf16[32,32,1024]{2,1,0:T(8,128)(2,1)S(1)}, u32[]{:S(2)}, u32[]{:S(2)}) %all-to-all-start.2) | async-done | bytes 2097184 | tf_op jit(solution)/shard_map/all_to_all | solution.py:15
  120.6 5.2 %all-to-all-start.1 = ((bf16[32,32,1024]{2,1,0:T(8,128)(2,1)}), bf16[32,32,1024]{2,1,0:T(8,128)(2,1)}, u32[]{:S(2)}, u32[]{:S(2)}) async-start(bf16[32,32,1024]{2,1,0:T(8,128)(2,1)} %bitcast.14), calls=%async_computation.1 | async-start | bytes 4194304 | tf_op jit(solution)/shard_map/all_to_all | solution.py:38
  125.8 4.1 %convolution_bitcast_fusion = f32[1024,576]{0,1:T(8,128)} fusion(bf16[1024,576]{1,0:T(8,128)(2,1)} %bitcast.13, bf16[1024,1024]{1,0:T(8,128)(2,1)S(1)} %bitcast.11), kind=kOutput, calls=%fused_computation.1 | convolution fusion | flops 1207959552 | bytes 5636096 | tf_op jit(solution)/shard_map/dot_general | solution.py:71
  129.9 49.8 %all-to-all-done.1 = bf16[32,32,1024]{2,1,0:T(8,128)(2,1)} async-done(((bf16[32,32,1024]{2,1,0:T(8,128)(2,1)}), bf16[32,32,1024]{2,1,0:T(8,128)(2,1)}, u32[]{:S(2)}, u32[]{:S(2)}) %all-to-all-start.1) | async-done | bytes 2097184 | tf_op jit(solution)/shard_map/all_to_all | solution.py:38
  179.8 2.6 %reduce_sum.12 = bf16[32,1024]{1,0:T(8,128)(2,1)} reduce(bf16[32,32,1024]{2,1,0:T(8,128)(2,1)} %all-to-all-done.1, bf16[]{:T(256)} %constant.68.clone.1), dimensions={0}, to_apply=%region_0.1 | reduce | flops 1015808 | bytes 2162690 | tf_op jit(solution)/shard_map/reduce_sum | solution.py:39
  (2 shorter events, 0.0 us)
Async XLA Ops:
  0.6 66.0 %copy-start = (bf16[1024,576]{0,1:T(8,128)(2,1)S(1)}, bf16[1024,576]{0,1:T(8,128)(2,1)}, u32[]{:S(2)}) copy-start(bf16[1024,576]{0,1:T(8,128)(2,1)} %param.5) | copy-start | bytes 3538948
  8.8 36.7 %copy-start.1 = (bf16[32,1024]{1,0:T(8,128)(2,1)S(1)}, bf16[32,1024]{1,0:T(8,128)(2,1)}, u32[]{:S(2)}) copy-start(bf16[32,1024]{1,0:T(8,128)(2,1)} %param.4) | copy-start | bytes 196612
  47.1 73.5 %all-to-all-start.2 = ((bf16[32,32,1024]{2,1,0:T(8,128)(2,1)}), bf16[32,32,1024]{2,1,0:T(8,128)(2,1)S(1)}, u32[]{:S(2)}, u32[]{:S(2)}) async-start(bf16[32,32,1024]{2,1,0:T(8,128)(2,1)} %broadcast_in_dim.37), calls=%async_computation.2 | async-start | bytes 4194304 | tf_op jit(solution)/shard_map/all_to_all | solution.py:15
  120.6 59.2 %all-to-all-start.1 = ((bf16[32,32,1024]{2,1,0:T(8,128)(2,1)}), bf16[32,32,1024]{2,1,0:T(8,128)(2,1)}, u32[]{:S(2)}, u32[]{:S(2)}) async-start(bf16[32,32,1024]{2,1,0:T(8,128)(2,1)} %bitcast.14), calls=%async_computation.1 | async-start | bytes 4194304 | tf_op jit(solution)/shard_map/all_to_all | solution.py:38
where the time goes:
time: 183 us; the launch traced here: 182 us
  waiting for transfers between devices  99.3 us (54%)
  blocking collectives  36.6 us (20%)
  starting transfers between devices  24.8 us (14%)
  other arithmetic  9.45 us (5%)
  matrix products  8.55 us (5%)
  local copies, waits for them, and re-layouts  2.89 us (2%)
    all_to_all x1, waiting for transfers between devices, summed_on_arrival(): lax.all_to_all(parts, axis, split_axis=0, concat_axis=0, tiled=True)  49.8 us
    all_to_all x1, waiting for transfers between devices, copy_for_each(): lax.all_to_all(jnp.broadcast_to(array[None], (devices, *array.shape)), ax...  49.5 us
    all_to_all x1, blocking collectives, copy_for_each(): lax.all_to_all(jnp.broadcast_to(array[None], (devices, *array.shape)), ax...  36.6 us
    all_to_all x1, starting transfers between devices, copy_for_each(): lax.all_to_all(jnp.broadcast_to(array[None], (devices, *array.shape)), ax...  19.6 us
    another operation x1, other arithmetic  5.67 us
    all_to_all x1, starting transfers between devices, summed_on_arrival(): lax.all_to_all(parts, axis, split_axis=0, concat_axis=0, tiled=True)  5.2 us
    dot_general x1, matrix products, per_device(): lax.dot_general(whole_grad, weight, (((1,), (1,)), ((), ())), preferred_e...  4.42 us
    dot_general x1, matrix products, outer_sum(): lax.dot_general(left, right, (((0,), (0,)), ((), ())), preferred_element_...  4.13 us
  transfers between devices with their start and end apart: 2, of which 2 were waited for; matrix products, arithmetic and copies ran while one was open for 5% of the time, Pallas kernels for 0%

commit v1 on v0

v1 whole, which is shorter than its diff:
```python
import math

import jax
import jax.numpy as jnp
from jax import lax
from jax.experimental import pallas as pl
from jax.experimental.pallas import tpu as pltpu
from jax.sharding import Mesh, PartitionSpec as P

QHEADS = 128
KVHEADS = 8
HEAD = 128
ROTATED = (QHEADS + KVHEADS) * HEAD

HALF_PI = (1.5703125, 4.837512969970703e-4, 7.549789948768648e-8)
ROW = ("yh", "x")
COL = ("yl", "zh", "zl", "c")
OWNERS = ("zl", "yl", "zh")
SWAP = ((0, 1), (1, 0))


def scaled_freq(within):
    base = jnp.exp(-(2.0 * within.astype(jnp.float32) / HEAD) * math.log(500000.0))
    wave = 2.0 * math.pi / base
    smooth = (8192.0 / wave - 1.0) / 3.0
    middle = (1.0 - smooth) * base / 8.0 + smooth * base
    return jnp.where(wave < 2048.0, base, jnp.where(wave > 8192.0, base / 8.0, middle))


def sine_cosine(angle):
    turns = jnp.floor(angle * (2.0 / math.pi) + 0.5)
    rest = angle
    for part in HALF_PI:
        rest = rest - turns * part
    square = rest * rest
    sine = rest + rest * square * (
        -1.6666654611e-1 + square * (8.3321608736e-3 + square * -1.9515295891e-4)
    )
    cosine = (
        1.0
        - 0.5 * square
        + square * square * (4.166664568298827e-2 + square * (-1.388731625493765e-3 + square * 2.443315711809948e-5))
    )
    quarter = turns.astype(jnp.int32)
    odd = (quarter & 1) == 1
    sine, cosine = jnp.where(odd, cosine, sine), jnp.where(odd, sine, cosine)
    sine = jnp.where((quarter & 2) == 2, -sine, sine)
    cosine = jnp.where(((quarter + 1) & 2) == 2, -cosine, cosine)
    return sine, cosine


def unrotate_kernel(place_ref, positions_ref, grad_ref, out_ref):
    rows, width = grad_ref.shape
    col_start, core = place_ref[0], place_ref[1]
    row = lax.broadcasted_iota(jnp.int32, (rows, rows), 0)
    column = lax.broadcasted_iota(jnp.int32, (rows, rows), 1)
    spread = jnp.where(row == column, positions_ref[...].astype(jnp.float32), 0.0)
    positions = jnp.sum(spread, axis=1, keepdims=True)
    lane = lax.broadcasted_iota(jnp.int32, (8, HEAD), 1)
    freq = scaled_freq(((col_start + lane) & (HEAD - 1)) >> 1)[:1]
    sine, cosine = sine_cosine(positions * freq)
    source = lax.broadcasted_iota(jnp.int32, (HEAD, HEAD), 0)
    target = lax.broadcasted_iota(jnp.int32, (HEAD, HEAD), 1)
    partner = jnp.where(source == (target ^ 1), jnp.where((target & 1) == 0, 1.0, -1.0), 0.0).astype(jnp.bfloat16)
    for start in range(0, width, HEAD):
        size = min(HEAD, width - start)
        block = grad_ref[:, start : start + size]
        swapped = jnp.dot(block, partner[:size, :size], preferred_element_type=jnp.float32)
        turned = block.astype(jnp.float32) * cosine[:, :size] + swapped * sine[:, :size]
        columns = col_start + start + lax.broadcasted_iota(jnp.int32, (rows, size), 1)
        result = jnp.where(columns < ROTATED, turned, block.astype(jnp.float32)).astype(jnp.bfloat16)
        half = rows // 2
        upper, lower = result[:half], result[half:]
        own = jnp.where(core == 0, upper, lower)
        other = jnp.where(core == 0, lower, upper)
        for copy in range(out_ref.shape[0]):
            out_ref[copy, :half, start : start + size] = own
            out_ref[copy, half:, start : start + size] = other


def unrotate(grad, positions, place, copies):
    rows, width = grad.shape
    return pl.pallas_call(
        unrotate_kernel,
        out_shape=jax.ShapeDtypeStruct((copies, rows, width), jnp.bfloat16),
        in_specs=[
            pl.BlockSpec(memory_space=pltpu.SMEM),
            pl.BlockSpec(memory_space=pltpu.VMEM),
            pl.BlockSpec(memory_space=pltpu.VMEM),
        ],
        out_specs=pl.BlockSpec(memory_space=pltpu.VMEM),
        name="unrotate",
    )(place, positions.reshape(1, rows), grad)


def exchange(parts, axes):
    return lax.all_to_all(parts, axes, 0, 0, tiled=True)


def copies_of(array, count):
    return jnp.broadcast_to(array[None], (count, *array.shape))


def over_width(left, right):
    return lax.dot_general(left, right, (((1,), (1,)), ((), ())), preferred_element_type=jnp.float32)


def over_tokens(left, right):
    return lax.dot_general(left, right, (((0,), (0,)), ((), ())), preferred_element_type=jnp.float32)


def per_device(inputs, weight, grad_out, positions):
    width = weight.shape[1]
    tokens, model = inputs.shape
    owners = lax.axis_size(OWNERS)
    place = jnp.stack([lax.axis_index(COL) * width, lax.axis_index("c")]).astype(jnp.int32)

    own_inputs = exchange(copies_of(inputs, owners), OWNERS).reshape(-1, model)
    other_inputs = lax.ppermute(own_inputs, "c", SWAP)

    sent = unrotate(grad_out, positions, place, lax.axis_size("yh"))
    grads = exchange(sent, "yh")
    half = grads.shape[1] // 2
    other_grads = exchange(copies_of(grads[:, half:].reshape(-1, width), lax.axis_size("x")), "x").reshape(-1, width)
    own_grads = exchange(copies_of(grads[:, :half].reshape(-1, width), lax.axis_size("x")), "x").reshape(-1, width)

    other_part = over_width(other_grads, weight).astype(jnp.bfloat16)
    arrived = lax.ppermute(other_part, "c", SWAP)
    own_part = (over_width(own_grads, weight) + arrived.astype(jnp.float32)).astype(jnp.bfloat16)
    parts = exchange(own_part.reshape(owners, tokens, model), OWNERS)
    input_grad = parts.astype(jnp.float32).sum(axis=0).astype(jnp.bfloat16)

    weight_grad = over_tokens(own_inputs, own_grads) + over_tokens(other_inputs, other_grads)
    return input_grad, weight_grad


def solution(mesh):
    sizes = {"yh": 4, "x": 4, "yl": 2, "zh": 2, "zl": 4, "c": 2}
    finer = Mesh(mesh.devices.reshape(tuple(sizes.values())), tuple(sizes))
    in_specs = (P(COL, ROW), P(ROW, COL), P(ROW, COL), P(ROW))
    out_specs = (P(COL, ROW), P(ROW, COL))
    return jax.shard_map(per_device, mesh=finer, in_specs=in_specs, out_specs=out_specs, check_vma=False)
```

time: 183 us -> 122 us (0.67)
  the two profiles are of different devices: /device:TPU:9 before, /device:TPU:25 now
where the time goes in v1:
time: 122 us; the launch traced here: 121 us
  waiting for transfers between devices  48 us (39%)
  starting transfers between devices  35.2 us (29%)
  blocking collectives  24.6 us (20%)
  matrix products  6.99 us (6%)
  local copies, waits for them, and re-layouts  2.47 us (2%)
  Pallas kernels  1.84 us (2%)
  other arithmetic  1.47 us (1%)
    all_to_all x3, waiting for transfers between devices, exchange(): return lax.all_to_all(parts, axes, 0, 0, tiled=True)  45.3 us
    all_to_all x3, starting transfers between devices, exchange(): return lax.all_to_all(parts, axes, 0, 0, tiled=True)  26.7 us
    all_to_all x2, blocking collectives, exchange(): return lax.all_to_all(parts, axes, 0, 0, tiled=True)  24.6 us
    ppermute x1, starting transfers between devices, per_device(): arrived = lax.ppermute(other_part, 'c', SWAP)  5.45 us
    dot_general x2, matrix products, over_tokens(): lax.dot_general(left, right, (((0,), (0,)), ((), ())), preferred_element_...  4.03 us
    ppermute x1, starting transfers between devices, per_device(): other_inputs = lax.ppermute(own_inputs, 'c', SWAP)  3.09 us
    dot_general x2, matrix products, over_width(): lax.dot_general(left, right, (((1,), (1,)), ((), ())), preferred_element_...  2.96 us
  transfers between devices with their start and end apart: 5, of which 5 were waited for; matrix products, arithmetic and copies ran while one was open for 6% of the time, Pallas kernels for 0%

profile of v1, /device:TPU:25, one launch (start us, length us, event | category | flops | bytes accessed | tf_op | source)
XLA Modules:
  0.0 121.3 jit_solution(10872156883086572607)
XLA Ops:
  0.6 0.0 copy-start
  0.7 0.6 pad_add_fusion.place_ref
  1.3 1.8 %unrotate.1 = bf16[4,64,576]{2,1,0:T(8,128)(2,1)} custom-call(s32[2]{0:T(128)} %pad_add_fusion.place_ref, s32[1,64]{1,0:T(1,128)} %bitcast.44, bf16[64,576]{1,0:T(8,128)(2,1)} %grad_ref.1), custom_call_target="tpu_custom_call" | custom-call | tf_op jit(solution)/shard_map/unrotate/pallas_call | solution.py:83
  3.1 14.9 %all_to_all.25 = bf16[4,64,576]{2,1,0:T(8,128)(2,1)S(1)} all-to-all(bf16[4,64,576]{2,1,0:T(8,128)(2,1)} %unrotate.1), channel_id=1, replica_groups=mesh['yh'=4,'x'=4,'yl'=2,'zh'=2,'zl'=4,'c'=2] {'yh'}, dimensions={0} | all-to-all | bytes 589824 | tf_op jit(solution)/shard_map/all_to_all | solution.py:97
  18.1 0.1 copy.10
  18.3 0.0 copy-start.4
  18.3 0.9 broadcast_in_dim.23
  19.2 4.0 %all-to-all-start.2 = ((bf16[4,128,576]{1,2,0:T(8,128)(2,1)}), bf16[4,128,576]{1,2,0:T(8,128)(2,1)S(1)}, u32[]{:S(2)}, u32[]{:S(2)}) async-start(bf16[4,128,576]{1,2,0:T(8,128)(2,1)} %broadcast_in_dim.23), calls=%async_computation.2 | async-start | bytes 1179648 | tf_op jit(solution)/shard_map/all_to_all | solution.py:97
  23.2 0.1 copy.8
  23.3 7.1 %all-to-all-done.2 = bf16[4,128,576]{1,2,0:T(8,128)(2,1)S(1)} async-done(((bf16[4,128,576]{1,2,0:T(8,128)(2,1)}), bf16[4,128,576]{1,2,0:T(8,128)(2,1)S(1)}, u32[]{:S(2)}, u32[]{:S(2)}) %all-to-all-start.2) | async-done | bytes 589856 | tf_op jit(solution)/shard_map/all_to_all | solution.py:97
  30.5 0.0 copy-start.1
  30.5 0.1 broadcast_in_dim.21
  30.6 9.7 %all_to_all.26 = bf16[4,128,576]{1,2,0:T(8,128)(2,1)S(1)} all-to-all(bf16[4,128,576]{1,2,0:T(8,128)(2,1)S(1)} %broadcast_in_dim.21), channel_id=1, replica_groups=mesh['yh'=4,'x'=4,'yl'=2,'zh'=2,'zl'=4,'c'=2] {'x'}, dimensions={0} | all-to-all | bytes 1179648 | tf_op jit(solution)/shard_map/all_to_all | solution.py:97
  40.2 0.0 copy-done.4
  40.2 0.0 copy-start.3
  40.2 1.2 broadcast_in_dim.24
  41.4 16.4 %all-to-all-start.4 = ((bf16[16,32,1024]{2,1,0:T(8,128)(2,1)}), bf16[16,32,1024]{2,1,0:T(8,128)(2,1)S(1)}, u32[]{:S(2)}, u32[]{:S(2)}) async-start(bf16[16,32,1024]{2,1,0:T(8,128)(2,1)} %broadcast_in_dim.24), calls=%async_computation.4 | async-start | bytes 2097152 | tf_op jit(solution)/shard_map/all_to_all | solution.py:97
  57.8 0.0 copy-done.1
  57.8 0.0 copy-done
  57.8 1.0 convolution_convert_fusion
  58.8 5.4 %collective-permute-start = (bf16[512,1024]{1,0:T(8,128)(2,1)S(1)}, bf16[512,1024]{1,0:T(8,128)(2,1)S(1)}, u32[]{:S(2)}, u32[]{:S(2)}) collective-permute-start(bf16[512,1024]{1,0:T(8,128)(2,1)S(1)} %convolution_convert_fusion), channel_id=1, source_target_pairs={{0,1},{1,0},{2,3},{3,2},{4,5},{5,4},{6,7},{7,6},{8,9},{9,8},{10,11... | collective-permute-start | bytes 3145736 | tf_op jit(solution)/shard_map/ppermute | solution.py:128
  64.2 2.3 %collective-permute-done = bf16[512,1024]{1,0:T(8,128)(2,1)S(1)} collective-permute-done((bf16[512,1024]{1,0:T(8,128)(2,1)S(1)}, bf16[512,1024]{1,0:T(8,128)(2,1)S(1)}, u32[]{:S(2)}, u32[]{:S(2)}) %collective-permute-start) | collective-permute-done | bytes 1048608 | tf_op jit(solution)/shard_map/ppermute | solution.py:128
  66.5 0.0 copy-done.3
  66.5 2.0 %add_convert_fusion = bf16[512,1024]{1,0:T(8,128)(2,1)} fusion(bf16[512,1024]{1,0:T(8,128)(2,1)S(1)} %collective-permute-done, bf16[1024,576]{0,1:T(8,128)(2,1)S(1)} %copy-done, bf16[4,128,576]{1,2,0:T(8,128)(2,1)S(1)} %all_to_all.26), kind=kOutput, calls=%fused_computation.1 | convolution fusion | flops 605552640 | bytes 3866624 | tf_op jit(solution)/shard_map/dot_general | solution.py:105
  68.5 16.7 %all-to-all-done.4 = bf16[16,32,1024]{2,1,0:T(8,128)(2,1)S(1)} async-done(((bf16[16,32,1024]{2,1,0:T(8,128)(2,1)}), bf16[16,32,1024]{2,1,0:T(8,128)(2,1)S(1)}, u32[]{:S(2)}, u32[]{:S(2)}) %all-to-all-start.4) | async-done | bytes 1048608 | tf_op jit(solution)/shard_map/all_to_all | solution.py:97
  85.2 6.3 %all-to-all-start.3 = ((bf16[16,32,1024]{2,1,0:T(8,128)(2,1)}), bf16[16,32,1024]{2,1,0:T(8,128)(2,1)S(1)}, u32[]{:S(2)}, u32[]{:S(2)}) async-start(bf16[16,32,1024]{2,1,0:T(8,128)(2,1)} %bitcast.41), calls=%async_computation.3 | async-start | bytes 2097152 | tf_op jit(solution)/shard_map/all_to_all | solution.py:97
  91.5 0.0 copy-start.2
  91.5 3.1 %collective-permute-start.1 = (bf16[512,1024]{1,0:T(8,128)(2,1)S(1)}, bf16[512,1024]{1,0:T(8,128)(2,1)S(1)}, u32[]{:S(2)}, u32[]{:S(2)}) collective-permute-start(bf16[512,1024]{1,0:T(8,128)(2,1)S(1)} %bitcast.39), channel_id=1, source_target_pairs={{0,1},{1,0},{2,3},{3,2},{4,5},{5,4},{6,7},{7,6},{8,9},{9,8},{10,11... | collective-permute-start | bytes 3145736 | tf_op jit(solution)/shard_map/ppermute | solution.py:119
  94.6 1.8 %fusion.2 = f32[576,1024]{1,0:T(8,128)S(1)} fusion(bf16[512,1024]{1,0:T(8,128)(2,1)S(1)} %bitcast.40, bf16[4,128,576]{1,2,0:T(8,128)(2,1)} %copy-done.3), kind=kOutput, calls=%fused_computation.5 | convolution fusion | flops 603979776 | bytes 3997696 | tf_op jit(solution)/shard_map/dot_general | solution.py:109
  96.4 0.4 collective-permute-done.1
  96.9 0.0 copy-done.2
  96.9 2.2 %add_bitcast_fusion = f32[1024,576]{0,1:T(8,128)} fusion(f32[576,1024]{1,0:T(8,128)S(1)} %fusion.2, bf16[512,1024]{1,0:T(8,128)(2,1)S(1)} %collective-permute-done.1, bf16[4,128,576]{1,2,0:T(8,128)(2,1)S(1)} %copy-done.2), kind=kOutput, calls=%fused_computation | convolution fusion | flops 604569600 | bytes 6356992 | tf_op jit(solution)/shard_map/dot_general | solution.py:109
  99.0 21.5 %all-to-all-done.3 = bf16[16,32,1024]{2,1,0:T(8,128)(2,1)S(1)} async-done(((bf16[16,32,1024]{2,1,0:T(8,128)(2,1)}), bf16[16,32,1024]{2,1,0:T(8,128)(2,1)S(1)}, u32[]{:S(2)}, u32[]{:S(2)}) %all-to-all-start.3) | async-done | bytes 1048608 | tf_op jit(solution)/shard_map/all_to_all | solution.py:97
  120.5 0.8 reduce_sum.12
  (1 shorter events, 0.0 us)
Async XLA Ops:
  0.6 57.1 %copy-start = (bf16[1024,576]{0,1:T(8,128)(2,1)S(1)}, bf16[1024,576]{0,1:T(8,128)(2,1)}, u32[]{:S(2)}) copy-start(bf16[1024,576]{0,1:T(8,128)(2,1)} %param.5) | copy-start | bytes 3538948
  18.3 22.0 %copy-start.4 = (bf16[32,1024]{1,0:T(8,128)(2,1)S(1)}, bf16[32,1024]{1,0:T(8,128)(2,1)}, u32[]{:S(2)}) copy-start(bf16[32,1024]{1,0:T(8,128)(2,1)} %param.4) | copy-start | bytes 196612
  19.2 11.3 %all-to-all-start.2 = ((bf16[4,128,576]{1,2,0:T(8,128)(2,1)}), bf16[4,128,576]{1,2,0:T(8,128)(2,1)S(1)}, u32[]{:S(2)}, u32[]{:S(2)}) async-start(bf16[4,128,576]{1,2,0:T(8,128)(2,1)} %broadcast_in_dim.23), calls=%async_computation.2 | async-start | bytes 1179648 | tf_op jit(solution)/shard_map/all_to_all | solution.py:97
  30.5 27.3 %copy-start.1 = (bf16[4,128,576]{1,2,0:T(8,128)(2,1)}, bf16[4,128,576]{1,2,0:T(8,128)(2,1)S(1)}, u32[]{:S(2)}) copy-start(bf16[4,128,576]{1,2,0:T(8,128)(2,1)S(1)} %all-to-all-done.2) | copy-start | bytes 1769476
  40.2 26.3 %copy-start.3 = (bf16[4,128,576]{1,2,0:T(8,128)(2,1)}, bf16[4,128,576]{1,2,0:T(8,128)(2,1)S(1)}, u32[]{:S(2)}) copy-start(bf16[4,128,576]{1,2,0:T(8,128)(2,1)S(1)} %all_to_all.26) | copy-start | bytes 1769476
  41.4 43.8 %all-to-all-start.4 = ((bf16[16,32,1024]{2,1,0:T(8,128)(2,1)}), bf16[16,32,1024]{2,1,0:T(8,128)(2,1)S(1)}, u32[]{:S(2)}, u32[]{:S(2)}) async-start(bf16[16,32,1024]{2,1,0:T(8,128)(2,1)} %broadcast_in_dim.24), calls=%async_computation.4 | async-start | bytes 2097152 | tf_op jit(solution)/shard_map/all_to_all | solution.py:97
  58.8 7.7 %collective-permute-start = (bf16[512,1024]{1,0:T(8,128)(2,1)S(1)}, bf16[512,1024]{1,0:T(8,128)(2,1)S(1)}, u32[]{:S(2)}, u32[]{:S(2)}) collective-permute-start(bf16[512,1024]{1,0:T(8,128)(2,1)S(1)} %convolution_convert_fusion), channel_id=1, source_target_pairs={{0,1},{1,0},{2,3},{3,2},{4,5},{5,4},{6,7},{7,6},{8,9},{9,8},{10,11... | collective-permute-start | bytes 3145736 | tf_op jit(solution)/shard_map/ppermute | solution.py:128
  85.2 35.3 %all-to-all-start.3 = ((bf16[16,32,1024]{2,1,0:T(8,128)(2,1)}), bf16[16,32,1024]{2,1,0:T(8,128)(2,1)S(1)}, u32[]{:S(2)}, u32[]{:S(2)}) async-start(bf16[16,32,1024]{2,1,0:T(8,128)(2,1)} %bitcast.41), calls=%async_computation.3 | async-start | bytes 2097152 | tf_op jit(solution)/shard_map/all_to_all | solution.py:97
  91.5 5.4 %copy-start.2 = (bf16[4,128,576]{1,2,0:T(8,128)(2,1)S(1)}, bf16[4,128,576]{1,2,0:T(8,128)(2,1)}, u32[]{:S(2)}) copy-start(bf16[4,128,576]{1,2,0:T(8,128)(2,1)} %copy-done.1) | copy-start | bytes 1769476
  91.5 5.4 %collective-permute-start.1 = (bf16[512,1024]{1,0:T(8,128)(2,1)S(1)}, bf16[512,1024]{1,0:T(8,128)(2,1)S(1)}, u32[]{:S(2)}, u32[]{:S(2)}) collective-permute-start(bf16[512,1024]{1,0:T(8,128)(2,1)S(1)} %bitcast.39), channel_id=1, source_target_pairs={{0,1},{1,0},{2,3},{3,2},{4,5},{5,4},{6,7},{7,6},{8,9},{9,8},{10,11... | collective-permute-start | bytes 3145736 | tf_op jit(solution)/shard_map/ppermute | solution.py:119

commit v2 on v1

v2 whole, which is shorter than its diff:
```python
import math

import jax
import jax.numpy as jnp
from jax import lax
from jax.experimental import pallas as pl
from jax.experimental.pallas import tpu as pltpu
from jax.sharding import Mesh, PartitionSpec as P

QHEADS = 128
KVHEADS = 8
HEAD = 128
ROTATED = (QHEADS + KVHEADS) * HEAD

HALF_PI = (1.5703125, 4.837512969970703e-4, 7.549789948768648e-8)
ROW = ("yh", "x")
COL = ("yl", "z4", "z2", "z1", "c")
SWAP = ((0, 1), (1, 0))


def scaled_freq(within):
    base = jnp.exp(-(2.0 * within.astype(jnp.float32) / HEAD) * math.log(500000.0))
    wave = 2.0 * math.pi / base
    smooth = (8192.0 / wave - 1.0) / 3.0
    middle = (1.0 - smooth) * base / 8.0 + smooth * base
    return jnp.where(wave < 2048.0, base, jnp.where(wave > 8192.0, base / 8.0, middle))


def sine_cosine(angle):
    turns = jnp.floor(angle * (2.0 / math.pi) + 0.5)
    rest = angle
    for part in HALF_PI:
        rest = rest - turns * part
    square = rest * rest
    sine = rest + rest * square * (
        -1.6666654611e-1 + square * (8.3321608736e-3 + square * -1.9515295891e-4)
    )
    cosine = (
        1.0
        - 0.5 * square
        + square * square * (4.166664568298827e-2 + square * (-1.388731625493765e-3 + square * 2.443315711809948e-5))
    )
    quarter = turns.astype(jnp.int32)
    odd = (quarter & 1) == 1
    sine, cosine = jnp.where(odd, cosine, sine), jnp.where(odd, sine, cosine)
    sine = jnp.where((quarter & 2) == 2, -sine, sine)
    cosine = jnp.where(((quarter + 1) & 2) == 2, -cosine, cosine)
    return sine, cosine


def unrotate_kernel(place_ref, positions_ref, own_ref, other_ref, out_ref):
    rows, width = own_ref.shape
    core = place_ref[1]
    wanted = lax.broadcasted_iota(jnp.int32, (rows, 2 * rows), 0) + core * rows
    column = lax.broadcasted_iota(jnp.int32, (rows, 2 * rows), 1)
    spread = jnp.where(wanted == column, positions_ref[...].astype(jnp.float32), 0.0)
    positions = jnp.sum(spread, axis=1, keepdims=True)
    lane = lax.broadcasted_iota(jnp.int32, (8, HEAD), 1)
    source = lax.broadcasted_iota(jnp.int32, (HEAD, HEAD), 0)
    target = lax.broadcasted_iota(jnp.int32, (HEAD, HEAD), 1)
    partner = jnp.where(source == (target ^ 1), jnp.where((target & 1) == 0, 1.0, -1.0), 0.0).astype(jnp.bfloat16)
    for side, (grad_ref, col_start) in enumerate(((own_ref, place_ref[0]), (other_ref, place_ref[2]))):
        freq = scaled_freq(((col_start + lane) & (HEAD - 1)) >> 1)[:1]
        sine, cosine = sine_cosine(positions * freq)
        for start in range(0, width, HEAD):
            size = min(HEAD, width - start)
            block = grad_ref[:, start : start + size]
            swapped = jnp.dot(block, partner[:size, :size], preferred_element_type=jnp.float32)
            turned = block.astype(jnp.float32) * cosine[:, :size] + swapped * sine[:, :size]
            columns = col_start + start + lax.broadcasted_iota(jnp.int32, (rows, size), 1)
            result = jnp.where(columns < ROTATED, turned, block.astype(jnp.float32)).astype(jnp.bfloat16)
            for copy in range(out_ref.shape[0]):
                out_ref[copy, :, side * width + start : side * width + start + size] = result


def unrotate(own, other, positions, place, copies):
    rows, width = own.shape
    return pl.pallas_call(
        unrotate_kernel,
        out_shape=jax.ShapeDtypeStruct((copies, rows, 2 * width), jnp.bfloat16),
        in_specs=[pl.BlockSpec(memory_space=pltpu.SMEM)] + [pl.BlockSpec(memory_space=pltpu.VMEM)] * 3,
        out_specs=pl.BlockSpec(memory_space=pltpu.VMEM),
        name="unrotate",
    )(place, positions.reshape(1, 2 * rows), own, other)


def exchange(parts, axes):
    return lax.all_to_all(parts, axes, 0, 0, tiled=True)


def copies_of(array, count):
    return jnp.broadcast_to(array[None], (count, *array.shape))


def swapped(array, axis):
    return lax.ppermute(array, axis, SWAP)


def in_order(own, other, axis, dim):
    first = lax.axis_index(axis) == 0
    return jnp.concatenate([jnp.where(first, own, other), jnp.where(first, other, own)], dim)


def contract(left, right, left_dim, right_dim):
    dims = (((left_dim,), (right_dim,)), ((), ()))
    return lax.dot_general(left, right, dims, preferred_element_type=jnp.float32)


def per_device(inputs, weight, grad_out, positions):
    width = weight.shape[1]
    tokens, model = inputs.shape
    core = lax.axis_index("c")
    col_start = lax.axis_index(COL) * width
    place = jnp.stack([col_start, core, col_start + (1 - 2 * core) * width]).astype(jnp.int32)

    upper, lower = grad_out[:tokens], grad_out[tokens:]
    first = core == 0
    other_raw = swapped(jnp.where(first, lower, upper), "c")
    sent = unrotate(jnp.where(first, upper, lower), other_raw, positions, place, lax.axis_size("yh"))
    sent, inputs, weight = lax.optimization_barrier((sent, inputs, weight))
    other_weight = swapped(weight, "c")

    own_inputs = inputs.reshape(1, 1, 1, tokens, model)
    for dim, axis in ((2, "z4"), (0, "z2"), (1, "z1")):
        own_inputs = in_order(own_inputs, swapped(own_inputs, axis), axis, dim)
    own_inputs = own_inputs.reshape(4, 2 * tokens, model)
    own_inputs = jnp.stack([own_inputs, swapped(own_inputs, "yl")], 1).reshape(-1, model)
    other_inputs = swapped(own_inputs, "c")

    grads = exchange(sent, "yh").reshape(2, -1, 2 * width)
    yl = lax.axis_index("yl") == 0
    grads = jnp.stack([jnp.where(yl, grads[0], grads[1]), jnp.where(yl, grads[1], grads[0])])
    grads = exchange(copies_of(grads, lax.axis_size("x")), "x")
    own_columns = grads[..., :width].reshape(-1, width)
    other_columns = swapped(grads[..., width:].reshape(-1, width), "c")

    both = jnp.concatenate([weight, other_weight], 1)
    far = contract(grads[:, 1].reshape(-1, 2 * width), both, 1, 1).astype(jnp.bfloat16)
    arrived = swapped(far, "yl").astype(jnp.float32)
    near = (contract(grads[:, 0].reshape(-1, 2 * width), both, 1, 1) + arrived).astype(jnp.bfloat16)
    parts = exchange(near.reshape(8, tokens, model), ("z2", "z1", "z4"))
    input_grad = parts.astype(jnp.float32).sum(axis=0).astype(jnp.bfloat16)

    weight_grad = contract(own_inputs, own_columns, 0, 0) + contract(other_inputs, other_columns, 0, 0)
    return input_grad, weight_grad


def solution(mesh):
    sizes = {"yh": 4, "x": 4, "yl": 2, "z4": 2, "z2": 2, "z1": 2, "c": 2}
    finer = Mesh(mesh.devices.reshape(tuple(sizes.values())), tuple(sizes))
    in_specs = (P(COL, ROW), P(ROW, COL), P(ROW, COL), P(ROW))
    out_specs = (P(COL, ROW), P(ROW, COL))
    return jax.shard_map(per_device, mesh=finer, in_specs=in_specs, out_specs=out_specs, check_vma=False)
```

time: 122 us -> 102 us (0.84)
  the two profiles are of different devices: /device:TPU:25 before, /device:TPU:67 now
where the time goes in v2:
time: 102 us
  starting transfers between devices  52.3 us (51%)
  waiting for transfers between devices  22 us (22%)
  matrix products  12 us (12%)
  local copies, waits for them, and re-layouts  7.63 us (7%)
  other arithmetic  4.95 us (5%)
  Pallas kernels  1.81 us (2%)
    ppermute x9, starting transfers between devices, swapped(): return lax.ppermute(array, axis, SWAP)  34.7 us
    all_to_all x3, starting transfers between devices, exchange(): return lax.all_to_all(parts, axes, 0, 0, tiled=True)  17.6 us
    dot_general x4, matrix products, contract(): lax.dot_general(left, right, dims, preferred_element_type=jnp.float32)  12 us
    all_to_all x3, waiting for transfers between devices, exchange(): return lax.all_to_all(parts, axes, 0, 0, tiled=True)  11.8 us
    ppermute x9, waiting for transfers between devices, swapped(): return lax.ppermute(array, axis, SWAP)  10.2 us
    concatenate x1, local copies, waits for them, and re-layouts, per_device(): both = jnp.concatenate([weight, other_weight], 1)  2.37 us
  transfers between devices with their start and end apart: 12, of which 7 were waited for; matrix products, arithmetic and copies ran while one was open for 22% of the time, Pallas kernels for 0%

profile of v2, /device:TPU:67, one launch (start us, length us, event | category | flops | bytes accessed | tf_op | source)
XLA Modules:
  0.0 101.6 jit_solution(6163030338421626911)
XLA Ops:
  0.6 1.4 %broadcast_select_fusion.8 = (bf16[32,576]{1,0:T(8,128)(2,1)S(1)}, bf16[32,576]{1,0:T(8,128)(2,1)}) fusion(pred[]{:T(512)S(6)} %eq.16, bf16[64,576]{1,0:T(8,128)(2,1)} %param.6), kind=kLoop, calls=%fused_computation.19 | loop fusion | flops 36864 | bytes 147457 | tf_op jit(solution)/shard_map/jit(_where)/select_n | solution.py:118
  2.1 2.6 %collective-permute-start = (bf16[32,576]{1,0:T(8,128)(2,1)S(1)}, bf16[32,576]{1,0:T(8,128)(2,1)S(1)}, u32[]{:S(2)}, u32[]{:S(2)}) collective-permute-start(bf16[32,576]{1,0:T(8,128)(2,1)S(1)} %get-tuple-element.18), channel_id=1, source_target_pairs={{0,1},{1,0},{2,3},{3,2},{4,5},{5,4},{6,7},{7,6},{8,9},{9,8},{10,11... | collective-permute-start | bytes 110600 | tf_op jit(solution)/shard_map/ppermute | solution.py:96
  4.7 0.6 pad_add_fusion.place_ref
  5.3 0.2 collective-permute-done.other_ref
  5.5 0.0 copy-start.2
  5.5 0.6 copy-done.2
  6.1 1.8 %unrotate.1 = bf16[4,32,1152]{2,1,0:T(8,128)(2,1)} custom-call(s32[3]{0:T(128)} %pad_add_fusion.place_ref, s32[1,64]{1,0:T(1,128)} %bitcast.39, bf16[32,576]{1,0:T(8,128)(2,1)} %get-tuple-element.19.own_ref, bf16[32,576]{1,0:T(8,128)(2,1)} %copy-done.2), custom_call_target="tpu_custom_call" | custom-call | tf_op jit(solution)/shard_map/unrotate/pallas_call | solution.py:78
  7.9 9.7 %collective-permute-start.3 = (bf16[1,1,1,32,1024]{4,3,2,1,0:T(8,128)(2,1)}, bf16[1,1,1,32,1024]{4,3,2,1,0:T(8,128)(2,1)S(1)}, u32[]{:S(2)}, u32[]{:S(2)}) collective-permute-start(bf16[1,1,1,32,1024]{4,3,2,1,0:T(8,128)(2,1)} %bitcast.38), channel_id=1, source_target_pairs={{0,8},{8,0},{1,9},{9,1},{2,10},{10,2},{3,11},{11,3},{4,12},{12,4},... | collective-permute-start | bytes 196616 | tf_op jit(solution)/shard_map/ppermute | solution.py:96
  17.7 6.8 %all-to-all-start = ((bf16[4,32,1152]{2,1,0:T(8,128)(2,1)}), bf16[4,32,1152]{2,1,0:T(8,128)(2,1)S(1)}, u32[]{:S(2)}, u32[]{:S(2)}) async-start(bf16[4,32,1152]{2,1,0:T(8,128)(2,1)} %unrotate.1), calls=%async_computation | async-start | bytes 589824 | tf_op jit(solution)/shard_map/all_to_all | solution.py:88
  24.5 0.0 collective-permute-done.3
  24.5 0.9 broadcast_select_fusion.7
  25.4 4.0 %collective-permute-start.4 = (bf16[1,1,2,32,1024]{4,3,2,1,0:T(8,128)(2,1)S(1)}, bf16[1,1,2,32,1024]{4,3,2,1,0:T(8,128)(2,1)S(1)}, u32[]{:S(2)}, u32[]{:S(2)}) collective-permute-start(bf16[1,1,2,32,1024]{4,3,2,1,0:T(8,128)(2,1)S(1)} %pad_maximum_fusion.4), channel_id=1, source_target_pairs={{0,4},{4,0},{1,5},{5,1},{2,6},{6,2},{3,7},{7,3},{8,12},{12,8},{9,1... | collective-permute-start | bytes 393224 | tf_op jit(solution)/shard_map/ppermute | solution.py:96
  29.4 3.1 %collective-permute-start.1 = (bf16[1024,576]{0,1:T(8,128)(2,1)}, bf16[1024,576]{0,1:T(8,128)(2,1)}, u32[]{:S(2)}, u32[]{:S(2)}) collective-permute-start(bf16[1024,576]{0,1:T(8,128)(2,1)} %param.5), channel_id=1, source_target_pairs={{0,1},{1,0},{2,3},{3,2},{4,5},{5,4},{6,7},{7,6},{8,9},{9,8},{10,11... | collective-permute-start | bytes 3538952 | tf_op jit(solution)/shard_map/ppermute | solution.py:96
  32.5 2.9 %collective-permute-done.4 = bf16[1,1,2,32,1024]{4,3,2,1,0:T(8,128)(2,1)S(1)} collective-permute-done((bf16[1,1,2,32,1024]{4,3,2,1,0:T(8,128)(2,1)S(1)}, bf16[1,1,2,32,1024]{4,3,2,1,0:T(8,128)(2,1)S(1)}, u32[]{:S(2)}, u32[]{:S(2)}) %collective-permute-start.4) | collective-permute-done | bytes 131104 | tf_op jit(solution)/shard_map/ppermute | solution.py:96
  35.4 0.0 all-to-all-done
  35.5 0.0 copy-start
  35.5 1.2 %broadcast_in_dim.2 = bf16[4,2,64,1152]{3,2,1,0:T(8,128)(2,1)} broadcast(bf16[2,64,1152]{2,1,0:T(8,128)(2,1)S(1)} %pad_maximum_fusion.2), dimensions={1,2,3} | broadcast | bytes 1474560 | tf_op jit(solution)/shard_map/broadcast_in_dim | solution.py:92
  36.7 4.3 %all-to-all-start.1 = ((bf16[4,2,64,1152]{3,2,1,0:T(8,128)(2,1)}), bf16[4,2,64,1152]{3,2,1,0:T(8,128)(2,1)S(1)}, u32[]{:S(2)}, u32[]{:S(2)}) async-start(bf16[4,2,64,1152]{3,2,1,0:T(8,128)(2,1)} %broadcast_in_dim.2), calls=%async_computation.1 | async-start | bytes 2359296 | tf_op jit(solution)/shard_map/all_to_all | solution.py:88
  41.0 2.2 %collective-permute-start.5 = (bf16[2,1,2,32,1024]{4,3,2,1,0:T(8,128)(2,1)S(1)}, bf16[2,1,2,32,1024]{4,3,2,1,0:T(8,128)(2,1)S(1)}, u32[]{:S(2)}, u32[]{:S(2)}) collective-permute-start(bf16[2,1,2,32,1024]{4,3,2,1,0:T(8,128)(2,1)S(1)} %pad_maximum_fusion.3), channel_id=1, source_target_pairs={{0,2},{2,0},{1,3},{3,1},{4,6},{6,4},{5,7},{7,5},{8,10},{10,8},{9,1... | collective-permute-start | bytes 786440 | tf_op jit(solution)/shard_map/ppermute | solution.py:96
  43.2 0.0 copy-done
  43.2 1.1 %constant_dynamic-update-slice_fusion.1 = bf16[1024,1152]{0,1:T(8,128)(2,1)} fusion(bf16[1024,576]{0,1:T(8,128)(2,1)S(1)} %copy-done), kind=kLoop, calls=%fused_computation.22 | loop fusion | bytes 2359296
  44.3 4.8 %collective-permute-done.5 = bf16[2,1,2,32,1024]{4,3,2,1,0:T(8,128)(2,1)S(1)} collective-permute-done((bf16[2,1,2,32,1024]{4,3,2,1,0:T(8,128)(2,1)S(1)}, bf16[2,1,2,32,1024]{4,3,2,1,0:T(8,128)(2,1)S(1)}, u32[]{:S(2)}, u32[]{:S(2)}) %collective-permute-start.5) | collective-permute-done | bytes 262176 | tf_op jit(solution)/shard_map/ppermute | solution.py:96
  49.2 0.1 pad_maximum_fusion.1
  49.3 2.5 %collective-permute-start.6 = (bf16[4,64,1024]{2,1,0:T(8,128)(2,1)S(1)}, bf16[4,64,1024]{2,1,0:T(8,128)(2,1)S(1)}, u32[]{:S(2)}, u32[]{:S(2)}) collective-permute-start(bf16[4,64,1024]{2,1,0:T(8,128)(2,1)S(1)} %bitcast.28), channel_id=1, source_target_pairs={{0,16},{16,0},{1,17},{17,1},{2,18},{18,2},{3,19},{19,3},{4,20},{20... | collective-permute-start | bytes 1572872 | tf_op jit(solution)/shard_map/ppermute | solution.py:96
  51.8 0.0 collective-permute-done.1
  51.8 2.4 %constant_dynamic-update-slice_fusion = bf16[1024,1152]{0,1:T(8,128)(2,1)} fusion(bf16[1024,1152]{0,1:T(8,128)(2,1)} %constant_dynamic-update-slice_fusion.1, bf16[1024,576]{0,1:T(8,128)(2,1)} %collective-permute-done.1), kind=kLoop, calls=%fused_computation.21 | loop fusion | bytes 2359296 | tf_op jit(solution)/shard_map/concatenate | solution.py:137
  54.1 0.9 all-to-all-done.1
  55.1 0.9 fusion.3
  56.0 3.3 %convolution_convert_fusion = bf16[256,1024]{1,0:T(8,128)(2,1)} fusion(bf16[256,1152]{1,0:T(8,128)(2,1)S(1)} %bitcast.32, bf16[1024,1152]{0,1:T(8,128)(2,1)} %constant_dynamic-update-slice_fusion), kind=kOutput, calls=%fused_computation.2 | convolution fusion | flops 604241920 | bytes 3473408 | tf_op jit(solution)/shard_map/dot_general | solution.py:106
  59.3 2.5 %collective-permute-start.2 = (bf16[256,1024]{1,0:T(8,128)(2,1)}, bf16[256,1024]{1,0:T(8,128)(2,1)}, u32[]{:S(2)}, u32[]{:S(2)}) collective-permute-start(bf16[256,1024]{1,0:T(8,128)(2,1)} %convolution_convert_fusion), channel_id=1, source_target_pairs={{0,16},{16,0},{1,17},{17,1},{2,18},{18,2},{3,19},{19,3},{4,20},{20... | collective-permute-start | bytes 1572872 | tf_op jit(solution)/shard_map/ppermute | solution.py:96
  61.8 0.3 collective-permute-done.6
  62.1 0.0 copy-start.1
  62.1 1.1 %pad_maximum_fusion = bf16[4,2,64,1024]{3,2,1,0:T(8,128)(2,1)} fusion(bf16[4,1,64,1024]{3,2,1,0:T(8,128)(2,1)S(1)} %bitcast.36, bf16[4,1,64,1024]{3,2,1,0:T(8,128)(2,1)S(1)} %bitcast.29), kind=kLoop, calls=%fused_computation.4 | loop fusion | flops 524288 | bytes 2097152 | tf_op jit(solution)/shard_map/stack | solution.py:127
  63.3 0.0 copy-done.1
  63.3 6.2 %collective-permute-start.7 = (bf16[512,1024]{1,0:T(8,128)(2,1)}, bf16[512,1024]{1,0:T(8,128)(2,1)S(1)}, u32[]{:S(2)}, u32[]{:S(2)}) collective-permute-start(bf16[512,1024]{1,0:T(8,128)(2,1)} %bitcast.15), channel_id=1, source_target_pairs={{0,1},{1,0},{2,3},{3,2},{4,5},{5,4},{6,7},{7,6},{8,9},{9,8},{10,11... | collective-permute-start | bytes 3145736 | tf_op jit(solution)/shard_map/ppermute | solution.py:96
  69.4 0.4 slice.41
  69.8 1.1 %copy.6 = bf16[512,576]{0,1:T(8,128)(2,1)} copy(bf16[512,576]{1,0:T(8,128)(2,1)S(1)} %bitcast.27) | data formatting | bytes 1179648 | tf_op jit(solution)/shard_map/reshape | solution.py:135
  70.9 1.9 %collective-permute-start.8 = (bf16[512,576]{0,1:T(8,128)(2,1)}, bf16[512,576]{0,1:T(8,128)(2,1)}, u32[]{:S(2)}, u32[]{:S(2)}) collective-permute-start(bf16[512,576]{0,1:T(8,128)(2,1)} %copy.6), channel_id=1, source_target_pairs={{0,1},{1,0},{2,3},{3,2},{4,5},{5,4},{6,7},{7,6},{8,9},{9,8},{10,11... | collective-permute-start | bytes 1769480 | tf_op jit(solution)/shard_map/ppermute | solution.py:96
  72.8 1.9 %collective-permute-done.2 = bf16[256,1024]{1,0:T(8,128)(2,1)} collective-permute-done((bf16[256,1024]{1,0:T(8,128)(2,1)}, bf16[256,1024]{1,0:T(8,128)(2,1)}, u32[]{:S(2)}, u32[]{:S(2)}) %collective-permute-start.2) | collective-permute-done | bytes 524320 | tf_op jit(solution)/shard_map/ppermute | solution.py:96
  74.7 3.6 %fusion = bf16[256,1024]{1,0:T(8,128)(2,1)} fusion(bf16[256,1152]{1,0:T(8,128)(2,1)} %bitcast.31, bf16[1024,1152]{0,1:T(8,128)(2,1)} %constant_dynamic-update-slice_fusion, bf16[256,1024]{1,0:T(8,128)(2,1)} %collective-permute-done.2), kind=kOutput, calls=%fused_computation.3 | convolution fusion | flops 604766208 | bytes 3997696 | tf_op jit(solution)/shard_map/dot_general | solution.py:106
  78.3 6.5 %all-to-all-start.2 = ((bf16[8,32,1024]{2,1,0:T(8,128)(2,1)}), bf16[8,32,1024]{2,1,0:T(8,128)(2,1)S(1)}, u32[]{:S(2)}, u32[]{:S(2)}) async-start(bf16[8,32,1024]{2,1,0:T(8,128)(2,1)} %bitcast.35), calls=%async_computation.2 | async-start | bytes 1048576 | tf_op jit(solution)/shard_map/all_to_all | solution.py:88
  84.8 1.9 %fusion.1 = f32[1024,576,1,1]{0,1,3,2:T(8,128)S(1)} fusion(bf16[4,2,64,1152]{3,2,1,0:T(8,128)(2,1)S(1)} %all-to-all-done.1, bf16[4,1,64,1024]{3,2,1,0:T(8,128)(2,1)} %bitcast.37, bf16[4,1,64,1024]{3,2,1,0:T(8,128)(2,1)S(1)} %bitcast.30), kind=kOutput, calls=%fused_computation.5 | convolution fusion | flops 604504064 | bytes 4063232 | tf_op jit(solution)/shard_map/dot_general | solution.py:106
  86.7 0.0 collective-permute-done.8
  86.7 0.0 collective-permute-done.7
  86.7 3.3 %bitcast_add_fusion = f32[1024,576]{0,1:T(8,128)} fusion(f32[1024,576,1,1]{0,1,3,2:T(8,128)S(1)} %fusion.1, bf16[512,576]{0,1:T(8,128)(2,1)} %collective-permute-done.8, bf16[512,1024]{1,0:T(8,128)(2,1)S(1)} %collective-permute-done.7), kind=kOutput, calls=%fused_computation | convolution fusion | flops 604569600 | bytes 6356992 | tf_op jit(solution)/shard_map/dot_general | solution.py:106
  90.0 10.9 %all-to-all-done.2 = bf16[8,32,1024]{2,1,0:T(8,128)(2,1)S(1)} async-done(((bf16[8,32,1024]{2,1,0:T(8,128)(2,1)}), bf16[8,32,1024]{2,1,0:T(8,128)(2,1)S(1)}, u32[]{:S(2)}, u32[]{:S(2)}) %all-to-all-start.2) | async-done | bytes 524320 | tf_op jit(solution)/shard_map/all_to_all | solution.py:88
  100.9 0.7 reduce_sum.12
  (6 shorter events, 0.2 us)
Async XLA Ops:
  2.1 3.4 %collective-permute-start = (bf16[32,576]{1,0:T(8,128)(2,1)S(1)}, bf16[32,576]{1,0:T(8,128)(2,1)S(1)}, u32[]{:S(2)}, u32[]{:S(2)}) collective-permute-start(bf16[32,576]{1,0:T(8,128)(2,1)S(1)} %get-tuple-element.18), channel_id=1, source_target_pairs={{0,1},{1,0},{2,3},{3,2},{4,5},{5,4},{6,7},{7,6},{8,9},{9,8},{10,11... | collective-permute-start | bytes 110600 | tf_op jit(solution)/shard_map/ppermute | solution.py:96
  5.5 0.6 copy-start.2
  7.9 16.6 %collective-permute-start.3 = (bf16[1,1,1,32,1024]{4,3,2,1,0:T(8,128)(2,1)}, bf16[1,1,1,32,1024]{4,3,2,1,0:T(8,128)(2,1)S(1)}, u32[]{:S(2)}, u32[]{:S(2)}) collective-permute-start(bf16[1,1,1,32,1024]{4,3,2,1,0:T(8,128)(2,1)} %bitcast.38), channel_id=1, source_target_pairs={{0,8},{8,0},{1,9},{9,1},{2,10},{10,2},{3,11},{11,3},{4,12},{12,4},... | collective-permute-start | bytes 196616 | tf_op jit(solution)/shard_map/ppermute | solution.py:96
  17.7 17.8 %all-to-all-start = ((bf16[4,32,1152]{2,1,0:T(8,128)(2,1)}), bf16[4,32,1152]{2,1,0:T(8,128)(2,1)S(1)}, u32[]{:S(2)}, u32[]{:S(2)}) async-start(bf16[4,32,1152]{2,1,0:T(8,128)(2,1)} %unrotate.1), calls=%async_computation | async-start | bytes 589824 | tf_op jit(solution)/shard_map/all_to_all | solution.py:88
  25.4 10.0 %collective-permute-start.4 = (bf16[1,1,2,32,1024]{4,3,2,1,0:T(8,128)(2,1)S(1)}, bf16[1,1,2,32,1024]{4,3,2,1,0:T(8,128)(2,1)S(1)}, u32[]{:S(2)}, u32[]{:S(2)}) collective-permute-start(bf16[1,1,2,32,1024]{4,3,2,1,0:T(8,128)(2,1)S(1)} %pad_maximum_fusion.4), channel_id=1, source_target_pairs={{0,4},{4,0},{1,5},{5,1},{2,6},{6,2},{3,7},{7,3},{8,12},{12,8},{9,1... | collective-permute-start | bytes 393224 | tf_op jit(solution)/shard_map/ppermute | solution.py:96
  29.4 22.4 %collective-permute-start.1 = (bf16[1024,576]{0,1:T(8,128)(2,1)}, bf16[1024,576]{0,1:T(8,128)(2,1)}, u32[]{:S(2)}, u32[]{:S(2)}) collective-permute-start(bf16[1024,576]{0,1:T(8,128)(2,1)} %param.5), channel_id=1, source_target_pairs={{0,1},{1,0},{2,3},{3,2},{4,5},{5,4},{6,7},{7,6},{8,9},{9,8},{10,11... | collective-permute-start | bytes 3538952 | tf_op jit(solution)/shard_map/ppermute | solution.py:96
  35.5 7.8 %copy-start = (bf16[1024,576]{0,1:T(8,128)(2,1)S(1)}, bf16[1024,576]{0,1:T(8,128)(2,1)}, u32[]{:S(2)}) copy-start(bf16[1024,576]{0,1:T(8,128)(2,1)} %param.5) | copy-start | bytes 3538948
  36.7 18.4 %all-to-all-start.1 = ((bf16[4,2,64,1152]{3,2,1,0:T(8,128)(2,1)}), bf16[4,2,64,1152]{3,2,1,0:T(8,128)(2,1)S(1)}, u32[]{:S(2)}, u32[]{:S(2)}) async-start(bf16[4,2,64,1152]{3,2,1,0:T(8,128)(2,1)} %broadcast_in_dim.2), calls=%async_computation.1 | async-start | bytes 2359296 | tf_op jit(solution)/shard_map/all_to_all | solution.py:88
  41.0 8.2 %collective-permute-start.5 = (bf16[2,1,2,32,1024]{4,3,2,1,0:T(8,128)(2,1)S(1)}, bf16[2,1,2,32,1024]{4,3,2,1,0:T(8,128)(2,1)S(1)}, u32[]{:S(2)}, u32[]{:S(2)}) collective-permute-start(bf16[2,1,2,32,1024]{4,3,2,1,0:T(8,128)(2,1)S(1)} %pad_maximum_fusion.3), channel_id=1, source_target_pairs={{0,2},{2,0},{1,3},{3,1},{4,6},{6,4},{5,7},{7,5},{8,10},{10,8},{9,1... | collective-permute-start | bytes 786440 | tf_op jit(solution)/shard_map/ppermute | solution.py:96
  49.3 12.9 %collective-permute-start.6 = (bf16[4,64,1024]{2,1,0:T(8,128)(2,1)S(1)}, bf16[4,64,1024]{2,1,0:T(8,128)(2,1)S(1)}, u32[]{:S(2)}, u32[]{:S(2)}) collective-permute-start(bf16[4,64,1024]{2,1,0:T(8,128)(2,1)S(1)} %bitcast.28), channel_id=1, source_target_pairs={{0,16},{16,0},{1,17},{17,1},{2,18},{18,2},{3,19},{19,3},{4,20},{20... | collective-permute-start | bytes 1572872 | tf_op jit(solution)/shard_map/ppermute | solution.py:96
  59.3 15.4 %collective-permute-start.2 = (bf16[256,1024]{1,0:T(8,128)(2,1)}, bf16[256,1024]{1,0:T(8,128)(2,1)}, u32[]{:S(2)}, u32[]{:S(2)}) collective-permute-start(bf16[256,1024]{1,0:T(8,128)(2,1)} %convolution_convert_fusion), channel_id=1, source_target_pairs={{0,16},{16,0},{1,17},{17,1},{2,18},{18,2},{3,19},{19,3},{4,20},{20... | collective-permute-start | bytes 1572872 | tf_op jit(solution)/shard_map/ppermute | solution.py:96
  62.1 1.1 %copy-start.1 = (bf16[4,64,1024]{2,1,0:T(8,128)(2,1)}, bf16[4,64,1024]{2,1,0:T(8,128)(2,1)S(1)}, u32[]{:S(2)}) copy-start(bf16[4,64,1024]{2,1,0:T(8,128)(2,1)S(1)} %collective-permute-done.6) | copy-start | bytes 1572868
  63.3 23.4 %collective-permute-start.7 = (bf16[512,1024]{1,0:T(8,128)(2,1)}, bf16[512,1024]{1,0:T(8,128)(2,1)S(1)}, u32[]{:S(2)}, u32[]{:S(2)}) collective-permute-start(bf16[512,1024]{1,0:T(8,128)(2,1)} %bitcast.15), channel_id=1, source_target_pairs={{0,1},{1,0},{2,3},{3,2},{4,5},{5,4},{6,7},{7,6},{8,9},{9,8},{10,11... | collective-permute-start | bytes 3145736 | tf_op jit(solution)/shard_map/ppermute | solution.py:96
  70.9 15.8 %collective-permute-start.8 = (bf16[512,576]{0,1:T(8,128)(2,1)}, bf16[512,576]{0,1:T(8,128)(2,1)}, u32[]{:S(2)}, u32[]{:S(2)}) collective-permute-start(bf16[512,576]{0,1:T(8,128)(2,1)} %copy.6), channel_id=1, source_target_pairs={{0,1},{1,0},{2,3},{3,2},{4,5},{5,4},{6,7},{7,6},{8,9},{9,8},{10,11... | collective-permute-start | bytes 1769480 | tf_op jit(solution)/shard_map/ppermute | solution.py:96
  78.3 22.6 %all-to-all-start.2 = ((bf16[8,32,1024]{2,1,0:T(8,128)(2,1)}), bf16[8,32,1024]{2,1,0:T(8,128)(2,1)S(1)}, u32[]{:S(2)}, u32[]{:S(2)}) async-start(bf16[8,32,1024]{2,1,0:T(8,128)(2,1)} %bitcast.35), calls=%async_computation.2 | async-start | bytes 1048576 | tf_op jit(solution)/shard_map/all_to_all | solution.py:88

commit v3 on v1

v3 whole, which is shorter than its diff:
```python
import math

import jax
import jax.numpy as jnp
from jax import lax
from jax.experimental import pallas as pl
from jax.experimental.pallas import tpu as pltpu
from jax.sharding import Mesh, PartitionSpec as P

QHEADS = 128
KVHEADS = 8
HEAD = 128
ROTATED = (QHEADS + KVHEADS) * HEAD

HALF_PI = (1.5703125, 4.837512969970703e-4, 7.549789948768648e-8)
ROW = ("yh", "x")
COL = ("yl", "z4", "z2", "z1", "c")
SWAP = ((0, 1), (1, 0))
STEP = 256


def scaled_freq(within):
    base = jnp.exp(-(2.0 * within.astype(jnp.float32) / HEAD) * math.log(500000.0))
    wave = 2.0 * math.pi / base
    smooth = (8192.0 / wave - 1.0) / 3.0
    middle = (1.0 - smooth) * base / 8.0 + smooth * base
    return jnp.where(wave < 2048.0, base, jnp.where(wave > 8192.0, base / 8.0, middle))


def sine_cosine(angle):
    turns = jnp.floor(angle * (2.0 / math.pi) + 0.5)
    rest = angle
    for part in HALF_PI:
        rest = rest - turns * part
    square = rest * rest
    sine = rest + rest * square * (
        -1.6666654611e-1 + square * (8.3321608736e-3 + square * -1.9515295891e-4)
    )
    cosine = (
        1.0
        - 0.5 * square
        + square * square * (4.166664568298827e-2 + square * (-1.388731625493765e-3 + square * 2.443315711809948e-5))
    )
    quarter = turns.astype(jnp.int32)
    odd = (quarter & 1) == 1
    sine, cosine = jnp.where(odd, cosine, sine), jnp.where(odd, sine, cosine)
    sine = jnp.where((quarter & 2) == 2, -sine, sine)
    cosine = jnp.where(((quarter + 1) & 2) == 2, -cosine, cosine)
    return sine, cosine


def unrotate_kernel(positions_ref, grad_ref, out_ref):
    rows, width = grad_ref.shape
    col_start = lax.axis_index(COL) * width
    row = lax.broadcasted_iota(jnp.int32, (rows, rows), 0)
    column = lax.broadcasted_iota(jnp.int32, (rows, rows), 1)
    spread = jnp.where(row == column, positions_ref[...].astype(jnp.float32), 0.0)
    positions = jnp.sum(spread, axis=1, keepdims=True)
    lane = lax.broadcasted_iota(jnp.int32, (8, HEAD), 1)
    freq = scaled_freq(((col_start + lane) & (HEAD - 1)) >> 1)[:1]
    sine, cosine = sine_cosine(positions * freq)
    source = lax.broadcasted_iota(jnp.int32, (HEAD, HEAD), 0)
    target = lax.broadcasted_iota(jnp.int32, (HEAD, HEAD), 1)
    partner = jnp.where(source == (target ^ 1), jnp.where((target & 1) == 0, 1.0, -1.0), 0.0).astype(jnp.bfloat16)
    half = out_ref.shape[2]
    for start in range(0, width, HEAD):
        size = min(HEAD, width - start)
        block = grad_ref[:, start : start + size]
        swapped = jnp.dot(block, partner[:size, :size], preferred_element_type=jnp.float32)
        turned = block.astype(jnp.float32) * cosine[:, :size] + swapped * sine[:, :size]
        columns = col_start + start + lax.broadcasted_iota(jnp.int32, (rows, size), 1)
        result = jnp.where(columns < ROTATED, turned, block.astype(jnp.float32)).astype(jnp.bfloat16)
        for copy in range(out_ref.shape[0]):
            for core in range(out_ref.shape[1]):
                out_ref[copy, core, :, start : start + size] = result[core * half : (core + 1) * half]


def unrotate(grad, positions, copies, cores):
    rows, width = grad.shape
    return pl.pallas_call(
        unrotate_kernel,
        out_shape=jax.ShapeDtypeStruct((copies, cores, rows // cores, width), jnp.bfloat16),
        in_specs=[pl.BlockSpec(memory_space=pltpu.VMEM)] * 2,
        out_specs=pl.BlockSpec(memory_space=pltpu.VMEM),
        name="unrotate",
    )(positions.reshape(1, rows), grad)


def arrange_kernel(arrived_ref, out_ref, parts_ref, sem):
    load = pltpu.make_async_copy(arrived_ref, parts_ref, sem)
    load.start()
    load.wait()
    width = parts_ref.shape[3]
    main = width // HEAD * HEAD
    rest = width - main
    yl, core = lax.axis_index("yl"), lax.axis_index("c")
    for far in range(2):
        for z4 in range(2):
            yh = (yl ^ far) * 2 + z4
            own = parts_ref[yh, core]
            other = parts_ref[yh, 1 - core]
            for copy in range(out_ref.shape[0]):
                out_ref[copy, far, z4, :, :main] = own[:, :main]
                out_ref[copy, far, z4, :, main : 2 * main] = other[:, :main]
                out_ref[copy, far, z4, :, 2 * main : 2 * main + rest] = own[:, main:]
                out_ref[copy, far, z4, :, 2 * main + rest :] = other[:, main:]


def arrange(parts, copies):
    tokens, width = parts.shape[2:]
    return pl.pallas_call(
        arrange_kernel,
        out_shape=jax.ShapeDtypeStruct((copies, 2, 2, tokens, 2 * width), jnp.bfloat16),
        in_specs=[pl.BlockSpec(memory_space=pl.ANY)],
        out_specs=pl.BlockSpec(memory_space=pltpu.VMEM),
        scratch_shapes=[pltpu.VMEM(parts.shape, parts.dtype), pltpu.SemaphoreType.DMA],
        compiler_params=pltpu.CompilerParams(vmem_limit_bytes=8 << 20),
        name="arrange",
    )(parts)


def total_of(grads_ref, own_ref, other_ref):
    groups, rows, width = grads_ref.shape
    main = own_ref.shape[0] // HEAD * HEAD
    last = jnp.concatenate([own_ref[main:], other_ref[main:]], axis=0)
    grads = grads_ref[...].reshape(groups * rows, width)
    total = jnp.dot(grads[:, :main], own_ref[:main], preferred_element_type=jnp.float32)
    total += jnp.dot(grads[:, main : 2 * main], other_ref[:main], preferred_element_type=jnp.float32)
    return total + jnp.dot(grads[:, 2 * main :], last, preferred_element_type=jnp.float32)


def load_part(arrived_ref, far, held_ref, sem):
    load = pltpu.make_async_copy(arrived_ref.at[:, far], held_ref, sem)
    load.start()
    load.wait()


def far_product_kernel(arrived_ref, own_ref, other_ref, out_ref, grads_ref, sem):
    @pl.when(pl.program_id(0) == 0)
    def _():
        load_part(arrived_ref, 1, grads_ref, sem)

    out_ref[...] = total_of(grads_ref, own_ref, other_ref).astype(out_ref.dtype)


def near_product_kernel(arrived_ref, own_ref, other_ref, added_ref, out_ref, grads_ref, sem):
    @pl.when(pl.program_id(0) == 0)
    def _():
        load_part(arrived_ref, 0, grads_ref, sem)

    total = total_of(grads_ref, own_ref, other_ref) + added_ref[...].astype(jnp.float32)
    out_ref[...] = total.astype(out_ref.dtype)


def input_product(grads, own_weight, other_weight, added=None):
    groups, _, rows, width = grads.shape
    columns, model = own_weight.shape
    by_column = lambda step: (0, step)
    weights = [pl.BlockSpec((columns, STEP), by_column)] * 2
    part = [pl.BlockSpec((groups * rows, STEP), by_column)]
    near = added is not None
    return pl.pallas_call(
        near_product_kernel if near else far_product_kernel,
        grid=(model // STEP,),
        out_shape=jax.ShapeDtypeStruct((groups * rows, model), jnp.bfloat16),
        in_specs=[pl.BlockSpec(memory_space=pl.ANY)] + weights + part * near,
        out_specs=part[0],
        scratch_shapes=[pltpu.VMEM((groups, rows, width), grads.dtype), pltpu.SemaphoreType.DMA],
        compiler_params=pltpu.CompilerParams(vmem_limit_bytes=12 << 20),
        cost_estimate=pl.CostEstimate(flops=2 * groups * rows * width * model, bytes_accessed=4 << 20, transcendentals=0),
        name="near_product" if near else "far_product",
    )(grads, own_weight, other_weight, *([added] * near))


def blocks_of(groups, size):
    own_yl = lax.axis_index("yl")
    for yl in range(2):
        for z4 in range(2):
            for group in range(groups):
                index = (yl * 2 + z4) * groups + group
                yield index, group, yl ^ own_yl, slice(z4 * size, (z4 + 1) * size)


def lend_kernel(arrived_ref, out_ref, grads_ref, sem):
    load = pltpu.make_async_copy(arrived_ref, grads_ref, sem)
    load.start()
    load.wait()
    groups, _, rows, width = grads_ref.shape
    columns = width // 2
    main = columns // HEAD * HEAD
    rest = columns - main
    half = rows // 2
    for index, group, far, place in blocks_of(groups, half):
        start = index * half
        lent = grads_ref[group, far, place]
        out_ref[start : start + half, :main] = lent[:, main : 2 * main]
        out_ref[start : start + half, main:columns] = lent[:, 2 * main + rest :]
    out_ref[:, columns:] = jnp.zeros_like(out_ref[:, columns:])


def lend(grads):
    groups, _, rows, width = grads.shape
    padded = pl.cdiv(width // 2, HEAD) * HEAD
    return pl.pallas_call(
        lend_kernel,
        out_shape=jax.ShapeDtypeStruct((2 * groups * rows, padded), grads.dtype),
        in_specs=[pl.BlockSpec(memory_space=pl.ANY)],
        out_specs=pl.BlockSpec(memory_space=pltpu.VMEM),
        scratch_shapes=[pltpu.VMEM(grads.shape, grads.dtype), pltpu.SemaphoreType.DMA],
        compiler_params=pltpu.CompilerParams(vmem_limit_bytes=8 << 20),
        name="lend",
    )(grads)


def weight_product_kernel(arrived_ref, lent_ref, inputs_ref, out_ref, grads_ref, held_ref, sem):
    groups, _, rows, width = grads_ref.shape
    columns = width // 2
    main = columns // HEAD * HEAD
    rest = columns - main
    half = rows // 2

    @pl.when(pl.program_id(0) == 0)
    def _():
        load = pltpu.make_async_copy(arrived_ref, grads_ref, sem)
        load.start()
        load.wait()
        core = lax.axis_index("c")
        for index, group, far, place in blocks_of(groups, half):
            own = pl.ds(pl.multiple_of((index * 2 + core) * half, half), half)
            other = pl.ds(pl.multiple_of((index * 2 + 1 - core) * half, half), half)
            held_ref[own, :main] = grads_ref[group, far, place, :main]
            held_ref[own, main:] = grads_ref[group, far, place, 2 * main : 2 * main + rest]
            held_ref[other] = lent_ref[index * half : (index + 1) * half, :columns]

    dims = (((0,), (0,)), ((), ()))
    out_ref[...] = lax.dot_general(held_ref[...], inputs_ref[...], dims, preferred_element_type=jnp.float32)


def weight_product(grads, lent, inputs):
    groups, _, rows, width = grads.shape
    columns, (tokens, model) = width // 2, inputs.shape
    by_column = lambda step: (0, step)
    return pl.pallas_call(
        weight_product_kernel,
        grid=(model // STEP,),
        out_shape=jax.ShapeDtypeStruct((columns, model), jnp.float32),
        in_specs=[
            pl.BlockSpec(memory_space=pl.ANY),
            pl.BlockSpec(lent.shape, lambda step: (0, 0)),
            pl.BlockSpec((tokens, STEP), by_column),
        ],
        out_specs=pl.BlockSpec((columns, STEP), by_column),
        scratch_shapes=[
            pltpu.VMEM(grads.shape, grads.dtype),
            pltpu.VMEM((tokens, columns), jnp.bfloat16),
            pltpu.SemaphoreType.DMA,
        ],
        compiler_params=pltpu.CompilerParams(vmem_limit_bytes=12 << 20),
        cost_estimate=pl.CostEstimate(flops=2 * tokens * columns * model, bytes_accessed=6 << 20, transcendentals=0),
        name="weight_product",
    )(grads, lent, inputs)


def exchange(parts, axes):
    return lax.all_to_all(parts, axes, 0, 0, tiled=True)


def swapped(array, axis):
    return lax.ppermute(array, axis, SWAP)


def per_device(inputs, weight, grad_out, positions):
    width = weight.shape[1]
    tokens, model = inputs.shape

    sent = unrotate(grad_out, positions, lax.axis_size("yh"), lax.axis_size("c"))
    sent, weight = lax.optimization_barrier((sent, weight))
    parts = exchange(sent.reshape(-1, tokens, width), ("yh", "c"))
    parts = arrange(parts.reshape(sent.shape), lax.axis_size("x"))
    grads = exchange(parts, "x").reshape(-1, 2, 2 * tokens, 2 * width)

    own_weight = weight.T
    other_weight = swapped(own_weight, "c")
    all_inputs = lax.all_gather(inputs, COL, axis=0, tiled=True)

    far = input_product(grads, own_weight, other_weight)
    later, _ = lax.optimization_barrier((grads, far))
    lent = swapped(lend(later), "c")
    near = input_product(grads, own_weight, other_weight, swapped(far, "yl"))
    parts = exchange(near.reshape(-1, tokens, model), ("z2", "z1", "z4"))
    weight_grad = weight_product(grads, lent, all_inputs).T
    parts, weight_grad = lax.optimization_barrier((parts, weight_grad))
    input_grad = parts.astype(jnp.float32).sum(axis=0).astype(jnp.bfloat16)
    return input_grad, weight_grad


def solution(mesh):
    sizes = {"yh": 4, "x": 4, "yl": 2, "z4": 2, "z2": 2, "z1": 2, "c": 2}
    finer = Mesh(mesh.devices.reshape(tuple(sizes.values())), tuple(sizes))
    in_specs = (P(COL, ROW), P(ROW, COL), P(ROW, COL), P(ROW))
    out_specs = (P(COL, ROW), P(ROW, COL))
    return jax.shard_map(per_device, mesh=finer, in_specs=in_specs, out_specs=out_specs, check_vma=False)
```

time: 122 us -> 104 us (0.85)
  the two profiles are of different devices: /device:TPU:25 before, /device:TPU:64 now
where the time goes in v3:
time: 104 us; the launch traced here: 103 us
  waiting for transfers between devices  44.4 us (43%)
  starting transfers between devices  30.2 us (29%)
  between operations  14.1 us (14%)
  Pallas kernels  10.3 us (10%)
  local copies, waits for them, and re-layouts  3.4 us (3%)
    all_to_all x3, waiting for transfers between devices, exchange(): return lax.all_to_all(parts, axes, 0, 0, tiled=True)  29.9 us
    all_to_all x3, starting transfers between devices, exchange(): return lax.all_to_all(parts, axes, 0, 0, tiled=True)  24 us
    ppermute x3, waiting for transfers between devices, swapped(): return lax.ppermute(array, axis, SWAP)  13.8 us
    ppermute x3, starting transfers between devices, swapped(): return lax.ppermute(array, axis, SWAP)  6.24 us
    pallas_call x1, Pallas kernels, weight_product(): pl.pallas_call(weight_product_kernel, grid=(model // STEP,), out_shape=ja...  3.98 us
    pallas_call x2, Pallas kernels, input_product(): pl.pallas_call(near_product_kernel if near else far_product_kernel, grid=...  3.78 us
    unnamed x8, local copies, waits for them, and re-layouts  3.4 us
  transfers between devices with their start and end apart: 7, of which 5 were waited for; matrix products, arithmetic and copies ran while one was open for 0% of the time, Pallas kernels for 10%

profile of v3, /device:TPU:64, one launch (start us, length us, event | category | flops | bytes accessed | tf_op | source)
XLA Modules:
  0.0 103.1 jit_solution(15570488771800755443)
XLA Ops:
  7.2 0.0 all-gather.2.cloned.1.call-start
  7.2 0.7 all-gather.2.cloned.1.call-update
  7.9 1.8 %unrotate.1 = bf16[4,2,32,576]{3,2,1,0:T(8,128)(2,1)} custom-call(s32[1,64]{1,0:T(1,128)} %bitcast.18, bf16[64,576]{1,0:T(8,128)(2,1)} %grad_ref.1), custom_call_target="tpu_custom_call" | custom-call | tf_op jit(solution)/shard_map/unrotate/pallas_call | solution.py:80
  9.7 7.1 %all-to-all-start = ((bf16[8,32,576]{2,1,0:T(8,128)(2,1)}), bf16[8,32,576]{2,1,0:T(8,128)(2,1)S(1)}, u32[]{:S(2)}, u32[]{:S(2)}) async-start(bf16[8,32,576]{2,1,0:T(8,128)(2,1)} %bitcast.17), calls=%async_computation | async-start | bytes 655360 | tf_op jit(solution)/shard_map/all_to_all | solution.py:265
  16.8 2.4 %collective-permute-start = (bf16[576,1024]{1,0:T(8,128)(2,1)}, bf16[576,1024]{1,0:T(8,128)(2,1)S(1)}, u32[]{:S(2)}, u32[]{:S(2)}) collective-permute-start(bf16[576,1024]{1,0:T(8,128)(2,1)} %bitcast.11), channel_id=1, source_target_pairs={{0,1},{1,0},{2,3},{3,2},{4,5},{5,4},{6,7},{7,6},{8,9},{9,8},{10,11... | collective-permute-start | bytes 3538952 | tf_op jit(solution)/shard_map/ppermute | solution.py:269
  19.2 11.1 %all-to-all-done = bf16[8,32,576]{2,1,0:T(8,128)(2,1)S(1)} async-done(((bf16[8,32,576]{2,1,0:T(8,128)(2,1)}), bf16[8,32,576]{2,1,0:T(8,128)(2,1)S(1)}, u32[]{:S(2)}, u32[]{:S(2)}) %all-to-all-start) | async-done | bytes 294944 | tf_op jit(solution)/shard_map/all_to_all | solution.py:265
  30.3 0.2 arrange.1
  30.6 0.0 copy-start.1
  30.6 1.0 copy-done.1
  31.6 0.0 copy-start
  31.6 4.4 %all-to-all-start.1 = ((bf16[4,2,2,32,1152]{4,3,2,1,0:T(8,128)(2,1)}), bf16[4,2,2,32,1152]{4,3,2,1,0:T(8,128)(2,1)S(1)}, u32[]{:S(2)}, u32[]{:S(2)}) async-start(bf16[4,2,2,32,1152]{4,3,2,1,0:T(8,128)(2,1)} %copy-done.1), calls=%async_computation.1 | async-start | bytes 2359296 | tf_op jit(solution)/shard_map/all_to_all | solution.py:265
  36.0 0.0 collective-permute-done.other_ref
  36.0 15.8 %all-to-all-done.1 = bf16[4,2,2,32,1152]{4,3,2,1,0:T(8,128)(2,1)S(1)} async-done(((bf16[4,2,2,32,1152]{4,3,2,1,0:T(8,128)(2,1)}), bf16[4,2,2,32,1152]{4,3,2,1,0:T(8,128)(2,1)S(1)}, u32[]{:S(2)}, u32[]{:S(2)}) %all-to-all-start.1) | async-done | bytes 1179680 | tf_op jit(solution)/shard_map/all_to_all | solution.py:265
  51.9 0.0 copy-done
  51.9 1.9 %far_product.1 = bf16[256,1024]{1,0:T(8,128)(2,1)S(1)} custom-call(bf16[4,2,64,1152]{3,2,1,0:T(8,128)(2,1)S(1)} %bitcast.7, bf16[576,1024]{1,0:T(8,128)(2,1)S(1)} %bitcast.12, bf16[576,1024]{1,0:T(8,128)(2,1)S(1)} %collective-permute-done.other_ref), custom_call_target="tpu_custom_call" | custom-call | flops 603979776 | bytes 4194304 | tf_op jit(solution)/shard_map/far_product/pallas_call | solution.py:162
  53.7 1.9 %collective-permute-start.1 = (bf16[256,1024]{1,0:T(8,128)(2,1)S(1)}, bf16[256,1024]{1,0:T(8,128)(2,1)S(1)}, u32[]{:S(2)}, u32[]{:S(2)}) collective-permute-start(bf16[256,1024]{1,0:T(8,128)(2,1)S(1)} %far_product.1), channel_id=1, source_target_pairs={{0,16},{16,0},{1,17},{17,1},{2,18},{18,2},{3,19},{19,3},{4,20},{20... | collective-permute-start | bytes 1572872 | tf_op jit(solution)/shard_map/ppermute | solution.py:269
  55.7 11.8 %collective-permute-done.1.added_ref = bf16[256,1024]{1,0:T(8,128)(2,1)S(1)} collective-permute-done((bf16[256,1024]{1,0:T(8,128)(2,1)S(1)}, bf16[256,1024]{1,0:T(8,128)(2,1)S(1)}, u32[]{:S(2)}, u32[]{:S(2)}) %collective-permute-start.1) | collective-permute-done | bytes 524320 | tf_op jit(solution)/shard_map/ppermute | solution.py:269
  67.4 1.9 %near_product.1 = bf16[256,1024]{1,0:T(8,128)(2,1)S(1)} custom-call(bf16[4,2,64,1152]{3,2,1,0:T(8,128)(2,1)S(1)} %bitcast.8, bf16[576,1024]{1,0:T(8,128)(2,1)S(1)} %bitcast.13, bf16[576,1024]{1,0:T(8,128)(2,1)S(1)} %collective-permute-done.other_ref, bf16[256,1024]{1,0:T(8,128)(2,1)S(1)} %collective-permute-done.1.added_ref), custom_call_target="tpu_custom_call" | custom-call | flops 603979776 | bytes 4194304 | tf_op jit(solution)/shard_map/near_product/pallas_call | solution.py:162
  69.4 0.0 copy-start.3
  69.4 0.8 copy-done.3
  70.2 12.4 %all-to-all-start.2 = ((bf16[8,32,1024]{2,1,0:T(8,128)(2,1)}), bf16[8,32,1024]{2,1,0:T(8,128)(2,1)S(1)}, u32[]{:S(2)}, u32[]{:S(2)}) async-start(bf16[8,32,1024]{2,1,0:T(8,128)(2,1)} %bitcast.14), calls=%async_computation.2 | async-start | bytes 1048576 | tf_op jit(solution)/shard_map/all_to_all | solution.py:265
  82.6 0.4 lend.1
  83.0 1.9 %collective-permute-start.2 = (bf16[512,640]{1,0:T(8,128)(2,1)S(1)}, bf16[512,640]{1,0:T(8,128)(2,1)S(1)}, u32[]{:S(2)}, u32[]{:S(2)}) collective-permute-start(bf16[512,640]{1,0:T(8,128)(2,1)S(1)} %lend.1), channel_id=1, source_target_pairs={{0,1},{1,0},{2,3},{3,2},{4,5},{5,4},{6,7},{7,6},{8,9},{9,8},{10,11... | collective-permute-start | bytes 1966088 | tf_op jit(solution)/shard_map/ppermute | solution.py:269
  85.0 2.1 %collective-permute-done.2.lent_ref = bf16[512,640]{1,0:T(8,128)(2,1)S(1)} collective-permute-done((bf16[512,640]{1,0:T(8,128)(2,1)S(1)}, bf16[512,640]{1,0:T(8,128)(2,1)S(1)}, u32[]{:S(2)}, u32[]{:S(2)}) %collective-permute-start.2) | collective-permute-done | bytes 655392 | tf_op jit(solution)/shard_map/ppermute | solution.py:269
  87.0 0.0 all-gather.2.cloned.1.call-done.inputs_ref
  87.0 0.0 copy-start.2
  87.0 1.6 %copy-done.2 = bf16[1024,1024]{1,0:T(8,128)(2,1)S(1)} copy-done((bf16[1024,1024]{1,0:T(8,128)(2,1)S(1)}, bf16[1024,1024]{1,0:T(8,128)(2,1)}, u32[]{:S(2)}) %copy-start.2) | copy-done | bytes 2097176
  88.6 4.0 %weight_product.1 = f32[576,1024]{1,0:T(8,128)} custom-call(bf16[4,2,64,1152]{3,2,1,0:T(8,128)(2,1)S(1)} %bitcast.10, bf16[512,640]{1,0:T(8,128)(2,1)S(1)} %collective-permute-done.2.lent_ref, bf16[1024,1024]{1,0:T(8,128)(2,1)S(1)} %copy-done.2), custom_call_target="tpu_custom_call" | custom-call | flops 1207959552 | bytes 6291456 | tf_op jit(solution)/shard_map/weight_product/pallas_call | solution.py:243
  92.6 2.9 %all-to-all-done.2 = bf16[8,32,1024]{2,1,0:T(8,128)(2,1)S(1)} async-done(((bf16[8,32,1024]{2,1,0:T(8,128)(2,1)}), bf16[8,32,1024]{2,1,0:T(8,128)(2,1)S(1)}, u32[]{:S(2)}, u32[]{:S(2)}) %all-to-all-start.2) | async-done | bytes 524320 | tf_op jit(solution)/shard_map/all_to_all | solution.py:265
  95.5 0.7 reduce_sum.12
Async XLA Ops:
  7.2 79.9 %all-gather.2.cloned.1.call-start = ((), (), s32[]{:S(2)}) async-start(), calls=%async_computation.3 | async-start | bytes 2162688 | tf_op jit(solution)/shard_map/all_gather | solution.py:284
  9.7 20.6 %all-to-all-start = ((bf16[8,32,576]{2,1,0:T(8,128)(2,1)}), bf16[8,32,576]{2,1,0:T(8,128)(2,1)S(1)}, u32[]{:S(2)}, u32[]{:S(2)}) async-start(bf16[8,32,576]{2,1,0:T(8,128)(2,1)} %bitcast.17), calls=%async_computation | async-start | bytes 655360 | tf_op jit(solution)/shard_map/all_to_all | solution.py:265
  16.8 19.2 %collective-permute-start = (bf16[576,1024]{1,0:T(8,128)(2,1)}, bf16[576,1024]{1,0:T(8,128)(2,1)S(1)}, u32[]{:S(2)}, u32[]{:S(2)}) collective-permute-start(bf16[576,1024]{1,0:T(8,128)(2,1)} %bitcast.11), channel_id=1, source_target_pairs={{0,1},{1,0},{2,3},{3,2},{4,5},{5,4},{6,7},{7,6},{8,9},{9,8},{10,11... | collective-permute-start | bytes 3538952 | tf_op jit(solution)/shard_map/ppermute | solution.py:269
  30.6 1.0 copy-start.1
  31.6 20.3 %copy-start = (bf16[1024,576]{0,1:T(8,128)(2,1)S(1)}, bf16[1024,576]{0,1:T(8,128)(2,1)}, u32[]{:S(2)}) copy-start(bf16[1024,576]{0,1:T(8,128)(2,1)} %param.5) | copy-start | bytes 3538948
  31.6 20.3 %all-to-all-start.1 = ((bf16[4,2,2,32,1152]{4,3,2,1,0:T(8,128)(2,1)}), bf16[4,2,2,32,1152]{4,3,2,1,0:T(8,128)(2,1)S(1)}, u32[]{:S(2)}, u32[]{:S(2)}) async-start(bf16[4,2,2,32,1152]{4,3,2,1,0:T(8,128)(2,1)} %copy-done.1), calls=%async_computation.1 | async-start | bytes 2359296 | tf_op jit(solution)/shard_map/all_to_all | solution.py:265
  53.7 13.7 %collective-permute-start.1 = (bf16[256,1024]{1,0:T(8,128)(2,1)S(1)}, bf16[256,1024]{1,0:T(8,128)(2,1)S(1)}, u32[]{:S(2)}, u32[]{:S(2)}) collective-permute-start(bf16[256,1024]{1,0:T(8,128)(2,1)S(1)} %far_product.1), channel_id=1, source_target_pairs={{0,16},{16,0},{1,17},{17,1},{2,18},{18,2},{3,19},{19,3},{4,20},{20... | collective-permute-start | bytes 1572872 | tf_op jit(solution)/shard_map/ppermute | solution.py:269
  69.4 0.8 copy-start.3
  70.2 25.4 %all-to-all-start.2 = ((bf16[8,32,1024]{2,1,0:T(8,128)(2,1)}), bf16[8,32,1024]{2,1,0:T(8,128)(2,1)S(1)}, u32[]{:S(2)}, u32[]{:S(2)}) async-start(bf16[8,32,1024]{2,1,0:T(8,128)(2,1)} %bitcast.14), calls=%async_computation.2 | async-start | bytes 1048576 | tf_op jit(solution)/shard_map/all_to_all | solution.py:265
  83.0 4.0 %collective-permute-start.2 = (bf16[512,640]{1,0:T(8,128)(2,1)S(1)}, bf16[512,640]{1,0:T(8,128)(2,1)S(1)}, u32[]{:S(2)}, u32[]{:S(2)}) collective-permute-start(bf16[512,640]{1,0:T(8,128)(2,1)S(1)} %lend.1), channel_id=1, source_target_pairs={{0,1},{1,0},{2,3},{3,2},{4,5},{5,4},{6,7},{7,6},{8,9},{9,8},{10,11... | collective-permute-start | bytes 1966088 | tf_op jit(solution)/shard_map/ppermute | solution.py:269
  87.0 1.6 %copy-start.2 = (bf16[1024,1024]{1,0:T(8,128)(2,1)S(1)}, bf16[1024,1024]{1,0:T(8,128)(2,1)}, u32[]{:S(2)}) copy-start(bf16[1024,1024]{1,0:T(8,128)(2,1)} %all-gather.2.cloned.1.call-done.inputs_ref) | copy-start | bytes 6291460
Sparse Core Ops, SparseCore 0:
  10.1 70.8 all-gather.1

commit v4 on v3

--- a/solution.py
+++ b/solution.py
@@ -1,3 +1,4 @@
+import functools
 import math
 
 import jax
@@ -86,7 +87,7 @@
     )(positions.reshape(1, rows), grad)
 
 
-def arrange_kernel(arrived_ref, out_ref, parts_ref, sem):
+def arrange_kernel(arrived_ref, out_ref, parts_ref, laid_ref, sem, out_sems):
     load = pltpu.make_async_copy(arrived_ref, parts_ref, sem)
     load.start()
     load.wait()
@@ -99,11 +100,15 @@
             yh = (yl ^ far) * 2 + z4
             own = parts_ref[yh, core]
             other = parts_ref[yh, 1 - core]
-            for copy in range(out_ref.shape[0]):
-                out_ref[copy, far, z4, :, :main] = own[:, :main]
-                out_ref[copy, far, z4, :, main : 2 * main] = other[:, :main]
-                out_ref[copy, far, z4, :, 2 * main : 2 * main + rest] = own[:, main:]
-                out_ref[copy, far, z4, :, 2 * main + rest :] = other[:, main:]
+            laid_ref[far, z4, :, :main] = own[:, :main]
+            laid_ref[far, z4, :, main : 2 * main] = other[:, :main]
+            laid_ref[far, z4, :, 2 * main : 2 * main + rest] = own[:, main:]
+            laid_ref[far, z4, :, 2 * main + rest :] = other[:, main:]
+    copies = [pltpu.make_async_copy(laid_ref, out_ref.at[i], out_sems.at[i]) for i in range(out_ref.shape[0])]
+    for copy in copies:
+        copy.start()
+    for copy in copies:
+        copy.wait()
 
 
 def arrange(parts, copies):
@@ -112,8 +117,13 @@
         arrange_kernel,
         out_shape=jax.ShapeDtypeStruct((copies, 2, 2, tokens, 2 * width), jnp.bfloat16),
         in_specs=[pl.BlockSpec(memory_space=pl.ANY)],
-        out_specs=pl.BlockSpec(memory_space=pltpu.VMEM),
-        scratch_shapes=[pltpu.VMEM(parts.shape, parts.dtype), pltpu.SemaphoreType.DMA],
+        out_specs=pl.BlockSpec(memory_space=pltpu.HBM),
+        scratch_shapes=[
+            pltpu.VMEM(parts.shape, parts.dtype),
+            pltpu.VMEM((2, 2, tokens, 2 * width), parts.dtype),
+            pltpu.SemaphoreType.DMA,
+            pltpu.SemaphoreType.DMA((copies,)),
+        ],
         compiler_params=pltpu.CompilerParams(vmem_limit_bytes=8 << 20),
         name="arrange",
     )(parts)
@@ -143,13 +153,25 @@
     out_ref[...] = total_of(grads_ref, own_ref, other_ref).astype(out_ref.dtype)
 
 
-def near_product_kernel(arrived_ref, own_ref, other_ref, added_ref, out_ref, grads_ref, sem):
-    @pl.when(pl.program_id(0) == 0)
+def near_product_kernel(arrived_ref, own_ref, other_ref, added_ref, out_ref, grads_ref, sem, held_ref, out_sems):
+    step = pl.program_id(0)
+
+    @pl.when(step == 0)
     def _():
         load_part(arrived_ref, 0, grads_ref, sem)
 
     total = total_of(grads_ref, own_ref, other_ref) + added_ref[...].astype(jnp.float32)
-    out_ref[...] = total.astype(out_ref.dtype)
+    held_ref[step] = total.astype(held_ref.dtype)
+
+    def store(at):
+        return pltpu.make_async_copy(held_ref.at[at], out_ref.at[:, pl.ds(at * STEP, STEP)], out_sems.at[at])
+
+    store(step).start()
+
+    @pl.when(step == pl.num_programs(0) - 1)
+    def _():
+        for at in range(held_ref.shape[0]):
+            store(at).wait()
 
 
 def input_product(grads, own_weight, other_weight, added=None):
@@ -159,13 +181,15 @@
     weights = [pl.BlockSpec((columns, STEP), by_column)] * 2
     part = [pl.BlockSpec((groups * rows, STEP), by_column)]
     near = added is not None
+    steps = model // STEP
+    store = [pltpu.VMEM((steps, groups * rows, STEP), jnp.bfloat16), pltpu.SemaphoreType.DMA((steps,))]
     return pl.pallas_call(
         near_product_kernel if near else far_product_kernel,
         grid=(model // STEP,),
         out_shape=jax.ShapeDtypeStruct((groups * rows, model), jnp.bfloat16),
         in_specs=[pl.BlockSpec(memory_space=pl.ANY)] + weights + part * near,
-        out_specs=part[0],
-        scratch_shapes=[pltpu.VMEM((groups, rows, width), grads.dtype), pltpu.SemaphoreType.DMA],
+        out_specs=pl.BlockSpec(memory_space=pltpu.HBM) if near else part[0],
+        scratch_shapes=[pltpu.VMEM((groups, rows, width), grads.dtype), pltpu.SemaphoreType.DMA] + store * near,
         compiler_params=pltpu.CompilerParams(vmem_limit_bytes=12 << 20),
         cost_estimate=pl.CostEstimate(flops=2 * groups * rows * width * model, bytes_accessed=4 << 20, transcendentals=0),
         name="near_product" if near else "far_product",
@@ -173,92 +197,80 @@
 
 
 def blocks_of(groups, size):
-    own_yl = lax.axis_index("yl")
-    for yl in range(2):
-        for z4 in range(2):
-            for group in range(groups):
-                index = (yl * 2 + z4) * groups + group
-                yield index, group, yl ^ own_yl, slice(z4 * size, (z4 + 1) * size)
-
-
-def lend_kernel(arrived_ref, out_ref, grads_ref, sem):
-    load = pltpu.make_async_copy(arrived_ref, grads_ref, sem)
-    load.start()
-    load.wait()
+    z1, z2, z4 = lax.axis_index("z1"), lax.axis_index("z2"), lax.axis_index("z4")
+    for index in range(4 * groups):
+        group = ((index >> 2 & 1) ^ z2) * 2 + ((index >> 3) ^ z1)
+        place = pl.ds(pl.multiple_of(((index >> 1 & 1) ^ z4) * size, size), size)
+        yield index * size, group, index & 1, place
+
+
+def weight_product_kernel(side, arrived_ref, first_ref, second_ref, *refs):
+    grads_ref, held_ref, sem = refs[-3:]
     groups, _, rows, width = grads_ref.shape
     columns = width // 2
     main = columns // HEAD * HEAD
     rest = columns - main
     half = rows // 2
-    for index, group, far, place in blocks_of(groups, half):
-        start = index * half
-        lent = grads_ref[group, far, place]
-        out_ref[start : start + half, :main] = lent[:, main : 2 * main]
-        out_ref[start : start + half, main:columns] = lent[:, 2 * main + rest :]
-    out_ref[:, columns:] = jnp.zeros_like(out_ref[:, columns:])
-
-
-def lend(grads):
-    groups, _, rows, width = grads.shape
-    padded = pl.cdiv(width // 2, HEAD) * HEAD
-    return pl.pallas_call(
-        lend_kernel,
-        out_shape=jax.ShapeDtypeStruct((2 * groups * rows, padded), grads.dtype),
-        in_specs=[pl.BlockSpec(memory_space=pl.ANY)],
-        out_specs=pl.BlockSpec(memory_space=pltpu.VMEM),
-        scratch_shapes=[pltpu.VMEM(grads.shape, grads.dtype), pltpu.SemaphoreType.DMA],
-        compiler_params=pltpu.CompilerParams(vmem_limit_bytes=8 << 20),
-        name="lend",
-    )(grads)
-
-
-def weight_product_kernel(arrived_ref, lent_ref, inputs_ref, out_ref, grads_ref, held_ref, sem):
-    groups, _, rows, width = grads_ref.shape
-    columns = width // 2
-    main = columns // HEAD * HEAD
-    rest = columns - main
-    half = rows // 2
-
-    @pl.when(pl.program_id(0) == 0)
+    split = first_ref.shape[0]
+    step = pl.program_id(0)
+    early = step < pl.num_programs(0) // 2
+
+    @pl.when(step == 0)
     def _():
         load = pltpu.make_async_copy(arrived_ref, grads_ref, sem)
         load.start()
         load.wait()
-        core = lax.axis_index("c")
-        for index, group, far, place in blocks_of(groups, half):
-            own = pl.ds(pl.multiple_of((index * 2 + core) * half, half), half)
-            other = pl.ds(pl.multiple_of((index * 2 + 1 - core) * half, half), half)
-            held_ref[own, :main] = grads_ref[group, far, place, :main]
-            held_ref[own, main:] = grads_ref[group, far, place, 2 * main : 2 * main + rest]
-            held_ref[other] = lent_ref[index * half : (index + 1) * half, :columns]
+        for start, group, far, place in blocks_of(groups, half):
+            held_ref[start : start + half, :main] = grads_ref[group, far, place, side * main : (side + 1) * main]
+            last = 2 * main + side * rest
+            held_ref[start : start + half, main:] = grads_ref[group, far, place, last : last + rest]
 
     dims = (((0,), (0,)), ((), ()))
-    out_ref[...] = lax.dot_general(held_ref[...], inputs_ref[...], dims, preferred_element_type=jnp.float32)
-
-
-def weight_product(grads, lent, inputs):
-    groups, _, rows, width = grads.shape
-    columns, (tokens, model) = width // 2, inputs.shape
+    total = lax.dot_general(held_ref[:split], first_ref[...], dims, preferred_element_type=jnp.float32)
+    total += lax.dot_general(held_ref[split:], second_ref[...], dims, preferred_element_type=jnp.float32)
+    if side == 0:
+        left_ref, right_ref, out_ref = refs[:3]
+        out_ref[...] = total + jnp.where(early, left_ref[...], right_ref[...]).astype(jnp.float32)
+    else:
+        left_ref, right_ref = refs[:2]
+
+        @pl.when(early)
+        def _():
+            left_ref[...] = total.astype(left_ref.dtype)
+
+        @pl.when(jnp.logical_not(early))
+        def _():
+            right_ref[...] = total.astype(right_ref.dtype)
+
+
+def weight_product(grads, first, second, added=None):
+    width = grads.shape[3]
+    columns, (tokens, model) = width // 2, first.shape
+    steps = model // STEP
     by_column = lambda step: (0, step)
+    whole = pl.BlockSpec((columns, STEP), by_column)
+    left = pl.BlockSpec((columns, STEP), lambda step: (0, jnp.minimum(step, steps // 2 - 1)))
+    right = pl.BlockSpec((columns, STEP), lambda step: (0, jnp.maximum(step - steps // 2, 0)))
+    own = added is not None
     return pl.pallas_call(
-        weight_product_kernel,
-        grid=(model // STEP,),
-        out_shape=jax.ShapeDtypeStruct((columns, model), jnp.float32),
-        in_specs=[
-            pl.BlockSpec(memory_space=pl.ANY),
-            pl.BlockSpec(lent.shape, lambda step: (0, 0)),
-            pl.BlockSpec((tokens, STEP), by_column),
-        ],
-        out_specs=pl.BlockSpec((columns, STEP), by_column),
+        functools.partial(weight_product_kernel, 0 if own else 1),
+        grid=(steps,),
+        out_shape=jax.ShapeDtypeStruct((columns, model), jnp.float32)
+        if own
+        else [jax.ShapeDtypeStruct((columns, model // 2), jnp.bfloat16)] * 2,
+        in_specs=[pl.BlockSpec(memory_space=pl.ANY)]
+        + [pl.BlockSpec((tokens, STEP), by_column)] * 2
+        + [left, right] * own,
+        out_specs=whole if own else [left, right],
         scratch_shapes=[
             pltpu.VMEM(grads.shape, grads.dtype),
-            pltpu.VMEM((tokens, columns), jnp.bfloat16),
+            pltpu.VMEM((2 * tokens, columns), jnp.bfloat16),
             pltpu.SemaphoreType.DMA,
         ],
-        compiler_params=pltpu.CompilerParams(vmem_limit_bytes=12 << 20),
-        cost_estimate=pl.CostEstimate(flops=2 * tokens * columns * model, bytes_accessed=6 << 20, transcendentals=0),
-        name="weight_product",
-    )(grads, lent, inputs)
+        compiler_params=pltpu.CompilerParams(vmem_limit_bytes=16 << 20),
+        cost_estimate=pl.CostEstimate(flops=4 * tokens * columns * model, bytes_accessed=6 << 20, transcendentals=0),
+        name="own_weight_product" if own else "other_weight_product",
+    )(grads, first, second, *(added if own else ()))
 
 
 def exchange(parts, axes):
@@ -267,6 +279,14 @@
 
 def swapped(array, axis):
     return lax.ppermute(array, axis, SWAP)
+
+
+def after(array, earlier):
+    return lax.optimization_barrier((array, earlier))[0]
+
+
+def doubled(array, axis):
+    return jnp.concatenate([array, swapped(array, axis)], 0)
 
 
 def per_device(inputs, weight, grad_out, positions):
@@ -274,21 +294,24 @@
     tokens, model = inputs.shape
 
     sent = unrotate(grad_out, positions, lax.axis_size("yh"), lax.axis_size("c"))
-    sent, weight = lax.optimization_barrier((sent, weight))
-    parts = exchange(sent.reshape(-1, tokens, width), ("yh", "c"))
-    parts = arrange(parts.reshape(sent.shape), lax.axis_size("x"))
+    own_weight = weight.T
+    own_inputs = doubled(after(inputs, sent), "yl")
+    arrived = exchange(sent.reshape(-1, tokens, width), ("yh", "c"))
+    arrived = after(arrived, own_inputs)
+    parts = arrange(arrived.reshape(sent.shape), lax.axis_size("x"))
+    other_weight = swapped(after(own_weight, sent), "c")
+    own_inputs = doubled(after(own_inputs, parts), "z4")
     grads = exchange(parts, "x").reshape(-1, 2, 2 * tokens, 2 * width)
-
-    own_weight = weight.T
-    other_weight = swapped(own_weight, "c")
-    all_inputs = lax.all_gather(inputs, COL, axis=0, tiled=True)
+    own_inputs = doubled(own_inputs, "z2")
 
     far = input_product(grads, own_weight, other_weight)
-    later, _ = lax.optimization_barrier((grads, far))
-    lent = swapped(lend(later), "c")
+    own_inputs = after(own_inputs, far)
+    second = swapped(own_inputs, "z1")
     near = input_product(grads, own_weight, other_weight, swapped(far, "yl"))
     parts = exchange(near.reshape(-1, tokens, model), ("z2", "z1", "z4"))
-    weight_grad = weight_product(grads, lent, all_inputs).T
+    second = after(second, near)
+    lent = [swapped(half, "c") for half in weight_product(grads, own_inputs, second)]
+    weight_grad = weight_product(grads, own_inputs, second, lent).T
     parts, weight_grad = lax.optimization_barrier((parts, weight_grad))
     input_grad = parts.astype(jnp.float32).sum(axis=0).astype(jnp.bfloat16)
     return input_grad, weight_grad

time: 104 us -> 99.6 us (0.958)
  the two profiles are of different devices: /device:TPU:64 before, /device:TPU:33 now
where the time goes in v4:
time: 99.6 us; the launch traced here: 98.8 us
  starting transfers between devices  56.3 us (57%)
  waiting for transfers between devices  20.3 us (20%)
  Pallas kernels  14.6 us (15%)
  other arithmetic  4.15 us (4%)
  local copies, waits for them, and re-layouts  2.68 us (3%)
    ppermute x8, starting transfers between devices, swapped(): return lax.ppermute(array, axis, SWAP)  36.2 us
    ppermute x8, waiting for transfers between devices, swapped(): return lax.ppermute(array, axis, SWAP)  20.3 us
    all_to_all x3, starting transfers between devices, exchange(): return lax.all_to_all(parts, axes, 0, 0, tiled=True)  20.1 us
    pallas_call x2, Pallas kernels, weight_product(): pl.pallas_call(functools.partial(weight_product_kernel, 0 if own else 1),...  8.39 us
    pallas_call x2, Pallas kernels, input_product(): pl.pallas_call(near_product_kernel if near else far_product_kernel, grid=...  3.85 us
    concatenate x2, other arithmetic, doubled(): return jnp.concatenate([array, swapped(array, axis)], 0)  3.44 us
    unnamed x15, local copies, waits for them, and re-layouts  2.67 us
  transfers between devices with their start and end apart: 11, of which 6 were waited for; matrix products, arithmetic and copies ran while one was open for 4% of the time, Pallas kernels for 13%

profile of v4, /device:TPU:33, one launch (start us, length us, event | category | flops | bytes accessed | tf_op | source)
XLA Modules:
  0.0 98.8 jit_solution(8179897442655198868)
XLA Ops:
  0.6 1.8 %unrotate.1 = bf16[4,2,32,576]{3,2,1,0:T(8,128)(2,1)} custom-call(s32[1,64]{1,0:T(1,128)} %bitcast.18, bf16[64,576]{1,0:T(8,128)(2,1)} %grad_ref.1), custom_call_target="tpu_custom_call" | custom-call | tf_op jit(solution)/shard_map/unrotate/pallas_call | solution.py:81
  2.5 9.2 %all-to-all-start = ((bf16[8,32,576]{2,1,0:T(8,128)(2,1)}), bf16[8,32,576]{2,1,0:T(8,128)(2,1)S(1)}, u32[]{:S(2)}, u32[]{:S(2)}) async-start(bf16[8,32,576]{2,1,0:T(8,128)(2,1)} %bitcast.17), calls=%async_computation | async-start | bytes 655360 | tf_op jit(solution)/shard_map/all_to_all | solution.py:277
  11.6 2.3 %collective-permute-start.1 = (bf16[576,1024]{1,0:T(8,128)(2,1)}, bf16[576,1024]{1,0:T(8,128)(2,1)S(1)}, u32[]{:S(2)}, u32[]{:S(2)}) collective-permute-start(bf16[576,1024]{1,0:T(8,128)(2,1)} %bitcast.11), channel_id=1, source_target_pairs={{0,1},{1,0},{2,3},{3,2},{4,5},{5,4},{6,7},{7,6},{8,9},{9,8},{10,11... | collective-permute-start | bytes 3538952 | tf_op jit(solution)/shard_map/ppermute | solution.py:281
  13.9 1.9 %collective-permute-start = (bf16[32,1024]{1,0:T(8,128)(2,1)}, bf16[32,1024]{1,0:T(8,128)(2,1)S(1)}, u32[]{:S(2)}, u32[]{:S(2)}) collective-permute-start(bf16[32,1024]{1,0:T(8,128)(2,1)} %param.4), channel_id=1, source_target_pairs={{0,16},{16,0},{1,17},{17,1},{2,18},{18,2},{3,19},{19,3},{4,20},{20... | collective-permute-start | bytes 196616 | tf_op jit(solution)/shard_map/ppermute | solution.py:281
  15.8 0.9 constant_dynamic-update-slice_fusion.1
  16.7 3.2 %collective-permute-done = bf16[32,1024]{1,0:T(8,128)(2,1)S(1)} collective-permute-done((bf16[32,1024]{1,0:T(8,128)(2,1)}, bf16[32,1024]{1,0:T(8,128)(2,1)S(1)}, u32[]{:S(2)}, u32[]{:S(2)}) %collective-permute-start) | collective-permute-done | bytes 65568 | tf_op jit(solution)/shard_map/ppermute | solution.py:281
  19.8 0.0 copy-start.3
  19.8 0.0 all-to-all-done
  19.9 0.5 arrange.1
  20.4 0.0 copy-start.1
  20.4 1.0 %copy-done.1 = bf16[4,2,2,32,1152]{4,3,2,1,0:T(8,128)(2,1)} copy-done((bf16[4,2,2,32,1152]{4,3,2,1,0:T(8,128)(2,1)}, bf16[4,2,2,32,1152]{4,3,2,1,0:T(8,128)(2,1)S(1)}, u32[]{:S(2)}) %copy-start.1) | copy-done | bytes 1179672
  21.4 0.0 copy-start
  21.4 0.0 copy-done.3
  21.4 4.4 %all-to-all-start.1 = ((bf16[4,2,2,32,1152]{4,3,2,1,0:T(8,128)(2,1)}), bf16[4,2,2,32,1152]{4,3,2,1,0:T(8,128)(2,1)S(1)}, u32[]{:S(2)}, u32[]{:S(2)}) async-start(bf16[4,2,2,32,1152]{4,3,2,1,0:T(8,128)(2,1)} %copy-done.1), calls=%async_computation.1 | async-start | bytes 2359296 | tf_op jit(solution)/shard_map/all_to_all | solution.py:277
  25.8 10.6 %collective-permute-start.3 = (bf16[64,1024]{1,0:T(8,128)(2,1)}, bf16[64,1024]{1,0:T(8,128)(2,1)S(1)}, u32[]{:S(2)}, u32[]{:S(2)}) collective-permute-start(bf16[64,1024]{1,0:T(8,128)(2,1)} %copy-done.3), channel_id=1, source_target_pairs={{0,8},{8,0},{1,9},{9,1},{2,10},{10,2},{3,11},{11,3},{4,12},{12,4},... | collective-permute-start | bytes 393224 | tf_op jit(solution)/shard_map/ppermute | solution.py:281
  36.4 3.4 %collective-permute-done.3 = bf16[64,1024]{1,0:T(8,128)(2,1)S(1)} collective-permute-done((bf16[64,1024]{1,0:T(8,128)(2,1)}, bf16[64,1024]{1,0:T(8,128)(2,1)S(1)}, u32[]{:S(2)}, u32[]{:S(2)}) %collective-permute-start.3) | collective-permute-done | bytes 131104 | tf_op jit(solution)/shard_map/ppermute | solution.py:281
  39.9 0.0 copy-start.5
  39.9 1.7 %pad_maximum_fusion.1 = bf16[128,1024]{1,0:T(8,128)(2,1)} fusion(bf16[64,1024]{1,0:T(8,128)(2,1)S(1)} %collective-permute-done.3, bf16[64,1024]{1,0:T(8,128)(2,1)} %copy-done.3), kind=kLoop, calls=%fused_computation.1 | loop fusion | flops 524288 | bytes 524288 | tf_op jit(solution)/shard_map/concatenate | solution.py:289
  41.5 7.5 %collective-permute-start.4 = (bf16[128,1024]{1,0:T(8,128)(2,1)}, bf16[128,1024]{1,0:T(8,128)(2,1)}, u32[]{:S(2)}, u32[]{:S(2)}) collective-permute-start(bf16[128,1024]{1,0:T(8,128)(2,1)} %pad_maximum_fusion.1), channel_id=1, source_target_pairs={{0,4},{4,0},{1,5},{5,1},{2,6},{6,2},{3,7},{7,3},{8,12},{12,8},{9,1... | collective-permute-start | bytes 786440 | tf_op jit(solution)/shard_map/ppermute | solution.py:281
  49.1 0.0 copy-done.5
  49.1 0.0 collective-permute-done.1.other_ref
  49.1 0.0 all-to-all-done.1
  49.1 0.0 copy-done
  49.1 0.0 copy-start.4
  49.1 0.0 copy-start.6
  49.1 1.9 %far_product.1 = bf16[256,1024]{1,0:T(8,128)(2,1)S(1)} custom-call(bf16[4,2,64,1152]{3,2,1,0:T(8,128)(2,1)S(1)} %bitcast.7, bf16[576,1024]{1,0:T(8,128)(2,1)S(1)} %bitcast.12, bf16[576,1024]{1,0:T(8,128)(2,1)S(1)} %collective-permute-done.1.other_ref), custom_call_target="tpu_custom_call" | custom-call | flops 603979776 | bytes 4194304 | tf_op jit(solution)/shard_map/far_product/pallas_call | solution.py:186
  51.0 2.1 %collective-permute-start.2 = (bf16[256,1024]{1,0:T(8,128)(2,1)S(1)}, bf16[256,1024]{1,0:T(8,128)(2,1)S(1)}, u32[]{:S(2)}, u32[]{:S(2)}) collective-permute-start(bf16[256,1024]{1,0:T(8,128)(2,1)S(1)} %far_product.1), channel_id=1, source_target_pairs={{0,16},{16,0},{1,17},{17,1},{2,18},{18,2},{3,19},{19,3},{4,20},{20... | collective-permute-start | bytes 1572872 | tf_op jit(solution)/shard_map/ppermute | solution.py:281
  53.2 8.2 %collective-permute-done.4 = bf16[128,1024]{1,0:T(8,128)(2,1)} collective-permute-done((bf16[128,1024]{1,0:T(8,128)(2,1)}, bf16[128,1024]{1,0:T(8,128)(2,1)}, u32[]{:S(2)}, u32[]{:S(2)}) %collective-permute-start.4) | collective-permute-done | bytes 262176 | tf_op jit(solution)/shard_map/ppermute | solution.py:281
  61.4 0.0 copy-done.4
  61.4 0.0 copy-done.6
  61.4 1.8 %pad_maximum_fusion.first_ref = bf16[256,1024]{1,0:T(8,128)(2,1)} fusion(bf16[128,1024]{1,0:T(8,128)(2,1)} %collective-permute-done.4, bf16[64,1024]{1,0:T(8,128)(2,1)S(1)} %copy-done.6, bf16[64,1024]{1,0:T(8,128)(2,1)S(1)} %copy-done.4), kind=kLoop, calls=%fused_computation | loop fusion | flops 1572864 | bytes 1048576 | tf_op jit(solution)/shard_map/concatenate | solution.py:289
  63.1 1.9 %collective-permute-start.5 = (bf16[256,1024]{1,0:T(8,128)(2,1)}, bf16[256,1024]{1,0:T(8,128)(2,1)}, u32[]{:S(2)}, u32[]{:S(2)}) collective-permute-start(bf16[256,1024]{1,0:T(8,128)(2,1)} %pad_maximum_fusion.first_ref), channel_id=1, source_target_pairs={{0,2},{2,0},{1,3},{3,1},{4,6},{6,4},{5,7},{7,5},{8,10},{10,8},{9,1... | collective-permute-start | bytes 1572872 | tf_op jit(solution)/shard_map/ppermute | solution.py:281
  65.1 0.4 collective-permute-done.2.added_ref
  65.5 2.0 %near_product.1 = bf16[256,1024]{1,0:T(8,128)(2,1)S(1)} custom-call(bf16[4,2,64,1152]{3,2,1,0:T(8,128)(2,1)S(1)} %bitcast.8, bf16[576,1024]{1,0:T(8,128)(2,1)S(1)} %bitcast.13, bf16[576,1024]{1,0:T(8,128)(2,1)S(1)} %collective-permute-done.1.other_ref, bf16[256,1024]{1,0:T(8,128)(2,1)S(1)} %collective-permute-done.2.added_ref), custom_call_target="tpu_custom_call" | custom-call | flops 603979776 | bytes 4194304 | tf_op jit(solution)/shard_map/near_product/pallas_call | solution.py:186
  67.5 0.0 copy-start.2
  67.5 0.8 copy-done.2
  68.3 6.6 %all-to-all-start.2 = ((bf16[8,32,1024]{2,1,0:T(8,128)(2,1)}), bf16[8,32,1024]{2,1,0:T(8,128)(2,1)S(1)}, u32[]{:S(2)}, u32[]{:S(2)}) async-start(bf16[8,32,1024]{2,1,0:T(8,128)(2,1)} %bitcast.14), calls=%async_computation.2 | async-start | bytes 1048576 | tf_op jit(solution)/shard_map/all_to_all | solution.py:277
  74.8 3.1 %collective-permute-done.5.second_ref = bf16[256,1024]{1,0:T(8,128)(2,1)} collective-permute-done((bf16[256,1024]{1,0:T(8,128)(2,1)}, bf16[256,1024]{1,0:T(8,128)(2,1)}, u32[]{:S(2)}, u32[]{:S(2)}) %collective-permute-start.5) | collective-permute-done | bytes 524320 | tf_op jit(solution)/shard_map/ppermute | solution.py:281
  77.9 3.7 %other_weight_product.1 = (bf16[576,512]{1,0:T(8,128)(2,1)S(1)}, bf16[576,512]{1,0:T(8,128)(2,1)S(1)}) custom-call(bf16[4,2,64,1152]{3,2,1,0:T(8,128)(2,1)S(1)} %bitcast.9, bf16[256,1024]{1,0:T(8,128)(2,1)} %pad_maximum_fusion.first_ref, bf16[256,1024]{1,0:T(8,128)(2,1)} %collective-permute-done.5.second_ref), custom_call_target="tpu_custom_call" | custom-call | flops 603979776 | bytes 6291456 | tf_op jit(solution)/shard_map/other_weight_product/pallas_call | solution.py:255
  81.6 7.9 %collective-permute-start.6 = (bf16[576,512]{1,0:T(8,128)(2,1)S(1)}, bf16[576,512]{1,0:T(8,128)(2,1)S(1)}, u32[]{:S(2)}, u32[]{:S(2)}) collective-permute-start(bf16[576,512]{1,0:T(8,128)(2,1)S(1)} %get-tuple-element.18), channel_id=1, source_target_pairs={{0,1},{1,0},{2,3},{3,2},{4,5},{5,4},{6,7},{7,6},{8,9},{9,8},{10,11... | collective-permute-start | bytes 1769480 | tf_op jit(solution)/shard_map/ppermute | solution.py:281
  89.5 1.9 %collective-permute-start.7 = (bf16[576,512]{1,0:T(8,128)(2,1)S(1)}, bf16[576,512]{1,0:T(8,128)(2,1)S(1)}, u32[]{:S(2)}, u32[]{:S(2)}) collective-permute-start(bf16[576,512]{1,0:T(8,128)(2,1)S(1)} %get-tuple-element.19), channel_id=1, source_target_pairs={{0,1},{1,0},{2,3},{3,2},{4,5},{5,4},{6,7},{7,6},{8,9},{9,8},{10,11... | collective-permute-start | bytes 1769480 | tf_op jit(solution)/shard_map/ppermute | solution.py:281
  91.4 0.0 collective-permute-done.6.refs_0_
  91.4 2.0 %collective-permute-done.7.refs_1_ = bf16[576,512]{1,0:T(8,128)(2,1)S(1)} collective-permute-done((bf16[576,512]{1,0:T(8,128)(2,1)S(1)}, bf16[576,512]{1,0:T(8,128)(2,1)S(1)}, u32[]{:S(2)}, u32[]{:S(2)}) %collective-permute-start.7) | collective-permute-done | bytes 589856 | tf_op jit(solution)/shard_map/ppermute | solution.py:281
  93.4 4.7 %own_weight_product.1 = f32[576,1024]{1,0:T(8,128)} custom-call(bf16[4,2,64,1152]{3,2,1,0:T(8,128)(2,1)S(1)} %bitcast.10, bf16[256,1024]{1,0:T(8,128)(2,1)} %pad_maximum_fusion.first_ref, bf16[256,1024]{1,0:T(8,128)(2,1)} %collective-permute-done.5.second_ref, bf16[576,512]{1,0:T(8,128)(2,1)S(1)} %collective-permute-done.6.refs_0_, ...), custom_call_target="tpu_custom_call" | custom-call | flops 603979776 | bytes 6291456 | tf_op jit(solution)/shard_map/own_weight_product/pallas_call | solution.py:255
  98.1 0.0 all-to-all-done.2
  98.1 0.7 reduce_sum.12
  (1 shorter events, 0.0 us)
Async XLA Ops:
  2.5 17.4 %all-to-all-start = ((bf16[8,32,576]{2,1,0:T(8,128)(2,1)}), bf16[8,32,576]{2,1,0:T(8,128)(2,1)S(1)}, u32[]{:S(2)}, u32[]{:S(2)}) async-start(bf16[8,32,576]{2,1,0:T(8,128)(2,1)} %bitcast.17), calls=%async_computation | async-start | bytes 655360 | tf_op jit(solution)/shard_map/all_to_all | solution.py:277
  11.6 37.5 %collective-permute-start.1 = (bf16[576,1024]{1,0:T(8,128)(2,1)}, bf16[576,1024]{1,0:T(8,128)(2,1)S(1)}, u32[]{:S(2)}, u32[]{:S(2)}) collective-permute-start(bf16[576,1024]{1,0:T(8,128)(2,1)} %bitcast.11), channel_id=1, source_target_pairs={{0,1},{1,0},{2,3},{3,2},{4,5},{5,4},{6,7},{7,6},{8,9},{9,8},{10,11... | collective-permute-start | bytes 3538952 | tf_op jit(solution)/shard_map/ppermute | solution.py:281
  13.9 6.0 %collective-permute-start = (bf16[32,1024]{1,0:T(8,128)(2,1)}, bf16[32,1024]{1,0:T(8,128)(2,1)S(1)}, u32[]{:S(2)}, u32[]{:S(2)}) collective-permute-start(bf16[32,1024]{1,0:T(8,128)(2,1)} %param.4), channel_id=1, source_target_pairs={{0,16},{16,0},{1,17},{17,1},{2,18},{18,2},{3,19},{19,3},{4,20},{20... | collective-permute-start | bytes 196616 | tf_op jit(solution)/shard_map/ppermute | solution.py:281
  19.8 1.5 %copy-start.3 = (bf16[64,1024]{1,0:T(8,128)(2,1)}, bf16[64,1024]{1,0:T(8,128)(2,1)S(1)}, u32[]{:S(2)}) copy-start(bf16[64,1024]{1,0:T(8,128)(2,1)S(1)} %constant_dynamic-update-slice_fusion) | copy-start | bytes 393220
  20.4 1.0 %copy-start.1 = (bf16[4,2,2,32,1152]{4,3,2,1,0:T(8,128)(2,1)}, bf16[4,2,2,32,1152]{4,3,2,1,0:T(8,128)(2,1)S(1)}, u32[]{:S(2)}) copy-start(bf16[4,2,2,32,1152]{4,3,2,1,0:T(8,128)(2,1)S(1)} %arrange.1) | copy-start | bytes 3538948
  21.4 27.7 %copy-start = (bf16[1024,576]{0,1:T(8,128)(2,1)S(1)}, bf16[1024,576]{0,1:T(8,128)(2,1)}, u32[]{:S(2)}) copy-start(bf16[1024,576]{0,1:T(8,128)(2,1)} %param.5) | copy-start | bytes 3538948
  21.4 27.7 %all-to-all-start.1 = ((bf16[4,2,2,32,1152]{4,3,2,1,0:T(8,128)(2,1)}), bf16[4,2,2,32,1152]{4,3,2,1,0:T(8,128)(2,1)S(1)}, u32[]{:S(2)}, u32[]{:S(2)}) async-start(bf16[4,2,2,32,1152]{4,3,2,1,0:T(8,128)(2,1)} %copy-done.1), calls=%async_computation.1 | async-start | bytes 2359296 | tf_op jit(solution)/shard_map/all_to_all | solution.py:277
  25.8 14.1 %collective-permute-start.3 = (bf16[64,1024]{1,0:T(8,128)(2,1)}, bf16[64,1024]{1,0:T(8,128)(2,1)S(1)}, u32[]{:S(2)}, u32[]{:S(2)}) collective-permute-start(bf16[64,1024]{1,0:T(8,128)(2,1)} %copy-done.3), channel_id=1, source_target_pairs={{0,8},{8,0},{1,9},{9,1},{2,10},{10,2},{3,11},{11,3},{4,12},{12,4},... | collective-permute-start | bytes 393224 | tf_op jit(solution)/shard_map/ppermute | solution.py:281
  39.9 9.2 %copy-start.5 = (bf16[64,1024]{1,0:T(8,128)(2,1)}, bf16[64,1024]{1,0:T(8,128)(2,1)S(1)}, u32[]{:S(2)}) copy-start(bf16[64,1024]{1,0:T(8,128)(2,1)S(1)} %collective-permute-done.3) | copy-start | bytes 393220
  41.5 19.8 %collective-permute-start.4 = (bf16[128,1024]{1,0:T(8,128)(2,1)}, bf16[128,1024]{1,0:T(8,128)(2,1)}, u32[]{:S(2)}, u32[]{:S(2)}) collective-permute-start(bf16[128,1024]{1,0:T(8,128)(2,1)} %pad_maximum_fusion.1), channel_id=1, source_target_pairs={{0,4},{4,0},{1,5},{5,1},{2,6},{6,2},{3,7},{7,3},{8,12},{12,8},{9,1... | collective-permute-start | bytes 786440 | tf_op jit(solution)/shard_map/ppermute | solution.py:281
  49.1 12.3 %copy-start.4 = (bf16[64,1024]{1,0:T(8,128)(2,1)S(1)}, bf16[64,1024]{1,0:T(8,128)(2,1)}, u32[]{:S(2)}) copy-start(bf16[64,1024]{1,0:T(8,128)(2,1)} %copy-done.3) | copy-start | bytes 393220
  49.1 12.2 %copy-start.6 = (bf16[64,1024]{1,0:T(8,128)(2,1)S(1)}, bf16[64,1024]{1,0:T(8,128)(2,1)}, u32[]{:S(2)}) copy-start(bf16[64,1024]{1,0:T(8,128)(2,1)} %copy-done.5) | copy-start | bytes 393220
  51.0 14.5 %collective-permute-start.2 = (bf16[256,1024]{1,0:T(8,128)(2,1)S(1)}, bf16[256,1024]{1,0:T(8,128)(2,1)S(1)}, u32[]{:S(2)}, u32[]{:S(2)}) collective-permute-start(bf16[256,1024]{1,0:T(8,128)(2,1)S(1)} %far_product.1), channel_id=1, source_target_pairs={{0,16},{16,0},{1,17},{17,1},{2,18},{18,2},{3,19},{19,3},{4,20},{20... | collective-permute-start | bytes 1572872 | tf_op jit(solution)/shard_map/ppermute | solution.py:281
  63.1 14.7 %collective-permute-start.5 = (bf16[256,1024]{1,0:T(8,128)(2,1)}, bf16[256,1024]{1,0:T(8,128)(2,1)}, u32[]{:S(2)}, u32[]{:S(2)}) collective-permute-start(bf16[256,1024]{1,0:T(8,128)(2,1)} %pad_maximum_fusion.first_ref), channel_id=1, source_target_pairs={{0,2},{2,0},{1,3},{3,1},{4,6},{6,4},{5,7},{7,5},{8,10},{10,8},{9,1... | collective-permute-start | bytes 1572872 | tf_op jit(solution)/shard_map/ppermute | solution.py:281
  67.5 0.8 copy-start.2
  68.3 29.8 %all-to-all-start.2 = ((bf16[8,32,1024]{2,1,0:T(8,128)(2,1)}), bf16[8,32,1024]{2,1,0:T(8,128)(2,1)S(1)}, u32[]{:S(2)}, u32[]{:S(2)}) async-start(bf16[8,32,1024]{2,1,0:T(8,128)(2,1)} %bitcast.14), calls=%async_computation.2 | async-start | bytes 1048576 | tf_op jit(solution)/shard_map/all_to_all | solution.py:277
  81.6 9.8 %collective-permute-start.6 = (bf16[576,512]{1,0:T(8,128)(2,1)S(1)}, bf16[576,512]{1,0:T(8,128)(2,1)S(1)}, u32[]{:S(2)}, u32[]{:S(2)}) collective-permute-start(bf16[576,512]{1,0:T(8,128)(2,1)S(1)} %get-tuple-element.18), channel_id=1, source_target_pairs={{0,1},{1,0},{2,3},{3,2},{4,5},{5,4},{6,7},{7,6},{8,9},{9,8},{10,11... | collective-permute-start | bytes 1769480 | tf_op jit(solution)/shard_map/ppermute | solution.py:281
  89.5 3.9 %collective-permute-start.7 = (bf16[576,512]{1,0:T(8,128)(2,1)S(1)}, bf16[576,512]{1,0:T(8,128)(2,1)S(1)}, u32[]{:S(2)}, u32[]{:S(2)}) collective-permute-start(bf16[576,512]{1,0:T(8,128)(2,1)S(1)} %get-tuple-element.19), channel_id=1, source_target_pairs={{0,1},{1,0},{2,3},{3,2},{4,5},{5,4},{6,7},{7,6},{8,9},{9,8},{10,11... | collective-permute-start | bytes 1769480 | tf_op jit(solution)/shard_map/ppermute | solution.py:281

commit v5 on v4

--- a/solution.py
+++ b/solution.py
@@ -17,7 +17,8 @@
 ROW = ("yh", "x")
 COL = ("yl", "z4", "z2", "z1", "c")
 SWAP = ((0, 1), (1, 0))
-STEP = 256
+STEP = 512
+WIDE = 512
 
 
 def scaled_freq(within):
@@ -205,7 +206,7 @@
 
 
 def weight_product_kernel(side, arrived_ref, first_ref, second_ref, *refs):
-    grads_ref, held_ref, sem = refs[-3:]
+    grads_ref, held_ref, turned_ref, sem = refs[-4:]
     groups, _, rows, width = grads_ref.shape
     columns = width // 2
     main = columns // HEAD * HEAD
@@ -223,11 +224,12 @@
         for start, group, far, place in blocks_of(groups, half):
             held_ref[start : start + half, :main] = grads_ref[group, far, place, side * main : (side + 1) * main]
             last = 2 * main + side * rest
-            held_ref[start : start + half, main:] = grads_ref[group, far, place, last : last + rest]
-
-    dims = (((0,), (0,)), ((), ()))
-    total = lax.dot_general(held_ref[:split], first_ref[...], dims, preferred_element_type=jnp.float32)
-    total += lax.dot_general(held_ref[split:], second_ref[...], dims, preferred_element_type=jnp.float32)
+            held_ref[start : start + half, main:columns] = grads_ref[group, far, place, last : last + rest]
+        held_ref[:, columns:] = jnp.zeros_like(held_ref[:, columns:])
+        turned_ref[...] = held_ref[...].T
+
+    total = jnp.dot(turned_ref[:columns, :split], first_ref[...], preferred_element_type=jnp.float32)
+    total += jnp.dot(turned_ref[:columns, split:], second_ref[...], preferred_element_type=jnp.float32)
     if side == 0:
         left_ref, right_ref, out_ref = refs[:3]
         out_ref[...] = total + jnp.where(early, left_ref[...], right_ref[...]).astype(jnp.float32)
@@ -246,11 +248,12 @@
 def weight_product(grads, first, second, added=None):
     width = grads.shape[3]
     columns, (tokens, model) = width // 2, first.shape
-    steps = model // STEP
+    padded = pl.cdiv(columns, HEAD) * HEAD
+    steps = model // WIDE
     by_column = lambda step: (0, step)
-    whole = pl.BlockSpec((columns, STEP), by_column)
-    left = pl.BlockSpec((columns, STEP), lambda step: (0, jnp.minimum(step, steps // 2 - 1)))
-    right = pl.BlockSpec((columns, STEP), lambda step: (0, jnp.maximum(step - steps // 2, 0)))
+    whole = pl.BlockSpec((columns, WIDE), by_column)
+    left = pl.BlockSpec((columns, WIDE), lambda step: (0, jnp.minimum(step, steps // 2 - 1)))
+    right = pl.BlockSpec((columns, WIDE), lambda step: (0, jnp.maximum(step - steps // 2, 0)))
     own = added is not None
     return pl.pallas_call(
         functools.partial(weight_product_kernel, 0 if own else 1),
@@ -259,15 +262,16 @@
         if own
         else [jax.ShapeDtypeStruct((columns, model // 2), jnp.bfloat16)] * 2,
         in_specs=[pl.BlockSpec(memory_space=pl.ANY)]
-        + [pl.BlockSpec((tokens, STEP), by_column)] * 2
+        + [pl.BlockSpec((tokens, WIDE), by_column)] * 2
         + [left, right] * own,
         out_specs=whole if own else [left, right],
         scratch_shapes=[
             pltpu.VMEM(grads.shape, grads.dtype),
-            pltpu.VMEM((2 * tokens, columns), jnp.bfloat16),
+            pltpu.VMEM((2 * tokens, padded), jnp.bfloat16),
+            pltpu.VMEM((padded, 2 * tokens), jnp.bfloat16),
             pltpu.SemaphoreType.DMA,
         ],
-        compiler_params=pltpu.CompilerParams(vmem_limit_bytes=16 << 20),
+        compiler_params=pltpu.CompilerParams(vmem_limit_bytes=24 << 20),
         cost_estimate=pl.CostEstimate(flops=4 * tokens * columns * model, bytes_accessed=6 << 20, transcendentals=0),
         name="own_weight_product" if own else "other_weight_product",
     )(grads, first, second, *(added if own else ()))
@@ -299,8 +303,8 @@
     arrived = exchange(sent.reshape(-1, tokens, width), ("yh", "c"))
     arrived = after(arrived, own_inputs)
     parts = arrange(arrived.reshape(sent.shape), lax.axis_size("x"))
+    own_inputs = doubled(own_inputs, "z4")
     other_weight = swapped(after(own_weight, sent), "c")
-    own_inputs = doubled(after(own_inputs, parts), "z4")
     grads = exchange(parts, "x").reshape(-1, 2, 2 * tokens, 2 * width)
     own_inputs = doubled(own_inputs, "z2")
 

time: 99.6 us -> 99.6 us (level)
  Pallas kernels: 14.6 us -> 11.3 us
  waiting for transfers between devices: 20.3 us -> 22.3 us
  starting transfers between devices: 56.3 us -> 57.6 us
    pallas_call x2, Pallas kernels: 8.39 us -> 6.27 us  [weight_product(): pl.pallas_call(functools.partial(weight_product_kernel, 0 if own else 1),...]
    ppermute x8, waiting for transfers between devices: 20.3 us -> 22.3 us  [swapped(): return lax.ppermute(array, axis, SWAP)]
    ppermute x8, starting transfers between devices: 36.2 us -> 37.6 us  [swapped(): return lax.ppermute(array, axis, SWAP)]
    pallas_call x2, Pallas kernels: 3.85 us -> 2.69 us  [input_product(): pl.pallas_call(near_product_kernel if near else far_product_kernel, grid=...]
    unnamed x15 -> x19, local copies, waits for them, and re-layouts: 2.67 us -> 2.68 us
  transfers between devices with their start and end apart: 11 -> 11, of which waited for: 6 -> 5; matrix products, arithmetic and copies ran while one was open for 4% -> 4% of each run, Pallas kernels for 13% -> 10%
where the time goes in v5:
time: 99.6 us; the launch traced here: 98.8 us
  starting transfers between devices  57.6 us (58%)
  waiting for transfers between devices  22.3 us (22%)
  Pallas kernels  11.3 us (11%)
  other arithmetic  4.13 us (4%)
  local copies, waits for them, and re-layouts  2.68 us (3%)
    ppermute x8, starting transfers between devices, swapped(): return lax.ppermute(array, axis, SWAP)  37.6 us
    ppermute x8, waiting for transfers between devices, swapped(): return lax.ppermute(array, axis, SWAP)  22.3 us
    all_to_all x3, starting transfers between devices, exchange(): return lax.all_to_all(parts, axes, 0, 0, tiled=True)  20 us
    pallas_call x2, Pallas kernels, weight_product(): pl.pallas_call(functools.partial(weight_product_kernel, 0 if own else 1),...  6.27 us
    concatenate x2, other arithmetic, doubled(): return jnp.concatenate([array, swapped(array, axis)], 0)  3.42 us
    pallas_call x2, Pallas kernels, input_product(): pl.pallas_call(near_product_kernel if near else far_product_kernel, grid=...  2.69 us
    unnamed x19, local copies, waits for them, and re-layouts  2.68 us
  transfers between devices with their start and end apart: 11, of which 5 were waited for; matrix products, arithmetic and copies ran while one was open for 4% of the time, Pallas kernels for 10%

profile of v5, /device:TPU:33, one launch (start us, length us, event | category | flops | bytes accessed | tf_op | source)
XLA Modules:
  0.0 98.8 jit_solution(785153038242636643)
XLA Ops:
  0.6 1.8 %unrotate.1 = bf16[4,2,32,576]{3,2,1,0:T(8,128)(2,1)} custom-call(s32[1,64]{1,0:T(1,128)} %bitcast.18, bf16[64,576]{1,0:T(8,128)(2,1)} %grad_ref.1), custom_call_target="tpu_custom_call" | custom-call | tf_op jit(solution)/shard_map/unrotate/pallas_call | solution.py:82
  2.5 9.2 %all-to-all-start = ((bf16[8,32,576]{2,1,0:T(8,128)(2,1)}), bf16[8,32,576]{2,1,0:T(8,128)(2,1)S(1)}, u32[]{:S(2)}, u32[]{:S(2)}) async-start(bf16[8,32,576]{2,1,0:T(8,128)(2,1)} %bitcast.17), calls=%async_computation | async-start | bytes 655360 | tf_op jit(solution)/shard_map/all_to_all | solution.py:281
  11.6 2.3 %collective-permute-start.1 = (bf16[576,1024]{1,0:T(8,128)(2,1)}, bf16[576,1024]{1,0:T(8,128)(2,1)S(1)}, u32[]{:S(2)}, u32[]{:S(2)}) collective-permute-start(bf16[576,1024]{1,0:T(8,128)(2,1)} %bitcast.11), channel_id=1, source_target_pairs={{0,1},{1,0},{2,3},{3,2},{4,5},{5,4},{6,7},{7,6},{8,9},{9,8},{10,11... | collective-permute-start | bytes 3538952 | tf_op jit(solution)/shard_map/ppermute | solution.py:285
  13.9 1.9 %collective-permute-start = (bf16[32,1024]{1,0:T(8,128)(2,1)}, bf16[32,1024]{1,0:T(8,128)(2,1)S(1)}, u32[]{:S(2)}, u32[]{:S(2)}) collective-permute-start(bf16[32,1024]{1,0:T(8,128)(2,1)} %param.4), channel_id=1, source_target_pairs={{0,16},{16,0},{1,17},{17,1},{2,18},{18,2},{3,19},{19,3},{4,20},{20... | collective-permute-start | bytes 196616 | tf_op jit(solution)/shard_map/ppermute | solution.py:285
  15.8 0.9 constant_dynamic-update-slice_fusion.1
  16.7 3.2 %collective-permute-done = bf16[32,1024]{1,0:T(8,128)(2,1)S(1)} collective-permute-done((bf16[32,1024]{1,0:T(8,128)(2,1)}, bf16[32,1024]{1,0:T(8,128)(2,1)S(1)}, u32[]{:S(2)}, u32[]{:S(2)}) %collective-permute-start) | collective-permute-done | bytes 65568 | tf_op jit(solution)/shard_map/ppermute | solution.py:285
  19.8 0.0 copy-start.4
  19.8 0.0 copy-start.8
  19.9 0.0 all-to-all-done
  19.9 0.5 arrange.1
  20.4 0.0 copy-start.1
  20.4 1.0 %copy-done.1 = bf16[4,2,2,32,1152]{4,3,2,1,0:T(8,128)(2,1)} copy-done((bf16[4,2,2,32,1152]{4,3,2,1,0:T(8,128)(2,1)}, bf16[4,2,2,32,1152]{4,3,2,1,0:T(8,128)(2,1)S(1)}, u32[]{:S(2)}) %copy-start.1) | copy-done | bytes 1179672
  21.4 0.0 copy-done.4
  21.4 0.0 copy-done.8
  21.4 4.4 %all-to-all-start.1 = ((bf16[4,2,2,32,1152]{4,3,2,1,0:T(8,128)(2,1)}), bf16[4,2,2,32,1152]{4,3,2,1,0:T(8,128)(2,1)S(1)}, u32[]{:S(2)}, u32[]{:S(2)}) async-start(bf16[4,2,2,32,1152]{4,3,2,1,0:T(8,128)(2,1)} %copy-done.1), calls=%async_computation.1 | async-start | bytes 2359296 | tf_op jit(solution)/shard_map/all_to_all | solution.py:281
  25.8 10.6 %collective-permute-start.3 = (bf16[64,1024]{1,0:T(8,128)(2,1)}, bf16[64,1024]{1,0:T(8,128)(2,1)S(1)}, u32[]{:S(2)}, u32[]{:S(2)}) collective-permute-start(bf16[64,1024]{1,0:T(8,128)(2,1)} %copy-done.8), channel_id=1, source_target_pairs={{0,8},{8,0},{1,9},{9,1},{2,10},{10,2},{3,11},{11,3},{4,12},{12,4},... | collective-permute-start | bytes 393224 | tf_op jit(solution)/shard_map/ppermute | solution.py:285
  36.5 3.4 %collective-permute-done.3 = bf16[64,1024]{1,0:T(8,128)(2,1)S(1)} collective-permute-done((bf16[64,1024]{1,0:T(8,128)(2,1)}, bf16[64,1024]{1,0:T(8,128)(2,1)S(1)}, u32[]{:S(2)}, u32[]{:S(2)}) %collective-permute-start.3) | collective-permute-done | bytes 131104 | tf_op jit(solution)/shard_map/ppermute | solution.py:285
  39.9 1.6 %pad_maximum_fusion.1 = bf16[128,1024]{1,0:T(8,128)(2,1)} fusion(bf16[64,1024]{1,0:T(8,128)(2,1)S(1)} %collective-permute-done.3, bf16[32,1024]{1,0:T(8,128)(2,1)} %copy-done.4, bf16[32,1024]{1,0:T(8,128)(2,1)} %param.4), kind=kLoop, calls=%fused_computation.1 | loop fusion | flops 786432 | bytes 524288 | tf_op jit(solution)/shard_map/concatenate | solution.py:293
  41.5 7.5 %collective-permute-start.4 = (bf16[128,1024]{1,0:T(8,128)(2,1)}, bf16[128,1024]{1,0:T(8,128)(2,1)}, u32[]{:S(2)}, u32[]{:S(2)}) collective-permute-start(bf16[128,1024]{1,0:T(8,128)(2,1)} %pad_maximum_fusion.1), channel_id=1, source_target_pairs={{0,4},{4,0},{1,5},{5,1},{2,6},{6,2},{3,7},{7,3},{8,12},{12,8},{9,1... | collective-permute-start | bytes 786440 | tf_op jit(solution)/shard_map/ppermute | solution.py:285
  49.1 0.0 copy-done.6
  49.1 0.0 collective-permute-done.1.other_ref
  49.1 0.0 all-to-all-done.1
  49.1 0.0 copy-done
  49.1 0.0 copy-start.3
  49.1 0.0 copy-start.5
  49.1 0.0 copy-start.7
  49.1 1.3 %far_product.1 = bf16[256,1024]{1,0:T(8,128)(2,1)S(1)} custom-call(bf16[4,2,64,1152]{3,2,1,0:T(8,128)(2,1)S(1)} %bitcast.7, bf16[576,1024]{1,0:T(8,128)(2,1)S(1)} %bitcast.12, bf16[576,1024]{1,0:T(8,128)(2,1)S(1)} %collective-permute-done.1.other_ref), custom_call_target="tpu_custom_call" | custom-call | flops 603979776 | bytes 4194304 | tf_op jit(solution)/shard_map/far_product/pallas_call | solution.py:187
  50.4 2.1 %collective-permute-start.2 = (bf16[256,1024]{1,0:T(8,128)(2,1)S(1)}, bf16[256,1024]{1,0:T(8,128)(2,1)S(1)}, u32[]{:S(2)}, u32[]{:S(2)}) collective-permute-start(bf16[256,1024]{1,0:T(8,128)(2,1)S(1)} %far_product.1), channel_id=1, source_target_pairs={{0,16},{16,0},{1,17},{17,1},{2,18},{18,2},{3,19},{19,3},{4,20},{20... | collective-permute-start | bytes 1572872 | tf_op jit(solution)/shard_map/ppermute | solution.py:285
  52.6 8.8 %collective-permute-done.4 = bf16[128,1024]{1,0:T(8,128)(2,1)} collective-permute-done((bf16[128,1024]{1,0:T(8,128)(2,1)}, bf16[128,1024]{1,0:T(8,128)(2,1)}, u32[]{:S(2)}, u32[]{:S(2)}) %collective-permute-start.4) | collective-permute-done | bytes 262176 | tf_op jit(solution)/shard_map/ppermute | solution.py:285
  61.3 0.0 copy-done.3
  61.3 0.0 copy-done.5
  61.4 0.0 copy-done.7
  61.4 1.8 %pad_maximum_fusion.first_ref = bf16[256,1024]{1,0:T(8,128)(2,1)} fusion(bf16[128,1024]{1,0:T(8,128)(2,1)} %collective-permute-done.4, bf16[64,1024]{1,0:T(8,128)(2,1)S(1)} %copy-done.7, bf16[32,1024]{1,0:T(8,128)(2,1)S(1)} %copy-done.5, bf16[32,1024]{1,0:T(8,128)(2,1)S(1)} %copy-done.3), kind=kLoop, calls=%fused_computation | loop fusion | flops 2097152 | bytes 1048576 | tf_op jit(solution)/shard_map/concatenate | solution.py:293
  63.1 1.9 %collective-permute-start.5 = (bf16[256,1024]{1,0:T(8,128)(2,1)}, bf16[256,1024]{1,0:T(8,128)(2,1)}, u32[]{:S(2)}, u32[]{:S(2)}) collective-permute-start(bf16[256,1024]{1,0:T(8,128)(2,1)} %pad_maximum_fusion.first_ref), channel_id=1, source_target_pairs={{0,2},{2,0},{1,3},{3,1},{4,6},{6,4},{5,7},{7,5},{8,10},{10,8},{9,1... | collective-permute-start | bytes 1572872 | tf_op jit(solution)/shard_map/ppermute | solution.py:285
  65.1 0.0 collective-permute-done.2.added_ref
  65.1 1.4 %near_product.1 = bf16[256,1024]{1,0:T(8,128)(2,1)S(1)} custom-call(bf16[4,2,64,1152]{3,2,1,0:T(8,128)(2,1)S(1)} %bitcast.8, bf16[576,1024]{1,0:T(8,128)(2,1)S(1)} %bitcast.13, bf16[576,1024]{1,0:T(8,128)(2,1)S(1)} %collective-permute-done.1.other_ref, bf16[256,1024]{1,0:T(8,128)(2,1)S(1)} %collective-permute-done.2.added_ref), custom_call_target="tpu_custom_call" | custom-call | flops 603979776 | bytes 4194304 | tf_op jit(solution)/shard_map/near_product/pallas_call | solution.py:187
  66.5 0.0 copy-start.2
  66.5 0.8 copy-done.2
  67.3 6.4 %all-to-all-start.2 = ((bf16[8,32,1024]{2,1,0:T(8,128)(2,1)}), bf16[8,32,1024]{2,1,0:T(8,128)(2,1)S(1)}, u32[]{:S(2)}, u32[]{:S(2)}) async-start(bf16[8,32,1024]{2,1,0:T(8,128)(2,1)} %bitcast.14), calls=%async_computation.2 | async-start | bytes 1048576 | tf_op jit(solution)/shard_map/all_to_all | solution.py:281
  73.6 5.0 %collective-permute-done.5.second_ref = bf16[256,1024]{1,0:T(8,128)(2,1)} collective-permute-done((bf16[256,1024]{1,0:T(8,128)(2,1)}, bf16[256,1024]{1,0:T(8,128)(2,1)}, u32[]{:S(2)}, u32[]{:S(2)}) %collective-permute-start.5) | collective-permute-done | bytes 524320 | tf_op jit(solution)/shard_map/ppermute | solution.py:285
  78.6 2.7 %other_weight_product.1 = (bf16[576,512]{1,0:T(8,128)(2,1)S(1)}, bf16[576,512]{1,0:T(8,128)(2,1)S(1)}) custom-call(bf16[4,2,64,1152]{3,2,1,0:T(8,128)(2,1)S(1)} %bitcast.9, bf16[256,1024]{1,0:T(8,128)(2,1)} %pad_maximum_fusion.first_ref, bf16[256,1024]{1,0:T(8,128)(2,1)} %collective-permute-done.5.second_ref), custom_call_target="tpu_custom_call" | custom-call | flops 603979776 | bytes 6291456 | tf_op jit(solution)/shard_map/other_weight_product/pallas_call | solution.py:258
  81.3 9.3 %collective-permute-start.6 = (bf16[576,512]{1,0:T(8,128)(2,1)S(1)}, bf16[576,512]{1,0:T(8,128)(2,1)S(1)}, u32[]{:S(2)}, u32[]{:S(2)}) collective-permute-start(bf16[576,512]{1,0:T(8,128)(2,1)S(1)} %get-tuple-element.16), channel_id=1, source_target_pairs={{0,1},{1,0},{2,3},{3,2},{4,5},{5,4},{6,7},{7,6},{8,9},{9,8},{10,11... | collective-permute-start | bytes 1769480 | tf_op jit(solution)/shard_map/ppermute | solution.py:285
  90.6 1.9 %collective-permute-start.7 = (bf16[576,512]{1,0:T(8,128)(2,1)S(1)}, bf16[576,512]{1,0:T(8,128)(2,1)S(1)}, u32[]{:S(2)}, u32[]{:S(2)}) collective-permute-start(bf16[576,512]{1,0:T(8,128)(2,1)S(1)} %get-tuple-element.17), channel_id=1, source_target_pairs={{0,1},{1,0},{2,3},{3,2},{4,5},{5,4},{6,7},{7,6},{8,9},{9,8},{10,11... | collective-permute-start | bytes 1769480 | tf_op jit(solution)/shard_map/ppermute | solution.py:285
  92.6 0.0 collective-permute-done.6.refs_0_
  92.6 2.0 %collective-permute-done.7.refs_1_ = bf16[576,512]{1,0:T(8,128)(2,1)S(1)} collective-permute-done((bf16[576,512]{1,0:T(8,128)(2,1)S(1)}, bf16[576,512]{1,0:T(8,128)(2,1)S(1)}, u32[]{:S(2)}, u32[]{:S(2)}) %collective-permute-start.7) | collective-permute-done | bytes 589856 | tf_op jit(solution)/shard_map/ppermute | solution.py:285
  94.5 3.5 %own_weight_product.1 = f32[576,1024]{1,0:T(8,128)} custom-call(bf16[4,2,64,1152]{3,2,1,0:T(8,128)(2,1)S(1)} %bitcast.10, bf16[256,1024]{1,0:T(8,128)(2,1)} %pad_maximum_fusion.first_ref, bf16[256,1024]{1,0:T(8,128)(2,1)} %collective-permute-done.5.second_ref, bf16[576,512]{1,0:T(8,128)(2,1)S(1)} %collective-permute-done.6.refs_0_, ...), custom_call_target="tpu_custom_call" | custom-call | flops 603979776 | bytes 6291456 | tf_op jit(solution)/shard_map/own_weight_product/pallas_call | solution.py:258
  98.1 0.0 all-to-all-done.2
  98.1 0.7 reduce_sum.12
  (3 shorter events, 0.0 us)
Async XLA Ops:
  2.5 17.4 %all-to-all-start = ((bf16[8,32,576]{2,1,0:T(8,128)(2,1)}), bf16[8,32,576]{2,1,0:T(8,128)(2,1)S(1)}, u32[]{:S(2)}, u32[]{:S(2)}) async-start(bf16[8,32,576]{2,1,0:T(8,128)(2,1)} %bitcast.17), calls=%async_computation | async-start | bytes 655360 | tf_op jit(solution)/shard_map/all_to_all | solution.py:281
  11.6 37.5 %collective-permute-start.1 = (bf16[576,1024]{1,0:T(8,128)(2,1)}, bf16[576,1024]{1,0:T(8,128)(2,1)S(1)}, u32[]{:S(2)}, u32[]{:S(2)}) collective-permute-start(bf16[576,1024]{1,0:T(8,128)(2,1)} %bitcast.11), channel_id=1, source_target_pairs={{0,1},{1,0},{2,3},{3,2},{4,5},{5,4},{6,7},{7,6},{8,9},{9,8},{10,11... | collective-permute-start | bytes 3538952 | tf_op jit(solution)/shard_map/ppermute | solution.py:285
  13.9 6.0 %collective-permute-start = (bf16[32,1024]{1,0:T(8,128)(2,1)}, bf16[32,1024]{1,0:T(8,128)(2,1)S(1)}, u32[]{:S(2)}, u32[]{:S(2)}) collective-permute-start(bf16[32,1024]{1,0:T(8,128)(2,1)} %param.4), channel_id=1, source_target_pairs={{0,16},{16,0},{1,17},{17,1},{2,18},{18,2},{3,19},{19,3},{4,20},{20... | collective-permute-start | bytes 196616 | tf_op jit(solution)/shard_map/ppermute | solution.py:285
  19.8 1.6 %copy-start.4 = (bf16[32,1024]{1,0:T(8,128)(2,1)}, bf16[32,1024]{1,0:T(8,128)(2,1)S(1)}, u32[]{:S(2)}) copy-start(bf16[32,1024]{1,0:T(8,128)(2,1)S(1)} %collective-permute-done) | copy-start | bytes 196612
  19.8 1.6 %copy-start.8 = (bf16[64,1024]{1,0:T(8,128)(2,1)}, bf16[64,1024]{1,0:T(8,128)(2,1)S(1)}, u32[]{:S(2)}) copy-start(bf16[64,1024]{1,0:T(8,128)(2,1)S(1)} %constant_dynamic-update-slice_fusion) | copy-start | bytes 393220
  20.4 1.0 %copy-start.1 = (bf16[4,2,2,32,1152]{4,3,2,1,0:T(8,128)(2,1)}, bf16[4,2,2,32,1152]{4,3,2,1,0:T(8,128)(2,1)S(1)}, u32[]{:S(2)}) copy-start(bf16[4,2,2,32,1152]{4,3,2,1,0:T(8,128)(2,1)S(1)} %arrange.1) | copy-start | bytes 3538948
  21.4 27.7 %copy-start = (bf16[1024,576]{0,1:T(8,128)(2,1)S(1)}, bf16[1024,576]{0,1:T(8,128)(2,1)}, u32[]{:S(2)}) copy-start(bf16[1024,576]{0,1:T(8,128)(2,1)} %param.5) | copy-start | bytes 3538948
  21.4 27.7 %all-to-all-start.1 = ((bf16[4,2,2,32,1152]{4,3,2,1,0:T(8,128)(2,1)}), bf16[4,2,2,32,1152]{4,3,2,1,0:T(8,128)(2,1)S(1)}, u32[]{:S(2)}, u32[]{:S(2)}) async-start(bf16[4,2,2,32,1152]{4,3,2,1,0:T(8,128)(2,1)} %copy-done.1), calls=%async_computation.1 | async-start | bytes 2359296 | tf_op jit(solution)/shard_map/all_to_all | solution.py:281
  25.8 14.1 %collective-permute-start.3 = (bf16[64,1024]{1,0:T(8,128)(2,1)}, bf16[64,1024]{1,0:T(8,128)(2,1)S(1)}, u32[]{:S(2)}, u32[]{:S(2)}) collective-permute-start(bf16[64,1024]{1,0:T(8,128)(2,1)} %copy-done.8), channel_id=1, source_target_pairs={{0,8},{8,0},{1,9},{9,1},{2,10},{10,2},{3,11},{11,3},{4,12},{12,4},... | collective-permute-start | bytes 393224 | tf_op jit(solution)/shard_map/ppermute | solution.py:285
  39.9 9.2 %copy-start.6 = (bf16[64,1024]{1,0:T(8,128)(2,1)}, bf16[64,1024]{1,0:T(8,128)(2,1)S(1)}, u32[]{:S(2)}) copy-start(bf16[64,1024]{1,0:T(8,128)(2,1)S(1)} %collective-permute-done.3) | copy-start | bytes 393220
  41.5 19.8 %collective-permute-start.4 = (bf16[128,1024]{1,0:T(8,128)(2,1)}, bf16[128,1024]{1,0:T(8,128)(2,1)}, u32[]{:S(2)}, u32[]{:S(2)}) collective-permute-start(bf16[128,1024]{1,0:T(8,128)(2,1)} %pad_maximum_fusion.1), channel_id=1, source_target_pairs={{0,4},{4,0},{1,5},{5,1},{2,6},{6,2},{3,7},{7,3},{8,12},{12,8},{9,1... | collective-permute-start | bytes 786440 | tf_op jit(solution)/shard_map/ppermute | solution.py:285
  49.1 12.3 %copy-start.3 = (bf16[32,1024]{1,0:T(8,128)(2,1)S(1)}, bf16[32,1024]{1,0:T(8,128)(2,1)}, u32[]{:S(2)}) copy-start(bf16[32,1024]{1,0:T(8,128)(2,1)} %param.4) | copy-start | bytes 196612
  49.1 12.2 %copy-start.5 = (bf16[32,1024]{1,0:T(8,128)(2,1)S(1)}, bf16[32,1024]{1,0:T(8,128)(2,1)}, u32[]{:S(2)}) copy-start(bf16[32,1024]{1,0:T(8,128)(2,1)} %copy-done.4) | copy-start | bytes 196612
  49.1 12.2 %copy-start.7 = (bf16[64,1024]{1,0:T(8,128)(2,1)S(1)}, bf16[64,1024]{1,0:T(8,128)(2,1)}, u32[]{:S(2)}) copy-start(bf16[64,1024]{1,0:T(8,128)(2,1)} %copy-done.6) | copy-start | bytes 393220
  50.4 14.6 %collective-permute-start.2 = (bf16[256,1024]{1,0:T(8,128)(2,1)S(1)}, bf16[256,1024]{1,0:T(8,128)(2,1)S(1)}, u32[]{:S(2)}, u32[]{:S(2)}) collective-permute-start(bf16[256,1024]{1,0:T(8,128)(2,1)S(1)} %far_product.1), channel_id=1, source_target_pairs={{0,16},{16,0},{1,17},{17,1},{2,18},{18,2},{3,19},{19,3},{4,20},{20... | collective-permute-start | bytes 1572872 | tf_op jit(solution)/shard_map/ppermute | solution.py:285
  63.1 15.5 %collective-permute-start.5 = (bf16[256,1024]{1,0:T(8,128)(2,1)}, bf16[256,1024]{1,0:T(8,128)(2,1)}, u32[]{:S(2)}, u32[]{:S(2)}) collective-permute-start(bf16[256,1024]{1,0:T(8,128)(2,1)} %pad_maximum_fusion.first_ref), channel_id=1, source_target_pairs={{0,2},{2,0},{1,3},{3,1},{4,6},{6,4},{5,7},{7,5},{8,10},{10,8},{9,1... | collective-permute-start | bytes 1572872 | tf_op jit(solution)/shard_map/ppermute | solution.py:285
  66.5 0.8 copy-start.2
  67.3 30.8 %all-to-all-start.2 = ((bf16[8,32,1024]{2,1,0:T(8,128)(2,1)}), bf16[8,32,1024]{2,1,0:T(8,128)(2,1)S(1)}, u32[]{:S(2)}, u32[]{:S(2)}) async-start(bf16[8,32,1024]{2,1,0:T(8,128)(2,1)} %bitcast.14), calls=%async_computation.2 | async-start | bytes 1048576 | tf_op jit(solution)/shard_map/all_to_all | solution.py:281
  81.3 11.2 %collective-permute-start.6 = (bf16[576,512]{1,0:T(8,128)(2,1)S(1)}, bf16[576,512]{1,0:T(8,128)(2,1)S(1)}, u32[]{:S(2)}, u32[]{:S(2)}) collective-permute-start(bf16[576,512]{1,0:T(8,128)(2,1)S(1)} %get-tuple-element.16), channel_id=1, source_target_pairs={{0,1},{1,0},{2,3},{3,2},{4,5},{5,4},{6,7},{7,6},{8,9},{9,8},{10,11... | collective-permute-start | bytes 1769480 | tf_op jit(solution)/shard_map/ppermute | solution.py:285
  90.6 3.9 %collective-permute-start.7 = (bf16[576,512]{1,0:T(8,128)(2,1)S(1)}, bf16[576,512]{1,0:T(8,128)(2,1)S(1)}, u32[]{:S(2)}, u32[]{:S(2)}) collective-permute-start(bf16[576,512]{1,0:T(8,128)(2,1)S(1)} %get-tuple-element.17), channel_id=1, source_target_pairs={{0,1},{1,0},{2,3},{3,2},{4,5},{5,4},{6,7},{7,6},{8,9},{9,8},{10,11... | collective-permute-start | bytes 1769480 | tf_op jit(solution)/shard_map/ppermute | solution.py:285

commit v6 on v5

--- a/solution.py
+++ b/solution.py
@@ -17,7 +17,7 @@
 ROW = ("yh", "x")
 COL = ("yl", "z4", "z2", "z1", "c")
 SWAP = ((0, 1), (1, 0))
-STEP = 512
+STEP = 256
 WIDE = 512
 
 
@@ -303,8 +303,8 @@
     arrived = exchange(sent.reshape(-1, tokens, width), ("yh", "c"))
     arrived = after(arrived, own_inputs)
     parts = arrange(arrived.reshape(sent.shape), lax.axis_size("x"))
-    own_inputs = doubled(own_inputs, "z4")
     other_weight = swapped(after(own_weight, sent), "c")
+    own_inputs = doubled(after(own_inputs, parts), "z4")
     grads = exchange(parts, "x").reshape(-1, 2, 2 * tokens, 2 * width)
     own_inputs = doubled(own_inputs, "z2")
 

time: 99.6 us -> 97.4 us (0.978)
  waiting for transfers between devices: 22.3 us -> 20.3 us
  starting transfers between devices: 57.6 us -> 56.3 us
  Pallas kernels: 11.3 us -> 12.4 us
    ppermute x8, waiting for transfers between devices: 22.3 us -> 20.3 us  [swapped(): return lax.ppermute(array, axis, SWAP)]
    ppermute x8, starting transfers between devices: 37.6 us -> 36.2 us  [swapped(): return lax.ppermute(array, axis, SWAP)]
    pallas_call x2, Pallas kernels: 2.69 us -> 3.85 us  [input_product(): pl.pallas_call(near_product_kernel if near else far_product_kernel, grid=...]
    unnamed x19 -> x15, local copies, waits for them, and re-layouts: 2.68 us -> 2.67 us
  transfers between devices with their start and end apart: 11 -> 11, of which waited for: 5 -> 6; matrix products, arithmetic and copies ran while one was open for 4% -> 4% of each run, Pallas kernels for 10% -> 11%
where the time goes in v6:
time: 97.4 us; the launch traced here: 96.7 us
  starting transfers between devices  56.3 us (58%)
  waiting for transfers between devices  20.3 us (21%)
  Pallas kernels  12.4 us (13%)
  other arithmetic  4.15 us (4%)
  local copies, waits for them, and re-layouts  2.68 us (3%)
    ppermute x8, starting transfers between devices, swapped(): return lax.ppermute(array, axis, SWAP)  36.2 us
    ppermute x8, waiting for transfers between devices, swapped(): return lax.ppermute(array, axis, SWAP)  20.3 us
    all_to_all x3, starting transfers between devices, exchange(): return lax.all_to_all(parts, axes, 0, 0, tiled=True)  20.1 us
    pallas_call x2, Pallas kernels, weight_product(): pl.pallas_call(functools.partial(weight_product_kernel, 0 if own else 1),...  6.27 us
    pallas_call x2, Pallas kernels, input_product(): pl.pallas_call(near_product_kernel if near else far_product_kernel, grid=...  3.85 us
    concatenate x2, other arithmetic, doubled(): return jnp.concatenate([array, swapped(array, axis)], 0)  3.44 us
    unnamed x15, local copies, waits for them, and re-layouts  2.67 us
  transfers between devices with their start and end apart: 11, of which 6 were waited for; matrix products, arithmetic and copies ran while one was open for 4% of the time, Pallas kernels for 11%

profile of v6, /device:TPU:33, one launch (start us, length us, event | category | flops | bytes accessed | tf_op | source)
XLA Modules:
  0.0 96.7 jit_solution(13091306485735956394)
XLA Ops:
  0.6 1.8 %unrotate.1 = bf16[4,2,32,576]{3,2,1,0:T(8,128)(2,1)} custom-call(s32[1,64]{1,0:T(1,128)} %bitcast.18, bf16[64,576]{1,0:T(8,128)(2,1)} %grad_ref.1), custom_call_target="tpu_custom_call" | custom-call | tf_op jit(solution)/shard_map/unrotate/pallas_call | solution.py:82
  2.5 9.2 %all-to-all-start = ((bf16[8,32,576]{2,1,0:T(8,128)(2,1)}), bf16[8,32,576]{2,1,0:T(8,128)(2,1)S(1)}, u32[]{:S(2)}, u32[]{:S(2)}) async-start(bf16[8,32,576]{2,1,0:T(8,128)(2,1)} %bitcast.17), calls=%async_computation | async-start | bytes 655360 | tf_op jit(solution)/shard_map/all_to_all | solution.py:281
  11.6 2.3 %collective-permute-start.1 = (bf16[576,1024]{1,0:T(8,128)(2,1)}, bf16[576,1024]{1,0:T(8,128)(2,1)S(1)}, u32[]{:S(2)}, u32[]{:S(2)}) collective-permute-start(bf16[576,1024]{1,0:T(8,128)(2,1)} %bitcast.11), channel_id=1, source_target_pairs={{0,1},{1,0},{2,3},{3,2},{4,5},{5,4},{6,7},{7,6},{8,9},{9,8},{10,11... | collective-permute-start | bytes 3538952 | tf_op jit(solution)/shard_map/ppermute | solution.py:285
  13.9 1.9 %collective-permute-start = (bf16[32,1024]{1,0:T(8,128)(2,1)}, bf16[32,1024]{1,0:T(8,128)(2,1)S(1)}, u32[]{:S(2)}, u32[]{:S(2)}) collective-permute-start(bf16[32,1024]{1,0:T(8,128)(2,1)} %param.4), channel_id=1, source_target_pairs={{0,16},{16,0},{1,17},{17,1},{2,18},{18,2},{3,19},{19,3},{4,20},{20... | collective-permute-start | bytes 196616 | tf_op jit(solution)/shard_map/ppermute | solution.py:285
  15.8 0.9 constant_dynamic-update-slice_fusion.1
  16.7 3.2 %collective-permute-done = bf16[32,1024]{1,0:T(8,128)(2,1)S(1)} collective-permute-done((bf16[32,1024]{1,0:T(8,128)(2,1)}, bf16[32,1024]{1,0:T(8,128)(2,1)S(1)}, u32[]{:S(2)}, u32[]{:S(2)}) %collective-permute-start) | collective-permute-done | bytes 65568 | tf_op jit(solution)/shard_map/ppermute | solution.py:285
  19.8 0.0 copy-start.3
  19.8 0.0 all-to-all-done
  19.9 0.5 arrange.1
  20.4 0.0 copy-start.1
  20.4 1.0 %copy-done.1 = bf16[4,2,2,32,1152]{4,3,2,1,0:T(8,128)(2,1)} copy-done((bf16[4,2,2,32,1152]{4,3,2,1,0:T(8,128)(2,1)}, bf16[4,2,2,32,1152]{4,3,2,1,0:T(8,128)(2,1)S(1)}, u32[]{:S(2)}) %copy-start.1) | copy-done | bytes 1179672
  21.4 0.0 copy-start
  21.4 0.0 copy-done.3
  21.4 4.4 %all-to-all-start.1 = ((bf16[4,2,2,32,1152]{4,3,2,1,0:T(8,128)(2,1)}), bf16[4,2,2,32,1152]{4,3,2,1,0:T(8,128)(2,1)S(1)}, u32[]{:S(2)}, u32[]{:S(2)}) async-start(bf16[4,2,2,32,1152]{4,3,2,1,0:T(8,128)(2,1)} %copy-done.1), calls=%async_computation.1 | async-start | bytes 2359296 | tf_op jit(solution)/shard_map/all_to_all | solution.py:281
  25.8 10.6 %collective-permute-start.3 = (bf16[64,1024]{1,0:T(8,128)(2,1)}, bf16[64,1024]{1,0:T(8,128)(2,1)S(1)}, u32[]{:S(2)}, u32[]{:S(2)}) collective-permute-start(bf16[64,1024]{1,0:T(8,128)(2,1)} %copy-done.3), channel_id=1, source_target_pairs={{0,8},{8,0},{1,9},{9,1},{2,10},{10,2},{3,11},{11,3},{4,12},{12,4},... | collective-permute-start | bytes 393224 | tf_op jit(solution)/shard_map/ppermute | solution.py:285
  36.4 3.4 %collective-permute-done.3 = bf16[64,1024]{1,0:T(8,128)(2,1)S(1)} collective-permute-done((bf16[64,1024]{1,0:T(8,128)(2,1)}, bf16[64,1024]{1,0:T(8,128)(2,1)S(1)}, u32[]{:S(2)}, u32[]{:S(2)}) %collective-permute-start.3) | collective-permute-done | bytes 131104 | tf_op jit(solution)/shard_map/ppermute | solution.py:285
  39.9 0.0 copy-start.5
  39.9 1.7 %pad_maximum_fusion.1 = bf16[128,1024]{1,0:T(8,128)(2,1)} fusion(bf16[64,1024]{1,0:T(8,128)(2,1)S(1)} %collective-permute-done.3, bf16[64,1024]{1,0:T(8,128)(2,1)} %copy-done.3), kind=kLoop, calls=%fused_computation.1 | loop fusion | flops 524288 | bytes 524288 | tf_op jit(solution)/shard_map/concatenate | solution.py:293
  41.5 7.5 %collective-permute-start.4 = (bf16[128,1024]{1,0:T(8,128)(2,1)}, bf16[128,1024]{1,0:T(8,128)(2,1)}, u32[]{:S(2)}, u32[]{:S(2)}) collective-permute-start(bf16[128,1024]{1,0:T(8,128)(2,1)} %pad_maximum_fusion.1), channel_id=1, source_target_pairs={{0,4},{4,0},{1,5},{5,1},{2,6},{6,2},{3,7},{7,3},{8,12},{12,8},{9,1... | collective-permute-start | bytes 786440 | tf_op jit(solution)/shard_map/ppermute | solution.py:285
  49.1 0.0 copy-done.5
  49.1 0.0 collective-permute-done.1.other_ref
  49.1 0.0 all-to-all-done.1
  49.1 0.0 copy-done
  49.1 0.0 copy-start.4
  49.1 0.0 copy-start.6
  49.1 1.9 %far_product.1 = bf16[256,1024]{1,0:T(8,128)(2,1)S(1)} custom-call(bf16[4,2,64,1152]{3,2,1,0:T(8,128)(2,1)S(1)} %bitcast.7, bf16[576,1024]{1,0:T(8,128)(2,1)S(1)} %bitcast.12, bf16[576,1024]{1,0:T(8,128)(2,1)S(1)} %collective-permute-done.1.other_ref), custom_call_target="tpu_custom_call" | custom-call | flops 603979776 | bytes 4194304 | tf_op jit(solution)/shard_map/far_product/pallas_call | solution.py:187
  51.0 2.1 %collective-permute-start.2 = (bf16[256,1024]{1,0:T(8,128)(2,1)S(1)}, bf16[256,1024]{1,0:T(8,128)(2,1)S(1)}, u32[]{:S(2)}, u32[]{:S(2)}) collective-permute-start(bf16[256,1024]{1,0:T(8,128)(2,1)S(1)} %far_product.1), channel_id=1, source_target_pairs={{0,16},{16,0},{1,17},{17,1},{2,18},{18,2},{3,19},{19,3},{4,20},{20... | collective-permute-start | bytes 1572872 | tf_op jit(solution)/shard_map/ppermute | solution.py:285
  53.2 8.2 %collective-permute-done.4 = bf16[128,1024]{1,0:T(8,128)(2,1)} collective-permute-done((bf16[128,1024]{1,0:T(8,128)(2,1)}, bf16[128,1024]{1,0:T(8,128)(2,1)}, u32[]{:S(2)}, u32[]{:S(2)}) %collective-permute-start.4) | collective-permute-done | bytes 262176 | tf_op jit(solution)/shard_map/ppermute | solution.py:285
  61.4 0.0 copy-done.4
  61.4 0.0 copy-done.6
  61.4 1.8 %pad_maximum_fusion.first_ref = bf16[256,1024]{1,0:T(8,128)(2,1)} fusion(bf16[128,1024]{1,0:T(8,128)(2,1)} %collective-permute-done.4, bf16[64,1024]{1,0:T(8,128)(2,1)S(1)} %copy-done.6, bf16[64,1024]{1,0:T(8,128)(2,1)S(1)} %copy-done.4), kind=kLoop, calls=%fused_computation | loop fusion | flops 1572864 | bytes 1048576 | tf_op jit(solution)/shard_map/concatenate | solution.py:293
  63.1 1.9 %collective-permute-start.5 = (bf16[256,1024]{1,0:T(8,128)(2,1)}, bf16[256,1024]{1,0:T(8,128)(2,1)}, u32[]{:S(2)}, u32[]{:S(2)}) collective-permute-start(bf16[256,1024]{1,0:T(8,128)(2,1)} %pad_maximum_fusion.first_ref), channel_id=1, source_target_pairs={{0,2},{2,0},{1,3},{3,1},{4,6},{6,4},{5,7},{7,5},{8,10},{10,8},{9,1... | collective-permute-start | bytes 1572872 | tf_op jit(solution)/shard_map/ppermute | solution.py:285
  65.1 0.4 collective-permute-done.2.added_ref
  65.5 2.0 %near_product.1 = bf16[256,1024]{1,0:T(8,128)(2,1)S(1)} custom-call(bf16[4,2,64,1152]{3,2,1,0:T(8,128)(2,1)S(1)} %bitcast.8, bf16[576,1024]{1,0:T(8,128)(2,1)S(1)} %bitcast.13, bf16[576,1024]{1,0:T(8,128)(2,1)S(1)} %collective-permute-done.1.other_ref, bf16[256,1024]{1,0:T(8,128)(2,1)S(1)} %collective-permute-done.2.added_ref), custom_call_target="tpu_custom_call" | custom-call | flops 603979776 | bytes 4194304 | tf_op jit(solution)/shard_map/near_product/pallas_call | solution.py:187
  67.5 0.0 copy-start.2
  67.5 0.8 copy-done.2
  68.3 6.6 %all-to-all-start.2 = ((bf16[8,32,1024]{2,1,0:T(8,128)(2,1)}), bf16[8,32,1024]{2,1,0:T(8,128)(2,1)S(1)}, u32[]{:S(2)}, u32[]{:S(2)}) async-start(bf16[8,32,1024]{2,1,0:T(8,128)(2,1)} %bitcast.14), calls=%async_computation.2 | async-start | bytes 1048576 | tf_op jit(solution)/shard_map/all_to_all | solution.py:281
  74.8 3.1 %collective-permute-done.5.second_ref = bf16[256,1024]{1,0:T(8,128)(2,1)} collective-permute-done((bf16[256,1024]{1,0:T(8,128)(2,1)}, bf16[256,1024]{1,0:T(8,128)(2,1)}, u32[]{:S(2)}, u32[]{:S(2)}) %collective-permute-start.5) | collective-permute-done | bytes 524320 | tf_op jit(solution)/shard_map/ppermute | solution.py:285
  77.9 2.7 %other_weight_product.1 = (bf16[576,512]{1,0:T(8,128)(2,1)S(1)}, bf16[576,512]{1,0:T(8,128)(2,1)S(1)}) custom-call(bf16[4,2,64,1152]{3,2,1,0:T(8,128)(2,1)S(1)} %bitcast.9, bf16[256,1024]{1,0:T(8,128)(2,1)} %pad_maximum_fusion.first_ref, bf16[256,1024]{1,0:T(8,128)(2,1)} %collective-permute-done.5.second_ref), custom_call_target="tpu_custom_call" | custom-call | flops 603979776 | bytes 6291456 | tf_op jit(solution)/shard_map/other_weight_product/pallas_call | solution.py:258
  80.6 7.9 %collective-permute-start.6 = (bf16[576,512]{1,0:T(8,128)(2,1)S(1)}, bf16[576,512]{1,0:T(8,128)(2,1)S(1)}, u32[]{:S(2)}, u32[]{:S(2)}) collective-permute-start(bf16[576,512]{1,0:T(8,128)(2,1)S(1)} %get-tuple-element.18), channel_id=1, source_target_pairs={{0,1},{1,0},{2,3},{3,2},{4,5},{5,4},{6,7},{7,6},{8,9},{9,8},{10,11... | collective-permute-start | bytes 1769480 | tf_op jit(solution)/shard_map/ppermute | solution.py:285
  88.5 1.9 %collective-permute-start.7 = (bf16[576,512]{1,0:T(8,128)(2,1)S(1)}, bf16[576,512]{1,0:T(8,128)(2,1)S(1)}, u32[]{:S(2)}, u32[]{:S(2)}) collective-permute-start(bf16[576,512]{1,0:T(8,128)(2,1)S(1)} %get-tuple-element.19), channel_id=1, source_target_pairs={{0,1},{1,0},{2,3},{3,2},{4,5},{5,4},{6,7},{7,6},{8,9},{9,8},{10,11... | collective-permute-start | bytes 1769480 | tf_op jit(solution)/shard_map/ppermute | solution.py:285
  90.4 0.0 collective-permute-done.6.refs_0_
  90.4 2.0 %collective-permute-done.7.refs_1_ = bf16[576,512]{1,0:T(8,128)(2,1)S(1)} collective-permute-done((bf16[576,512]{1,0:T(8,128)(2,1)S(1)}, bf16[576,512]{1,0:T(8,128)(2,1)S(1)}, u32[]{:S(2)}, u32[]{:S(2)}) %collective-permute-start.7) | collective-permute-done | bytes 589856 | tf_op jit(solution)/shard_map/ppermute | solution.py:285
  92.4 3.5 %own_weight_product.1 = f32[576,1024]{1,0:T(8,128)} custom-call(bf16[4,2,64,1152]{3,2,1,0:T(8,128)(2,1)S(1)} %bitcast.10, bf16[256,1024]{1,0:T(8,128)(2,1)} %pad_maximum_fusion.first_ref, bf16[256,1024]{1,0:T(8,128)(2,1)} %collective-permute-done.5.second_ref, bf16[576,512]{1,0:T(8,128)(2,1)S(1)} %collective-permute-done.6.refs_0_, ...), custom_call_target="tpu_custom_call" | custom-call | flops 603979776 | bytes 6291456 | tf_op jit(solution)/shard_map/own_weight_product/pallas_call | solution.py:258
  96.0 0.0 all-to-all-done.2
  96.0 0.7 reduce_sum.12
  (1 shorter events, 0.0 us)
Async XLA Ops:
  2.5 17.4 %all-to-all-start = ((bf16[8,32,576]{2,1,0:T(8,128)(2,1)}), bf16[8,32,576]{2,1,0:T(8,128)(2,1)S(1)}, u32[]{:S(2)}, u32[]{:S(2)}) async-start(bf16[8,32,576]{2,1,0:T(8,128)(2,1)} %bitcast.17), calls=%async_computation | async-start | bytes 655360 | tf_op jit(solution)/shard_map/all_to_all | solution.py:281
  11.6 37.5 %collective-permute-start.1 = (bf16[576,1024]{1,0:T(8,128)(2,1)}, bf16[576,1024]{1,0:T(8,128)(2,1)S(1)}, u32[]{:S(2)}, u32[]{:S(2)}) collective-permute-start(bf16[576,1024]{1,0:T(8,128)(2,1)} %bitcast.11), channel_id=1, source_target_pairs={{0,1},{1,0},{2,3},{3,2},{4,5},{5,4},{6,7},{7,6},{8,9},{9,8},{10,11... | collective-permute-start | bytes 3538952 | tf_op jit(solution)/shard_map/ppermute | solution.py:285
  13.9 6.0 %collective-permute-start = (bf16[32,1024]{1,0:T(8,128)(2,1)}, bf16[32,1024]{1,0:T(8,128)(2,1)S(1)}, u32[]{:S(2)}, u32[]{:S(2)}) collective-permute-start(bf16[32,1024]{1,0:T(8,128)(2,1)} %param.4), channel_id=1, source_target_pairs={{0,16},{16,0},{1,17},{17,1},{2,18},{18,2},{3,19},{19,3},{4,20},{20... | collective-permute-start | bytes 196616 | tf_op jit(solution)/shard_map/ppermute | solution.py:285
  19.8 1.5 %copy-start.3 = (bf16[64,1024]{1,0:T(8,128)(2,1)}, bf16[64,1024]{1,0:T(8,128)(2,1)S(1)}, u32[]{:S(2)}) copy-start(bf16[64,1024]{1,0:T(8,128)(2,1)S(1)} %constant_dynamic-update-slice_fusion) | copy-start | bytes 393220
  20.4 1.0 %copy-start.1 = (bf16[4,2,2,32,1152]{4,3,2,1,0:T(8,128)(2,1)}, bf16[4,2,2,32,1152]{4,3,2,1,0:T(8,128)(2,1)S(1)}, u32[]{:S(2)}) copy-start(bf16[4,2,2,32,1152]{4,3,2,1,0:T(8,128)(2,1)S(1)} %arrange.1) | copy-start | bytes 3538948
  21.4 27.7 %copy-start = (bf16[1024,576]{0,1:T(8,128)(2,1)S(1)}, bf16[1024,576]{0,1:T(8,128)(2,1)}, u32[]{:S(2)}) copy-start(bf16[1024,576]{0,1:T(8,128)(2,1)} %param.5) | copy-start | bytes 3538948
  21.4 27.7 %all-to-all-start.1 = ((bf16[4,2,2,32,1152]{4,3,2,1,0:T(8,128)(2,1)}), bf16[4,2,2,32,1152]{4,3,2,1,0:T(8,128)(2,1)S(1)}, u32[]{:S(2)}, u32[]{:S(2)}) async-start(bf16[4,2,2,32,1152]{4,3,2,1,0:T(8,128)(2,1)} %copy-done.1), calls=%async_computation.1 | async-start | bytes 2359296 | tf_op jit(solution)/shard_map/all_to_all | solution.py:281
  25.8 14.1 %collective-permute-start.3 = (bf16[64,1024]{1,0:T(8,128)(2,1)}, bf16[64,1024]{1,0:T(8,128)(2,1)S(1)}, u32[]{:S(2)}, u32[]{:S(2)}) collective-permute-start(bf16[64,1024]{1,0:T(8,128)(2,1)} %copy-done.3), channel_id=1, source_target_pairs={{0,8},{8,0},{1,9},{9,1},{2,10},{10,2},{3,11},{11,3},{4,12},{12,4},... | collective-permute-start | bytes 393224 | tf_op jit(solution)/shard_map/ppermute | solution.py:285
  39.9 9.2 %copy-start.5 = (bf16[64,1024]{1,0:T(8,128)(2,1)}, bf16[64,1024]{1,0:T(8,128)(2,1)S(1)}, u32[]{:S(2)}) copy-start(bf16[64,1024]{1,0:T(8,128)(2,1)S(1)} %collective-permute-done.3) | copy-start | bytes 393220
  41.5 19.8 %collective-permute-start.4 = (bf16[128,1024]{1,0:T(8,128)(2,1)}, bf16[128,1024]{1,0:T(8,128)(2,1)}, u32[]{:S(2)}, u32[]{:S(2)}) collective-permute-start(bf16[128,1024]{1,0:T(8,128)(2,1)} %pad_maximum_fusion.1), channel_id=1, source_target_pairs={{0,4},{4,0},{1,5},{5,1},{2,6},{6,2},{3,7},{7,3},{8,12},{12,8},{9,1... | collective-permute-start | bytes 786440 | tf_op jit(solution)/shard_map/ppermute | solution.py:285
  49.1 12.3 %copy-start.4 = (bf16[64,1024]{1,0:T(8,128)(2,1)S(1)}, bf16[64,1024]{1,0:T(8,128)(2,1)}, u32[]{:S(2)}) copy-start(bf16[64,1024]{1,0:T(8,128)(2,1)} %copy-done.3) | copy-start | bytes 393220
  49.1 12.2 %copy-start.6 = (bf16[64,1024]{1,0:T(8,128)(2,1)S(1)}, bf16[64,1024]{1,0:T(8,128)(2,1)}, u32[]{:S(2)}) copy-start(bf16[64,1024]{1,0:T(8,128)(2,1)} %copy-done.5) | copy-start | bytes 393220
  51.0 14.5 %collective-permute-start.2 = (bf16[256,1024]{1,0:T(8,128)(2,1)S(1)}, bf16[256,1024]{1,0:T(8,128)(2,1)S(1)}, u32[]{:S(2)}, u32[]{:S(2)}) collective-permute-start(bf16[256,1024]{1,0:T(8,128)(2,1)S(1)} %far_product.1), channel_id=1, source_target_pairs={{0,16},{16,0},{1,17},{17,1},{2,18},{18,2},{3,19},{19,3},{4,20},{20... | collective-permute-start | bytes 1572872 | tf_op jit(solution)/shard_map/ppermute | solution.py:285
  63.1 14.7 %collective-permute-start.5 = (bf16[256,1024]{1,0:T(8,128)(2,1)}, bf16[256,1024]{1,0:T(8,128)(2,1)}, u32[]{:S(2)}, u32[]{:S(2)}) collective-permute-start(bf16[256,1024]{1,0:T(8,128)(2,1)} %pad_maximum_fusion.first_ref), channel_id=1, source_target_pairs={{0,2},{2,0},{1,3},{3,1},{4,6},{6,4},{5,7},{7,5},{8,10},{10,8},{9,1... | collective-permute-start | bytes 1572872 | tf_op jit(solution)/shard_map/ppermute | solution.py:285
  67.5 0.8 copy-start.2
  68.3 27.7 %all-to-all-start.2 = ((bf16[8,32,1024]{2,1,0:T(8,128)(2,1)}), bf16[8,32,1024]{2,1,0:T(8,128)(2,1)S(1)}, u32[]{:S(2)}, u32[]{:S(2)}) async-start(bf16[8,32,1024]{2,1,0:T(8,128)(2,1)} %bitcast.14), calls=%async_computation.2 | async-start | bytes 1048576 | tf_op jit(solution)/shard_map/all_to_all | solution.py:281
  80.6 9.8 %collective-permute-start.6 = (bf16[576,512]{1,0:T(8,128)(2,1)S(1)}, bf16[576,512]{1,0:T(8,128)(2,1)S(1)}, u32[]{:S(2)}, u32[]{:S(2)}) collective-permute-start(bf16[576,512]{1,0:T(8,128)(2,1)S(1)} %get-tuple-element.18), channel_id=1, source_target_pairs={{0,1},{1,0},{2,3},{3,2},{4,5},{5,4},{6,7},{7,6},{8,9},{9,8},{10,11... | collective-permute-start | bytes 1769480 | tf_op jit(solution)/shard_map/ppermute | solution.py:285
  88.5 3.9 %collective-permute-start.7 = (bf16[576,512]{1,0:T(8,128)(2,1)S(1)}, bf16[576,512]{1,0:T(8,128)(2,1)S(1)}, u32[]{:S(2)}, u32[]{:S(2)}) collective-permute-start(bf16[576,512]{1,0:T(8,128)(2,1)S(1)} %get-tuple-element.19), channel_id=1, source_target_pairs={{0,1},{1,0},{2,3},{3,2},{4,5},{5,4},{6,7},{7,6},{8,9},{9,8},{10,11... | collective-permute-start | bytes 1769480 | tf_op jit(solution)/shard_map/ppermute | solution.py:285

commit v7 on v6

--- a/solution.py
+++ b/solution.py
@@ -303,8 +303,8 @@
     arrived = exchange(sent.reshape(-1, tokens, width), ("yh", "c"))
     arrived = after(arrived, own_inputs)
     parts = arrange(arrived.reshape(sent.shape), lax.axis_size("x"))
-    other_weight = swapped(after(own_weight, sent), "c")
-    own_inputs = doubled(after(own_inputs, parts), "z4")
+    own_inputs = doubled(own_inputs, "z4")
+    other_weight = swapped(after(own_weight, parts), "c")
     grads = exchange(parts, "x").reshape(-1, 2, 2 * tokens, 2 * width)
     own_inputs = doubled(own_inputs, "z2")
 

time: 97.4 us -> 104 us (1.068)
  the two profiles are of different devices: /device:TPU:33 before, /device:TPU:1 now
where the time goes in v7:
time: 104 us
  starting transfers between devices  58.1 us (56%)
  waiting for transfers between devices  25.4 us (24%)
  Pallas kernels  12.4 us (12%)
  other arithmetic  4.13 us (4%)
  local copies, waits for them, and re-layouts  2.68 us (3%)
    ppermute x8, starting transfers between devices, swapped(): return lax.ppermute(array, axis, SWAP)  37.7 us
    ppermute x8, waiting for transfers between devices, swapped(): return lax.ppermute(array, axis, SWAP)  22.5 us
    all_to_all x3, starting transfers between devices, exchange(): return lax.all_to_all(parts, axes, 0, 0, tiled=True)  20.4 us
    pallas_call x2, Pallas kernels, weight_product(): pl.pallas_call(functools.partial(weight_product_kernel, 0 if own else 1),...  6.27 us
    pallas_call x2, Pallas kernels, input_product(): pl.pallas_call(near_product_kernel if near else far_product_kernel, grid=...  3.85 us
    concatenate x2, other arithmetic, doubled(): return jnp.concatenate([array, swapped(array, axis)], 0)  3.42 us
    all_to_all x3, waiting for transfers between devices, exchange(): return lax.all_to_all(parts, axes, 0, 0, tiled=True)  2.85 us
    unnamed x19, local copies, waits for them, and re-layouts  2.68 us
  transfers between devices with their start and end apart: 11, of which 7 were waited for; matrix products, arithmetic and copies ran while one was open for 4% of the time, Pallas kernels for 10%

profile of v7, /device:TPU:1, one launch (start us, length us, event | category | flops | bytes accessed | tf_op | source)
XLA Modules:
  0.0 103.6 jit_solution(6670375919444087098)
XLA Ops:
  0.6 1.8 %unrotate.1 = bf16[4,2,32,576]{3,2,1,0:T(8,128)(2,1)} custom-call(s32[1,64]{1,0:T(1,128)} %bitcast.18, bf16[64,576]{1,0:T(8,128)(2,1)} %grad_ref.1), custom_call_target="tpu_custom_call" | custom-call | tf_op jit(solution)/shard_map/unrotate/pallas_call | solution.py:82
  2.5 0.0 copy-start
  2.5 10.3 %all-to-all-start = ((bf16[8,32,576]{2,1,0:T(8,128)(2,1)}), bf16[8,32,576]{2,1,0:T(8,128)(2,1)S(1)}, u32[]{:S(2)}, u32[]{:S(2)}) async-start(bf16[8,32,576]{2,1,0:T(8,128)(2,1)} %bitcast.17), calls=%async_computation | async-start | bytes 655360 | tf_op jit(solution)/shard_map/all_to_all | solution.py:281
  12.8 1.9 %collective-permute-start = (bf16[32,1024]{1,0:T(8,128)(2,1)}, bf16[32,1024]{1,0:T(8,128)(2,1)S(1)}, u32[]{:S(2)}, u32[]{:S(2)}) collective-permute-start(bf16[32,1024]{1,0:T(8,128)(2,1)} %param.4), channel_id=1, source_target_pairs={{0,16},{16,0},{1,17},{17,1},{2,18},{18,2},{3,19},{19,3},{4,20},{20... | collective-permute-start | bytes 196616 | tf_op jit(solution)/shard_map/ppermute | solution.py:285
  14.7 0.9 constant_dynamic-update-slice_fusion.1
  15.6 6.1 %collective-permute-done = bf16[32,1024]{1,0:T(8,128)(2,1)S(1)} collective-permute-done((bf16[32,1024]{1,0:T(8,128)(2,1)}, bf16[32,1024]{1,0:T(8,128)(2,1)S(1)}, u32[]{:S(2)}, u32[]{:S(2)}) %collective-permute-start) | collective-permute-done | bytes 65568 | tf_op jit(solution)/shard_map/ppermute | solution.py:285
  21.7 0.0 copy-start.8
  21.7 2.8 %all-to-all-done = bf16[8,32,576]{2,1,0:T(8,128)(2,1)S(1)} async-done(((bf16[8,32,576]{2,1,0:T(8,128)(2,1)}), bf16[8,32,576]{2,1,0:T(8,128)(2,1)S(1)}, u32[]{:S(2)}, u32[]{:S(2)}) %all-to-all-start) | async-done | bytes 294944 | tf_op jit(solution)/shard_map/all_to_all | solution.py:281
  24.5 0.5 arrange.1
  25.0 0.0 copy-start.1
  25.0 1.0 copy-done.1
  26.0 0.0 copy-done
  26.0 2.9 %collective-permute-start.1 = (bf16[576,1024]{1,0:T(8,128)(2,1)S(1)}, bf16[576,1024]{1,0:T(8,128)(2,1)S(1)}, u32[]{:S(2)}, u32[]{:S(2)}) collective-permute-start(bf16[576,1024]{1,0:T(8,128)(2,1)S(1)} %bitcast.11), channel_id=1, source_target_pairs={{0,1},{1,0},{2,3},{3,2},{4,5},{5,4},{6,7},{7,6},{8,9},{9,8},{10,11... | collective-permute-start | bytes 3538952 | tf_op jit(solution)/shard_map/ppermute | solution.py:285
  29.0 0.0 copy-done.4
  29.0 0.0 copy-done.8
  29.0 3.5 %all-to-all-start.1 = ((bf16[4,2,2,32,1152]{4,3,2,1,0:T(8,128)(2,1)}), bf16[4,2,2,32,1152]{4,3,2,1,0:T(8,128)(2,1)S(1)}, u32[]{:S(2)}, u32[]{:S(2)}) async-start(bf16[4,2,2,32,1152]{4,3,2,1,0:T(8,128)(2,1)} %copy-done.1), calls=%async_computation.1 | async-start | bytes 2359296 | tf_op jit(solution)/shard_map/all_to_all | solution.py:281
  32.5 10.6 %collective-permute-start.3 = (bf16[64,1024]{1,0:T(8,128)(2,1)}, bf16[64,1024]{1,0:T(8,128)(2,1)S(1)}, u32[]{:S(2)}, u32[]{:S(2)}) collective-permute-start(bf16[64,1024]{1,0:T(8,128)(2,1)} %copy-done.8), channel_id=1, source_target_pairs={{0,8},{8,0},{1,9},{9,1},{2,10},{10,2},{3,11},{11,3},{4,12},{12,4},... | collective-permute-start | bytes 393224 | tf_op jit(solution)/shard_map/ppermute | solution.py:285
  43.1 3.9 %collective-permute-done.3 = bf16[64,1024]{1,0:T(8,128)(2,1)S(1)} collective-permute-done((bf16[64,1024]{1,0:T(8,128)(2,1)}, bf16[64,1024]{1,0:T(8,128)(2,1)S(1)}, u32[]{:S(2)}, u32[]{:S(2)}) %collective-permute-start.3) | collective-permute-done | bytes 131104 | tf_op jit(solution)/shard_map/ppermute | solution.py:285
  47.0 1.6 %pad_maximum_fusion.1 = bf16[128,1024]{1,0:T(8,128)(2,1)} fusion(bf16[64,1024]{1,0:T(8,128)(2,1)S(1)} %collective-permute-done.3, bf16[32,1024]{1,0:T(8,128)(2,1)} %copy-done.4, bf16[32,1024]{1,0:T(8,128)(2,1)} %param.4), kind=kLoop, calls=%fused_computation.1 | loop fusion | flops 786432 | bytes 524288 | tf_op jit(solution)/shard_map/concatenate | solution.py:293
  48.6 0.0 copy-done.6
  48.6 7.1 %collective-permute-start.4 = (bf16[128,1024]{1,0:T(8,128)(2,1)}, bf16[128,1024]{1,0:T(8,128)(2,1)}, u32[]{:S(2)}, u32[]{:S(2)}) collective-permute-start(bf16[128,1024]{1,0:T(8,128)(2,1)} %pad_maximum_fusion.1), channel_id=1, source_target_pairs={{0,4},{4,0},{1,5},{5,1},{2,6},{6,2},{3,7},{7,3},{8,12},{12,8},{9,1... | collective-permute-start | bytes 786440 | tf_op jit(solution)/shard_map/ppermute | solution.py:285
  55.8 0.0 all-to-all-done.1
  55.8 0.0 collective-permute-done.1.other_ref
  55.8 0.0 copy-start.3
  55.8 0.0 copy-start.5
  55.8 0.0 copy-start.7
  55.8 1.9 %far_product.1 = bf16[256,1024]{1,0:T(8,128)(2,1)S(1)} custom-call(bf16[4,2,64,1152]{3,2,1,0:T(8,128)(2,1)S(1)} %bitcast.7, bf16[576,1024]{1,0:T(8,128)(2,1)S(1)} %bitcast.12, bf16[576,1024]{1,0:T(8,128)(2,1)S(1)} %collective-permute-done.1.other_ref), custom_call_target="tpu_custom_call" | custom-call | flops 603979776 | bytes 4194304 | tf_op jit(solution)/shard_map/far_product/pallas_call | solution.py:187
  57.7 2.9 %collective-permute-start.2 = (bf16[256,1024]{1,0:T(8,128)(2,1)S(1)}, bf16[256,1024]{1,0:T(8,128)(2,1)S(1)}, u32[]{:S(2)}, u32[]{:S(2)}) collective-permute-start(bf16[256,1024]{1,0:T(8,128)(2,1)S(1)} %far_product.1), channel_id=1, source_target_pairs={{0,16},{16,0},{1,17},{17,1},{2,18},{18,2},{3,19},{19,3},{4,20},{20... | collective-permute-start | bytes 1572872 | tf_op jit(solution)/shard_map/ppermute | solution.py:285
  60.6 7.3 %collective-permute-done.4 = bf16[128,1024]{1,0:T(8,128)(2,1)} collective-permute-done((bf16[128,1024]{1,0:T(8,128)(2,1)}, bf16[128,1024]{1,0:T(8,128)(2,1)}, u32[]{:S(2)}, u32[]{:S(2)}) %collective-permute-start.4) | collective-permute-done | bytes 262176 | tf_op jit(solution)/shard_map/ppermute | solution.py:285
  67.9 0.0 copy-done.3
  67.9 0.0 copy-done.5
  67.9 0.0 copy-done.7
  67.9 1.8 %pad_maximum_fusion.first_ref = bf16[256,1024]{1,0:T(8,128)(2,1)} fusion(bf16[128,1024]{1,0:T(8,128)(2,1)} %collective-permute-done.4, bf16[64,1024]{1,0:T(8,128)(2,1)S(1)} %copy-done.7, bf16[32,1024]{1,0:T(8,128)(2,1)S(1)} %copy-done.5, bf16[32,1024]{1,0:T(8,128)(2,1)S(1)} %copy-done.3), kind=kLoop, calls=%fused_computation | loop fusion | flops 2097152 | bytes 1048576 | tf_op jit(solution)/shard_map/concatenate | solution.py:293
  69.7 1.9 %collective-permute-start.5 = (bf16[256,1024]{1,0:T(8,128)(2,1)}, bf16[256,1024]{1,0:T(8,128)(2,1)}, u32[]{:S(2)}, u32[]{:S(2)}) collective-permute-start(bf16[256,1024]{1,0:T(8,128)(2,1)} %pad_maximum_fusion.first_ref), channel_id=1, source_target_pairs={{0,2},{2,0},{1,3},{3,1},{4,6},{6,4},{5,7},{7,5},{8,10},{10,8},{9,1... | collective-permute-start | bytes 1572872 | tf_op jit(solution)/shard_map/ppermute | solution.py:285
  71.6 0.6 collective-permute-done.2.added_ref
  72.2 2.0 %near_product.1 = bf16[256,1024]{1,0:T(8,128)(2,1)S(1)} custom-call(bf16[4,2,64,1152]{3,2,1,0:T(8,128)(2,1)S(1)} %bitcast.8, bf16[576,1024]{1,0:T(8,128)(2,1)S(1)} %bitcast.13, bf16[576,1024]{1,0:T(8,128)(2,1)S(1)} %collective-permute-done.1.other_ref, bf16[256,1024]{1,0:T(8,128)(2,1)S(1)} %collective-permute-done.2.added_ref), custom_call_target="tpu_custom_call" | custom-call | flops 603979776 | bytes 4194304 | tf_op jit(solution)/shard_map/near_product/pallas_call | solution.py:187
  74.2 0.0 copy-start.2
  74.2 0.8 copy-done.2
  75.0 6.5 %all-to-all-start.2 = ((bf16[8,32,1024]{2,1,0:T(8,128)(2,1)}), bf16[8,32,1024]{2,1,0:T(8,128)(2,1)S(1)}, u32[]{:S(2)}, u32[]{:S(2)}) async-start(bf16[8,32,1024]{2,1,0:T(8,128)(2,1)} %bitcast.14), calls=%async_computation.2 | async-start | bytes 1048576 | tf_op jit(solution)/shard_map/all_to_all | solution.py:281
  81.5 2.7 %collective-permute-done.5.second_ref = bf16[256,1024]{1,0:T(8,128)(2,1)} collective-permute-done((bf16[256,1024]{1,0:T(8,128)(2,1)}, bf16[256,1024]{1,0:T(8,128)(2,1)}, u32[]{:S(2)}, u32[]{:S(2)}) %collective-permute-start.5) | collective-permute-done | bytes 524320 | tf_op jit(solution)/shard_map/ppermute | solution.py:285
  84.2 2.7 %other_weight_product.1 = (bf16[576,512]{1,0:T(8,128)(2,1)S(1)}, bf16[576,512]{1,0:T(8,128)(2,1)S(1)}) custom-call(bf16[4,2,64,1152]{3,2,1,0:T(8,128)(2,1)S(1)} %bitcast.9, bf16[256,1024]{1,0:T(8,128)(2,1)} %pad_maximum_fusion.first_ref, bf16[256,1024]{1,0:T(8,128)(2,1)} %collective-permute-done.5.second_ref), custom_call_target="tpu_custom_call" | custom-call | flops 603979776 | bytes 6291456 | tf_op jit(solution)/shard_map/other_weight_product/pallas_call | solution.py:258
  86.9 8.5 %collective-permute-start.6 = (bf16[576,512]{1,0:T(8,128)(2,1)S(1)}, bf16[576,512]{1,0:T(8,128)(2,1)S(1)}, u32[]{:S(2)}, u32[]{:S(2)}) collective-permute-start(bf16[576,512]{1,0:T(8,128)(2,1)S(1)} %get-tuple-element.16), channel_id=1, source_target_pairs={{0,1},{1,0},{2,3},{3,2},{4,5},{5,4},{6,7},{7,6},{8,9},{9,8},{10,11... | collective-permute-start | bytes 1769480 | tf_op jit(solution)/shard_map/ppermute | solution.py:285
  95.4 1.9 %collective-permute-start.7 = (bf16[576,512]{1,0:T(8,128)(2,1)S(1)}, bf16[576,512]{1,0:T(8,128)(2,1)S(1)}, u32[]{:S(2)}, u32[]{:S(2)}) collective-permute-start(bf16[576,512]{1,0:T(8,128)(2,1)S(1)} %get-tuple-element.17), channel_id=1, source_target_pairs={{0,1},{1,0},{2,3},{3,2},{4,5},{5,4},{6,7},{7,6},{8,9},{9,8},{10,11... | collective-permute-start | bytes 1769480 | tf_op jit(solution)/shard_map/ppermute | solution.py:285
  97.3 0.0 collective-permute-done.6.refs_0_
  97.4 2.0 %collective-permute-done.7.refs_1_ = bf16[576,512]{1,0:T(8,128)(2,1)S(1)} collective-permute-done((bf16[576,512]{1,0:T(8,128)(2,1)S(1)}, bf16[576,512]{1,0:T(8,128)(2,1)S(1)}, u32[]{:S(2)}, u32[]{:S(2)}) %collective-permute-start.7) | collective-permute-done | bytes 589856 | tf_op jit(solution)/shard_map/ppermute | solution.py:285
  99.3 3.5 %own_weight_product.1 = f32[576,1024]{1,0:T(8,128)} custom-call(bf16[4,2,64,1152]{3,2,1,0:T(8,128)(2,1)S(1)} %bitcast.10, bf16[256,1024]{1,0:T(8,128)(2,1)} %pad_maximum_fusion.first_ref, bf16[256,1024]{1,0:T(8,128)(2,1)} %collective-permute-done.5.second_ref, bf16[576,512]{1,0:T(8,128)(2,1)S(1)} %collective-permute-done.6.refs_0_, ...), custom_call_target="tpu_custom_call" | custom-call | flops 603979776 | bytes 6291456 | tf_op jit(solution)/shard_map/own_weight_product/pallas_call | solution.py:258
  102.9 0.0 all-to-all-done.2
  102.9 0.7 reduce_sum.12
  (3 shorter events, 0.0 us)
Async XLA Ops:
  2.5 23.6 %copy-start = (bf16[1024,576]{0,1:T(8,128)(2,1)S(1)}, bf16[1024,576]{0,1:T(8,128)(2,1)}, u32[]{:S(2)}) copy-start(bf16[1024,576]{0,1:T(8,128)(2,1)} %param.5) | copy-start | bytes 3538948
  2.5 22.1 %all-to-all-start = ((bf16[8,32,576]{2,1,0:T(8,128)(2,1)}), bf16[8,32,576]{2,1,0:T(8,128)(2,1)S(1)}, u32[]{:S(2)}, u32[]{:S(2)}) async-start(bf16[8,32,576]{2,1,0:T(8,128)(2,1)} %bitcast.17), calls=%async_computation | async-start | bytes 655360 | tf_op jit(solution)/shard_map/all_to_all | solution.py:281
  12.8 8.8 %collective-permute-start = (bf16[32,1024]{1,0:T(8,128)(2,1)}, bf16[32,1024]{1,0:T(8,128)(2,1)S(1)}, u32[]{:S(2)}, u32[]{:S(2)}) collective-permute-start(bf16[32,1024]{1,0:T(8,128)(2,1)} %param.4), channel_id=1, source_target_pairs={{0,16},{16,0},{1,17},{17,1},{2,18},{18,2},{3,19},{19,3},{4,20},{20... | collective-permute-start | bytes 196616 | tf_op jit(solution)/shard_map/ppermute | solution.py:285
  21.6 7.3 %copy-start.4 = (bf16[32,1024]{1,0:T(8,128)(2,1)}, bf16[32,1024]{1,0:T(8,128)(2,1)S(1)}, u32[]{:S(2)}) copy-start(bf16[32,1024]{1,0:T(8,128)(2,1)S(1)} %collective-permute-done) | copy-start | bytes 196612
  21.7 7.3 %copy-start.8 = (bf16[64,1024]{1,0:T(8,128)(2,1)}, bf16[64,1024]{1,0:T(8,128)(2,1)S(1)}, u32[]{:S(2)}) copy-start(bf16[64,1024]{1,0:T(8,128)(2,1)S(1)} %constant_dynamic-update-slice_fusion) | copy-start | bytes 393220
  25.0 1.0 copy-start.1
  26.0 29.7 %collective-permute-start.1 = (bf16[576,1024]{1,0:T(8,128)(2,1)S(1)}, bf16[576,1024]{1,0:T(8,128)(2,1)S(1)}, u32[]{:S(2)}, u32[]{:S(2)}) collective-permute-start(bf16[576,1024]{1,0:T(8,128)(2,1)S(1)} %bitcast.11), channel_id=1, source_target_pairs={{0,1},{1,0},{2,3},{3,2},{4,5},{5,4},{6,7},{7,6},{8,9},{9,8},{10,11... | collective-permute-start | bytes 3538952 | tf_op jit(solution)/shard_map/ppermute | solution.py:285
  29.0 26.8 %all-to-all-start.1 = ((bf16[4,2,2,32,1152]{4,3,2,1,0:T(8,128)(2,1)}), bf16[4,2,2,32,1152]{4,3,2,1,0:T(8,128)(2,1)S(1)}, u32[]{:S(2)}, u32[]{:S(2)}) async-start(bf16[4,2,2,32,1152]{4,3,2,1,0:T(8,128)(2,1)} %copy-done.1), calls=%async_computation.1 | async-start | bytes 2359296 | tf_op jit(solution)/shard_map/all_to_all | solution.py:281
  32.5 14.4 %collective-permute-start.3 = (bf16[64,1024]{1,0:T(8,128)(2,1)}, bf16[64,1024]{1,0:T(8,128)(2,1)S(1)}, u32[]{:S(2)}, u32[]{:S(2)}) collective-permute-start(bf16[64,1024]{1,0:T(8,128)(2,1)} %copy-done.8), channel_id=1, source_target_pairs={{0,8},{8,0},{1,9},{9,1},{2,10},{10,2},{3,11},{11,3},{4,12},{12,4},... | collective-permute-start | bytes 393224 | tf_op jit(solution)/shard_map/ppermute | solution.py:285
  47.0 1.6 %copy-start.6 = (bf16[64,1024]{1,0:T(8,128)(2,1)}, bf16[64,1024]{1,0:T(8,128)(2,1)S(1)}, u32[]{:S(2)}) copy-start(bf16[64,1024]{1,0:T(8,128)(2,1)S(1)} %collective-permute-done.3) | copy-start | bytes 393220
  48.6 19.3 %collective-permute-start.4 = (bf16[128,1024]{1,0:T(8,128)(2,1)}, bf16[128,1024]{1,0:T(8,128)(2,1)}, u32[]{:S(2)}, u32[]{:S(2)}) collective-permute-start(bf16[128,1024]{1,0:T(8,128)(2,1)} %pad_maximum_fusion.1), channel_id=1, source_target_pairs={{0,4},{4,0},{1,5},{5,1},{2,6},{6,2},{3,7},{7,3},{8,12},{12,8},{9,1... | collective-permute-start | bytes 786440 | tf_op jit(solution)/shard_map/ppermute | solution.py:285
  55.8 12.1 %copy-start.3 = (bf16[32,1024]{1,0:T(8,128)(2,1)S(1)}, bf16[32,1024]{1,0:T(8,128)(2,1)}, u32[]{:S(2)}) copy-start(bf16[32,1024]{1,0:T(8,128)(2,1)} %param.4) | copy-start | bytes 196612
  55.8 12.1 %copy-start.5 = (bf16[32,1024]{1,0:T(8,128)(2,1)S(1)}, bf16[32,1024]{1,0:T(8,128)(2,1)}, u32[]{:S(2)}) copy-start(bf16[32,1024]{1,0:T(8,128)(2,1)} %copy-done.4) | copy-start | bytes 196612
  55.8 12.1 %copy-start.7 = (bf16[64,1024]{1,0:T(8,128)(2,1)S(1)}, bf16[64,1024]{1,0:T(8,128)(2,1)}, u32[]{:S(2)}) copy-start(bf16[64,1024]{1,0:T(8,128)(2,1)} %copy-done.6) | copy-start | bytes 393220
  57.7 14.5 %collective-permute-start.2 = (bf16[256,1024]{1,0:T(8,128)(2,1)S(1)}, bf16[256,1024]{1,0:T(8,128)(2,1)S(1)}, u32[]{:S(2)}, u32[]{:S(2)}) collective-permute-start(bf16[256,1024]{1,0:T(8,128)(2,1)S(1)} %far_product.1), channel_id=1, source_target_pairs={{0,16},{16,0},{1,17},{17,1},{2,18},{18,2},{3,19},{19,3},{4,20},{20... | collective-permute-start | bytes 1572872 | tf_op jit(solution)/shard_map/ppermute | solution.py:285
  69.7 14.5 %collective-permute-start.5 = (bf16[256,1024]{1,0:T(8,128)(2,1)}, bf16[256,1024]{1,0:T(8,128)(2,1)}, u32[]{:S(2)}, u32[]{:S(2)}) collective-permute-start(bf16[256,1024]{1,0:T(8,128)(2,1)} %pad_maximum_fusion.first_ref), channel_id=1, source_target_pairs={{0,2},{2,0},{1,3},{3,1},{4,6},{6,4},{5,7},{7,5},{8,10},{10,8},{9,1... | collective-permute-start | bytes 1572872 | tf_op jit(solution)/shard_map/ppermute | solution.py:285
  74.2 0.8 copy-start.2
  75.0 27.9 %all-to-all-start.2 = ((bf16[8,32,1024]{2,1,0:T(8,128)(2,1)}), bf16[8,32,1024]{2,1,0:T(8,128)(2,1)S(1)}, u32[]{:S(2)}, u32[]{:S(2)}) async-start(bf16[8,32,1024]{2,1,0:T(8,128)(2,1)} %bitcast.14), calls=%async_computation.2 | async-start | bytes 1048576 | tf_op jit(solution)/shard_map/all_to_all | solution.py:281
  86.9 10.4 %collective-permute-start.6 = (bf16[576,512]{1,0:T(8,128)(2,1)S(1)}, bf16[576,512]{1,0:T(8,128)(2,1)S(1)}, u32[]{:S(2)}, u32[]{:S(2)}) collective-permute-start(bf16[576,512]{1,0:T(8,128)(2,1)S(1)} %get-tuple-element.16), channel_id=1, source_target_pairs={{0,1},{1,0},{2,3},{3,2},{4,5},{5,4},{6,7},{7,6},{8,9},{9,8},{10,11... | collective-permute-start | bytes 1769480 | tf_op jit(solution)/shard_map/ppermute | solution.py:285
  95.4 3.9 %collective-permute-start.7 = (bf16[576,512]{1,0:T(8,128)(2,1)S(1)}, bf16[576,512]{1,0:T(8,128)(2,1)S(1)}, u32[]{:S(2)}, u32[]{:S(2)}) collective-permute-start(bf16[576,512]{1,0:T(8,128)(2,1)S(1)} %get-tuple-element.17), channel_id=1, source_target_pairs={{0,1},{1,0},{2,3},{3,2},{4,5},{5,4},{6,7},{7,6},{8,9},{9,8},{10,11... | collective-permute-start | bytes 1769480 | tf_op jit(solution)/shard_map/ppermute | solution.py:285
